TPU v7x, 32 devices: a whole 2x2x4 slice. The times are simulated.
32 devices in a mesh: dp: 8 (over z, y), tensor: 4 (over x, core).
Axes of the slice: x: 2, y: 2, z: 4, core: 2. Of those that a mesh axis runs over, the one named last changes fastest.
Arguments:
- token_ids: int32 [1024], P('dp'), may hold values from 0 to 31999
- targets: int32 [1024], P('dp'), may hold values from 0 to 31999
- loss_offsets: int32 [128], P('dp'), may hold values from 0 to 127, as said below
- routes: int32 [1024, 2], P('dp'), may hold values from 0 to 3, all different within a row; in each aligned block of 128 rows (0 to 127, 128 to 255, ...) at most 128 rows name the same one
- picture_start: int32 [1, 1], replicated, may hold values from 0 to 768, as said below
- buckets: int32 [2047], replicated, may hold values from 0 to 31
- embedding: float32 [32000, 768], P('tensor', 'dp')
- embedding_first: float32 [32000, 768], P('tensor', 'dp'), may hold values from -4.5776367e-05 to 4.5776367e-05
- embedding_second: float32 [32000, 768], P('tensor', 'dp'), may hold values from 2.837829e-10 to 1.1569611e-09
- attn_proj: float32 [3, 768, 768], P(None, 'dp', 'tensor'), may hold values from -0.109375 to 0.109375
- attn_proj_first: float32 [3, 768, 768], P(None, 'dp', 'tensor'), may hold values from -9.1552734e-05 to 9.1552734e-05
- attn_proj_second: float32 [3, 768, 768], P(None, 'dp', 'tensor'), may hold values from 1.1569611e-09 to 4.5841855e-09
- out_proj: float32 [768, 768], P('tensor', 'dp'), may hold values from -1.75 to 1.75
- out_proj_first: float32 [768, 768], P('tensor', 'dp'), may hold values from -9.1552734e-05 to 9.1552734e-05
- out_proj_second: float32 [768, 768], P('tensor', 'dp'), may hold values from 1.1569611e-09 to 4.5841855e-09
- router: float32 [4, 768], P(None, 'dp'), may hold values from -0.078125 to 0.078125
- router_first: float32 [4, 768], P(None, 'dp'), may hold values from -0.00030517578 to 0.00030517578
- router_second: float32 [4, 768], P(None, 'dp'), may hold values from 1.0259844e-08 to 4.1475964e-08
- expert_in: float32 [768, 12288], P(None, ('dp', 'tensor')), may hold values from -0.21875 to 0.21875
- expert_in_first: float32 [768, 12288], P(None, ('dp', 'tensor')), may hold values from -9.1552734e-05 to 9.1552734e-05
- expert_in_second: float32 [768, 12288], P(None, ('dp', 'tensor')), may hold values from 1.1569611e-09 to 4.5841855e-09
- expert_out: float32 [12288, 768], P(('dp', 'tensor')), may hold values from -0.109375 to 0.109375
- expert_out_first: float32 [12288, 768], P(('dp', 'tensor')), may hold values from -9.1552734e-05 to 9.1552734e-05
- expert_out_second: float32 [12288, 768], P(('dp', 'tensor')), may hold values from 1.1569611e-09 to 4.5841855e-09
- norm_gains: float32 [3, 768], P(None, 'dp')
- norm_gains_first: float32 [3, 768], P(None, 'dp'), may hold values from -0.00036621094 to 0.00036621094
- norm_gains_second: float32 [3, 768], P(None, 'dp'), may hold values from 3.2744183e-09 to 1.3097673e-08
- position_bias: float32 [12, 32], P('tensor'), may hold values from -6 to 6
- position_bias_first: float32 [12, 32], P('tensor'), may hold values from -0.0009765625 to 0.0009765625
- position_bias_second: float32 [12, 32], P('tensor'), may hold values from 1.1569611e-07 to 4.5841855e-07
Outputs:
- new_embedding: float32 [32000, 768], P('tensor', 'dp')
- new_embedding_first: float32 [32000, 768], P('tensor', 'dp')
- new_embedding_second: float32 [32000, 768], P('tensor', 'dp')
- new_attn_proj: float32 [3, 768, 768], P(None, 'dp', 'tensor')
- new_attn_proj_first: float32 [3, 768, 768], P(None, 'dp', 'tensor')
- new_attn_proj_second: float32 [3, 768, 768], P(None, 'dp', 'tensor')
- new_out_proj: float32 [768, 768], P('tensor', 'dp')
- new_out_proj_first: float32 [768, 768], P('tensor', 'dp')
- new_out_proj_second: float32 [768, 768], P('tensor', 'dp')
- new_router: float32 [4, 768], P(None, 'dp')
- new_router_first: float32 [4, 768], P(None, 'dp')
- new_router_second: float32 [4, 768], P(None, 'dp')
- new_expert_in: float32 [768, 12288], P(None, ('dp', 'tensor'))
- new_expert_in_first: float32 [768, 12288], P(None, ('dp', 'tensor'))
- new_expert_in_second: float32 [768, 12288], P(None, ('dp', 'tensor'))
- new_expert_out: float32 [12288, 768], P(('dp', 'tensor'))
- new_expert_out_first: float32 [12288, 768], P(('dp', 'tensor'))
- new_expert_out_second: float32 [12288, 768], P(('dp', 'tensor'))
- new_norm_gains: float32 [3, 768], P(None, 'dp')
- new_norm_gains_first: float32 [3, 768], P(None, 'dp')
- new_norm_gains_second: float32 [3, 768], P(None, 'dp')
- new_position_bias: float32 [12, 32], P('tensor')
- new_position_bias_first: float32 [12, 32], P('tensor')
- new_position_bias_second: float32 [12, 32], P('tensor')
- grad_norm: float32 [], replicated
- loss_sum: float32 [], replicated
- loss_count: float32 [], replicated
Inputs may be any that keep to these rules, and one draw needn't show every extreme that they name: `loss_offsets`: in each aligned block of 16 entries the offsets are distinct. `picture_start`: increasing along each row; the pieces of 256 positions do not intersect and end inside their sequence. The two routes of a token differ; among the rows of one device no expert is named more than 128 times, a bound that some block reaches.
All inputs are finite; a program needn't handle non-finite values.
Results may differ from a plain program's by a relative error of at most 0.02.
The roundings to bfloat16 on the way count: a program that leaves them out, or rounds other values in their place, can miss the bound.
Values may be sent and summed in bfloat16 or wider, within the bound.
A program may use at most 256 MiB of HBM per device.

v0:
```python
import math

import jax
import jax.numpy as jnp
from jax import lax
from jax.sharding import PartitionSpec as P

HD = 64
VOCAB = 32000
PIECE = 256
SEQ = 4096
STEP = 10


SMOOTH = 0.1
ZLOSS = 0.0001
NORM_EPS = 1e-06
MAX_NORM = 1.0
BETA1 = 0.9
BETA2 = 0.95
ADAM_EPS = 1e-08
RATES = (0.04, 0.04, 1.0, 0.03, 0.07, 0.035, 1.0, 0.7)
DECAYS = (0.1, 0.1, 0.1, 0.1, 0.1, 0.1, 0.0, 0.0)
NEGATIVE = -1e30
HIGH = lax.Precision.HIGHEST


def merged(shard, axis, combine):
    everything = jax.tree.map(lambda part: lax.all_gather(part, axis), shard)
    initial = jax.tree.map(lambda part: part[0], everything)

    def lap(k, so_far):
        return combine(so_far, jax.tree.map(lambda part: part[k], everything))

    return lax.fori_loop(1, lax.axis_size(axis), lap, initial)


def normed(v, g):
    return v * lax.rsqrt(jnp.mean(v * v, -1, keepdims=True) + NORM_EPS) * g


def norm_back(v, g, upstream):
    unused, pull = jax.vjp(normed, v, g)
    return pull(upstream)


def picture_of(positions, starts, width):
    inside = (positions[:, None] >= starts[None, :]) & (
        positions[:, None] < starts[None, :] + width
    )
    number = jnp.arange(starts.shape[0], dtype=jnp.int32) + 1
    return jnp.sum(inside.astype(jnp.int32) * number[None, :], 1) - 1


def rel_window(relative, query_start, query_count, key_start, key_count, length):
    centre = query_start - key_start + length - 1
    window = lax.dynamic_slice_in_dim(
        relative, centre - key_count + 1, query_count + key_count - 1, 1
    )
    span = query_count + key_count
    wrapped = jnp.concatenate(
        [
            jnp.flip(window[:, :key_count], 1),
            jnp.zeros((window.shape[0], 1), window.dtype),
            jnp.flip(window[:, key_count:], 1),
        ],
        1,
    )
    tiled = jnp.tile(wrapped, (1, query_count))[:, : query_count * (span - 1)]
    return tiled.reshape(window.shape[0], query_count, span - 1)[:, :, :key_count]


def tensor_total(value):
    return lax.psum(value, "tensor")


def route_exchange(value):
    return lax.all_to_all(value, "dp", split_axis=0, concat_axis=0, tiled=True)


def combine_stats(left, right):
    peak = jnp.maximum(left[0], right[0])
    total = left[1] * jnp.exp(left[0] - peak) + right[1] * jnp.exp(right[0] - peak)
    return (peak, total, left[2] + right[2], left[3] + right[3])


def adam_update(weight, first, second, grad, rate, decay):
    first = BETA1 * first + (1 - BETA1) * grad
    second = BETA2 * second + (1 - BETA2) * grad * grad
    fixed_first = first / (1 - BETA1**STEP)
    fixed_second = second / (1 - BETA2**STEP)
    weight = weight - rate * (fixed_first / (jnp.sqrt(fixed_second) + ADAM_EPS) + decay * weight)
    return (weight, first, second)


def local(
    token_ids,
    targets,
    loss_offsets,
    routes,
    picture_start,
    buckets,
    embedding,
    embedding_first,
    embedding_second,
    attn_proj,
    attn_proj_first,
    attn_proj_second,
    out_proj,
    out_proj_first,
    out_proj_second,
    router,
    router_first,
    router_second,
    expert_in,
    expert_in_first,
    expert_in_second,
    expert_out,
    expert_out_first,
    expert_out_second,
    norm_gains,
    norm_gains_first,
    norm_gains_second,
    position_bias,
    position_bias_first,
    position_bias_second,
):
    f32 = jnp.float32
    bf16 = jnp.bfloat16
    dp_count = lax.axis_size("dp")
    tensor_count = lax.axis_size("tensor")
    dp_place = lax.axis_index("dp")
    tensor_place = lax.axis_index("tensor")
    rows = token_ids.shape[0]
    every = rows * dp_count
    length = min(SEQ, every)
    seqs = every // length
    sub = rows // seqs
    scale = 1.0 / math.sqrt(HD)
    vocab_rows = embedding.shape[0]
    table, projection, output_map, router_full, gain_full = (
        lax.all_gather(embedding.astype(bf16), "dp", axis=1, tiled=True),
        lax.all_gather(attn_proj.astype(bf16), "dp", axis=1, tiled=True),
        lax.all_gather(out_proj.astype(bf16), "dp", axis=1, tiled=True),
        lax.all_gather(router.astype(bf16), "dp", axis=1, tiled=True),
        lax.all_gather(norm_gains.astype(bf16), "dp", axis=1, tiled=True),
    )
    gain = gain_full.astype(f32)
    features = table.shape[1]
    offset = token_ids - tensor_place * vocab_rows
    owned = (offset >= 0) & (offset < vocab_rows)
    offset = jnp.clip(offset, 0, vocab_rows - 1)
    looked = jnp.take(table, offset, axis=0).astype(f32)
    stream_in = tensor_total(jnp.where(owned[:, None], looked, 0.0))
    pos_here = dp_place * sub + jnp.arange(sub, dtype=jnp.int32)
    seq_positions = jnp.arange(length, dtype=jnp.int32)
    picture_all = jax.vmap(lambda starts: picture_of(seq_positions, starts, PIECE))(picture_start)
    picture_here = lax.dynamic_slice_in_dim(picture_all, dp_place * sub, sub, 1)
    bucket_ids = jnp.arange(position_bias.shape[1], dtype=jnp.int32)
    bucket_hot = (bucket_ids[:, None] == buckets[None, :]).astype(f32)
    relative = jnp.dot(position_bias, bucket_hot, precision=HIGH)
    normed_in = normed(stream_in, gain[0]).astype(bf16)
    fresh = jnp.einsum("td,sde->ste", normed_in, projection, preferred_element_type=f32).astype(
        bf16
    )
    width = fresh.shape[2]
    heads = width // HD
    keys_local = fresh[1].reshape(seqs, sub, width)
    values_local = fresh[2].reshape(seqs, sub, width)
    query_heads = fresh[0].reshape(seqs, sub, heads, HD)
    keys_all, values_all = (
        lax.all_gather(keys_local, "dp", axis=1, tiled=True),
        lax.all_gather(values_local, "dp", axis=1, tiled=True),
    )
    block = min(512, length)
    blocks = length // block
    block_ids = jnp.arange(blocks, dtype=jnp.int32)

    def pair_scores(q_heads, q_pos, q_pic, k_heads, k_pos, k_pic, bias):
        raw = (
            jnp.einsum("sqhd,skhd->shqk", q_heads, k_heads, preferred_element_type=f32) * scale
            + bias[None]
        )
        allowed = (k_pos[None, :] <= q_pos[:, None])[None] | (
            k_pic[:, None, :] == q_pic[:, :, None]
        ) & (q_pic[:, :, None] >= 0)
        return jnp.where(allowed[:, None], raw, NEGATIVE)

    def key_slice(source, start):
        return lax.dynamic_slice_in_dim(source, start, block, 1).reshape(seqs, block, heads, HD)

    def own_bias(start):
        return rel_window(relative, dp_place * sub, sub, start, block, length)

    def fwd_scores(index, key_source):
        start = index * block
        key_pos = start + jnp.arange(block, dtype=jnp.int32)
        return pair_scores(
            query_heads,
            pos_here,
            picture_here,
            key_slice(key_source, start),
            key_pos,
            lax.dynamic_slice_in_dim(picture_all, start, block, 1),
            own_bias(start),
        )

    def max_step(carry, index):
        top, total = carry
        s = fwd_scores(index, keys_all)
        new_top = jnp.maximum(top, jnp.max(s, -1))
        terms = jnp.where(s > 0.5 * NEGATIVE, jnp.exp(s - new_top[..., None]), 0.0)
        total = total * jnp.exp(top - new_top) + jnp.sum(terms, -1)
        return ((new_top, total), None)

    start_top = jnp.full((seqs, heads, sub), NEGATIVE, f32)
    (top, total), unused = lax.scan(
        max_step, (start_top, jnp.zeros((seqs, heads, sub), f32)), block_ids
    )
    log_total = top + jnp.log(total)

    def out_step(accum, index):
        s = fwd_scores(index, keys_all)
        probs = jnp.exp(s - log_total[..., None]).astype(bf16)
        value_heads = key_slice(values_all, index * block)
        return (
            accum + jnp.einsum("shqk,skhd->sqhd", probs, value_heads, preferred_element_type=f32),
            None,
        )

    attended, unused = lax.scan(out_step, jnp.zeros((seqs, sub, heads, HD), f32), block_ids)
    attended_low = attended.reshape(rows, width).astype(bf16)
    stream_mid = stream_in + tensor_total(
        jnp.dot(attended_low, output_map, preferred_element_type=f32)
    )
    normed_mid = normed(stream_mid, gain[1]).astype(bf16)
    router_logits = jnp.dot(normed_mid, router_full.T, preferred_element_type=f32)
    gates = jax.nn.softmax(jnp.take_along_axis(router_logits, routes, 1), -1)
    experts = router_full.shape[0]
    top_k = routes.shape[1]
    capacity = 2 * rows * top_k // experts
    flat = routes.reshape(-1)
    owner = jnp.arange(rows * top_k, dtype=jnp.int32) // top_k
    hits = (flat[:, None] == jnp.arange(experts, dtype=jnp.int32)[None, :]).astype(jnp.int32)
    slot = jnp.sum(jnp.cumsum(hits, 0) * hits, 1) - 1
    first_row = 2 * flat * capacity + slot

    def pack(values):
        buffer = jnp.zeros((experts, capacity, features), bf16).at[flat, slot].set(values)
        return jnp.repeat(buffer, 2, axis=0).reshape(2 * experts * capacity, features)

    def unpack(values):
        return values[first_row].astype(f32) + values[first_row + capacity].astype(f32)

    in_low = expert_in.astype(bf16)
    out_low = expert_out.astype(bf16)
    arrived = route_exchange(pack(normed_mid[owner]))
    inner = jnp.dot(arrived, in_low, preferred_element_type=f32)
    active = jax.nn.gelu(inner).astype(bf16)
    produced = jnp.dot(active, out_low, preferred_element_type=f32).astype(bf16)
    returned = unpack(route_exchange(produced))
    mixed = jnp.sum((gates.reshape(-1)[:, None] * returned).reshape(rows, top_k, features), 1)
    stream_out = stream_mid + tensor_total(mixed)
    normed_out = normed(stream_out, gain[2]).astype(bf16)
    picked = normed_out[loss_offsets]
    logits = jnp.dot(picked, table.T, preferred_element_type=f32)
    wanted = targets[loss_offsets] - tensor_place * vocab_rows
    hit = jnp.arange(vocab_rows, dtype=jnp.int32)[None, :] == wanted[:, None]
    local_top = jnp.max(logits, -1)
    stats = (
        local_top,
        jnp.sum(jnp.exp(logits - local_top[:, None]), -1),
        jnp.sum(jnp.where(hit, logits, 0.0), -1),
        jnp.sum(logits, -1),
    )
    peak, vocab_total, target_logit, logit_sum = merged(stats, "tensor", combine_stats)
    loss_total = peak + jnp.log(vocab_total)
    weight = (picture_here.reshape(rows)[loss_offsets] < 0).astype(f32)
    per_row = (
        loss_total
        - (1 - SMOOTH) * target_logit
        - SMOOTH * logit_sum / VOCAB
        + ZLOSS * loss_total * loss_total
    )
    loss_local = jnp.sum(weight * per_row)
    soft = jnp.exp(logits - loss_total[:, None])
    d_logits = (
        weight[:, None]
        * (
            (1 + 2 * ZLOSS * loss_total)[:, None] * soft
            - (1 - SMOOTH) * hit.astype(f32)
            - SMOOTH / VOCAB
        )
    ).astype(bf16)
    d_picked = jnp.dot(d_logits, table, preferred_element_type=f32)
    grad_table = jnp.dot(d_logits.T, picked, preferred_element_type=f32)
    d_normed_out = tensor_total(jnp.zeros((rows, features), f32).at[loss_offsets].add(d_picked))
    d_stream_out, grad_final = norm_back(stream_out, gain[2], d_normed_out)
    d_piece = (gates.reshape(-1)[:, None] * d_stream_out[owner]).astype(bf16)
    d_arrived = route_exchange(pack(d_piece))
    d_active = jnp.dot(d_arrived, out_low.T, preferred_element_type=f32)
    unused, gelu_pull = jax.vjp(jax.nn.gelu, inner)
    d_inner = gelu_pull(d_active)[0].astype(bf16)
    grad_out = jnp.dot(active.T, d_arrived, preferred_element_type=f32)
    grad_in = jnp.dot(arrived.T, d_inner, preferred_element_type=f32)
    sent_back = jnp.dot(d_inner, in_low.T, preferred_element_type=f32).astype(bf16)
    d_routes = unpack(route_exchange(sent_back))
    gate_part = jnp.sum(d_stream_out[owner] * returned, -1).reshape(rows, top_k)
    route_part = jnp.sum(d_routes.reshape(rows, top_k, features), 1)
    d_from_experts, d_gates = tensor_total((route_part, gate_part))
    d_chosen = gates * (d_gates - jnp.sum(gates * d_gates, -1, keepdims=True))
    expert_hot = (routes[..., None] == jnp.arange(experts, dtype=jnp.int32)).astype(f32)
    d_router_logits = jnp.sum(expert_hot * d_chosen[..., None], 1).astype(bf16)
    grad_router = jnp.dot(d_router_logits.T, normed_mid, preferred_element_type=f32)
    d_normed_mid = d_from_experts + jnp.dot(
        d_router_logits, router_full, preferred_element_type=f32
    )
    d_from_mid, grad_middle = norm_back(stream_mid, gain[1], d_normed_mid)
    d_stream_mid = d_stream_out + d_from_mid
    d_attn_low = d_stream_mid.astype(bf16)
    grad_output_map = jnp.dot(attended_low.T, d_attn_low, preferred_element_type=f32)
    d_attended = jnp.dot(d_attn_low, output_map.T, preferred_element_type=f32).astype(bf16)
    d_heads = d_attended.reshape(seqs, sub, heads, HD)
    delta = jnp.moveaxis(jnp.sum(d_heads.astype(f32) * attended, -1), 2, 1)
    key_source, value_source = (
        lax.all_gather(keys_local, "dp", axis=1, tiled=True),
        lax.all_gather(values_local, "dp", axis=1, tiled=True),
    )

    def score_grads(
        q_heads, q_pos, q_pic, k_heads, k_pos, k_pic, bias, totals, deltas, dq_heads, v_heads
    ):
        s = pair_scores(q_heads, q_pos, q_pic, k_heads, k_pos, k_pic, bias)
        probs = jnp.exp(s - totals[..., None])
        d_probs = jnp.einsum("sqhd,skhd->shqk", dq_heads, v_heads, preferred_element_type=f32)
        d_scores = (probs * (d_probs - deltas[..., None])).astype(bf16)
        return (probs, d_scores)

    def key_step(carry, index):
        d_query, d_rel = carry
        start = index * block
        key_pos = start + jnp.arange(block, dtype=jnp.int32)
        key_heads = key_slice(key_source, start)
        value_heads = key_slice(value_source, start)
        bias, bias_pull = jax.vjp(
            lambda table_rel: rel_window(table_rel, dp_place * sub, sub, start, block, length),
            relative,
        )
        probs, d_scores = score_grads(
            query_heads,
            pos_here,
            picture_here,
            key_heads,
            key_pos,
            lax.dynamic_slice_in_dim(picture_all, start, block, 1),
            bias,
            log_total,
            delta,
            d_heads,
            value_heads,
        )
        d_query = (
            d_query
            + jnp.einsum("shqk,skhd->sqhd", d_scores, key_heads, preferred_element_type=f32) * scale
        )
        d_rel = d_rel + bias_pull(jnp.sum(d_scores.astype(f32), 0))[0]
        d_key = (
            jnp.einsum("shqk,sqhd->skhd", d_scores, query_heads, preferred_element_type=f32) * scale
        )
        d_value = jnp.einsum(
            "shqk,sqhd->skhd", probs.astype(bf16), d_heads, preferred_element_type=f32
        )
        joined = jnp.concatenate(
            [d_key.reshape(seqs, block, width), d_value.reshape(seqs, block, width)], 2
        )
        return ((d_query, d_rel), joined)

    start_carry = (jnp.zeros((seqs, sub, heads, HD), f32), jnp.zeros(relative.shape, f32))
    (d_query, d_rel), key_terms = lax.scan(key_step, start_carry, block_ids)
    d_bias = jnp.dot(d_rel, bucket_hot.T, precision=HIGH)
    ordered = jnp.moveaxis(key_terms, 0, 1).reshape(seqs, length, 2 * width)
    key_grads = lax.psum_scatter(ordered, "dp", scatter_dimension=1, tiled=True).reshape(
        rows, 2 * width
    )
    d_fresh = jnp.stack(
        [d_query.reshape(rows, width), key_grads[:, :width], key_grads[:, width:]]
    ).astype(bf16)
    grad_proj = jnp.einsum("td,ste->sde", normed_in, d_fresh, preferred_element_type=f32)
    d_normed_in = tensor_total(
        jnp.einsum("ste,sde->td", d_fresh, projection, preferred_element_type=f32)
    )
    d_from_in, grad_first = norm_back(stream_in, gain[0], d_normed_in)
    d_stream_in = d_stream_mid + d_from_in
    grad_table = grad_table + jnp.zeros((vocab_rows, features), f32).at[offset].add(
        jnp.where(owned[:, None], d_stream_in, 0.0)
    )
    sum_table, sum_proj, sum_output, sum_router, sum_gains = (
        lax.psum_scatter(grad_table, "dp", scatter_dimension=1, tiled=True),
        lax.psum_scatter(grad_proj, "dp", scatter_dimension=1, tiled=True),
        lax.psum_scatter(grad_output_map, "dp", scatter_dimension=1, tiled=True),
        lax.psum_scatter(grad_router, "dp", scatter_dimension=1, tiled=True),
        lax.psum_scatter(
            jnp.stack([grad_first, grad_middle, grad_final]), "dp", scatter_dimension=1, tiled=True
        ),
    )
    sum_bias = lax.psum(d_bias, "dp")
    squares = (
        jnp.sum(sum_table * sum_table)
        + jnp.sum(sum_proj * sum_proj)
        + jnp.sum(sum_output * sum_output)
        + jnp.sum(grad_in * grad_in)
        + jnp.sum(grad_out * grad_out)
        + (jnp.sum(sum_router * sum_router) + jnp.sum(sum_gains * sum_gains)) / tensor_count
        + jnp.sum(sum_bias * sum_bias) / dp_count
    )
    total_squares, loss_sum, loss_count = lax.psum(
        (squares, loss_local / tensor_count, jnp.sum(weight) / tensor_count), ("dp", "tensor")
    )
    grad_norm = jnp.sqrt(total_squares)
    clip = MAX_NORM / jnp.maximum(grad_norm, MAX_NORM)
    params = (
        embedding,
        attn_proj,
        out_proj,
        router,
        expert_in,
        expert_out,
        norm_gains,
        position_bias,
    )
    firsts = (
        embedding_first,
        attn_proj_first,
        out_proj_first,
        router_first,
        expert_in_first,
        expert_out_first,
        norm_gains_first,
        position_bias_first,
    )
    seconds = (
        embedding_second,
        attn_proj_second,
        out_proj_second,
        router_second,
        expert_in_second,
        expert_out_second,
        norm_gains_second,
        position_bias_second,
    )
    grads = (sum_table, sum_proj, sum_output, sum_router, grad_in, grad_out, sum_gains, sum_bias)
    results = []
    for index in range(8):
        results.extend(
            adam_update(
                params[index],
                firsts[index],
                seconds[index],
                clip * grads[index],
                RATES[index],
                DECAYS[index],
            )
        )
    return (
        results[0],
        results[1],
        results[2],
        results[3],
        results[4],
        results[5],
        results[6],
        results[7],
        results[8],
        results[9],
        results[10],
        results[11],
        results[12],
        results[13],
        results[14],
        results[15],
        results[16],
        results[17],
        results[18],
        results[19],
        results[20],
        results[21],
        results[22],
        results[23],
        grad_norm,
        loss_sum,
        loss_count,
    )


def solution(mesh):
    in_specs = (
        P("dp"),
        P("dp"),
        P("dp"),
        P("dp", None),
        P(),
        P(),
        P("tensor", "dp"),
        P("tensor", "dp"),
        P("tensor", "dp"),
        P(None, "dp", "tensor"),
        P(None, "dp", "tensor"),
        P(None, "dp", "tensor"),
        P("tensor", "dp"),
        P("tensor", "dp"),
        P("tensor", "dp"),
        P(None, "dp"),
        P(None, "dp"),
        P(None, "dp"),
        P(None, ("dp", "tensor")),
        P(None, ("dp", "tensor")),
        P(None, ("dp", "tensor")),
        P(("dp", "tensor"), None),
        P(("dp", "tensor"), None),
        P(("dp", "tensor"), None),
        P(None, "dp"),
        P(None, "dp"),
        P(None, "dp"),
        P("tensor", None),
        P("tensor", None),
        P("tensor", None),
    )
    out_specs = (
        P("tensor", "dp"),
        P("tensor", "dp"),
        P("tensor", "dp"),
        P(None, "dp", "tensor"),
        P(None, "dp", "tensor"),
        P(None, "dp", "tensor"),
        P("tensor", "dp"),
        P("tensor", "dp"),
        P("tensor", "dp"),
        P(None, "dp"),
        P(None, "dp"),
        P(None, "dp"),
        P(None, ("dp", "tensor")),
        P(None, ("dp", "tensor")),
        P(None, ("dp", "tensor")),
        P(("dp", "tensor"), None),
        P(("dp", "tensor"), None),
        P(("dp", "tensor"), None),
        P(None, "dp"),
        P(None, "dp"),
        P(None, "dp"),
        P("tensor", None),
        P("tensor", None),
        P("tensor", None),
        P(),
        P(),
        P(),
    )
    return jax.shard_map(local, mesh=mesh, in_specs=in_specs, out_specs=out_specs, check_vma=False)
```

profile of v0, /device:TPU:0, one launch (start us, length us, event | category | flops | bytes accessed | tf_op | source)
XLA Modules:
  0.0 1683.3 jit_solution(10430473580805703198)
XLA Ops:
  11.8 22.4 %all-gather.4 = bf16[8,96,3]{1,2,0:T(4,128)(2,1)S(1)} all-gather(bf16[1,96,3]{1,2,0:T(4,128)(2,1)S(1)} %convert_bitcast_fusion.3), channel_id=1, replica_groups=mesh['dp'=8,'tensor'=4] {'dp'}, dimensions={0}, use_global_device_ids=true | all-gather | bytes 5184 | tf_op jit(solution)/shard_map/all_gather | solution.py:146
  36.1 43.0 %all_gather.49 = bf16[3,768,192]{2,0,1:T(4,128)(2,1)S(1)} all-gather(bf16[3,96,192]{2,0,1:T(4,128)(2,1)S(1)} %copy.255), channel_id=1, replica_groups=mesh['dp'=8,'tensor'=4] {'dp'}, dimensions={1}, use_global_device_ids=true | all-gather | bytes 995328 | tf_op jit(solution)/shard_map/all_gather | solution.py:143
  81.4 35.4 %all_gather.52 = bf16[192,768]{0,1:T(8,128)(2,1)} all-gather(bf16[192,96]{0,1:T(8,128)(2,1)S(1)} %copy.257), channel_id=1, replica_groups=mesh['dp'=8,'tensor'=4] {'dp'}, dimensions={1}, use_global_device_ids=true | all-gather | bytes 331776 | tf_op jit(solution)/shard_map/all_gather | solution.py:144
  117.0 88.3 %all-gather.8.cloned.1.call-done = bf16[8000,768]{0,1:T(8,128)(2,1)} async-done(((bf16[8000,96]{0,1:T(8,128)(2,1)}), bf16[8000,768]{0,1:T(8,128)(2,1)}) %all-gather.8.cloned.1.call-update) | async-done | bytes 12288016 | tf_op jit(solution)/shard_map/all_gather | solution.py:142
  205.4 16.5 copy.253
  230.4 31.2 %all-reduce.17.cloned.1.call-done = f32[128,768]{1,0:T(8,128)} async-done(((f32[128,768]{1,0:T(8,128)}), f32[128,768]{1,0:T(8,128)}) %all-reduce.17.cloned.1.call-update) | async-done | bytes 393232 | tf_op jit(solution)/shard_map/psum | solution.py:74
  264.3 28.1 %all_gather.51 = bf16[1,1024,192]{1,2,0:T(8,128)(2,1)} all-gather(bf16[1,128,192]{1,2,0:T(8,128)(2,1)S(1)} %get-tuple-element.1695), channel_id=1, replica_groups=mesh['dp'=8,'tensor'=4] {'dp'}, dimensions={1}, use_global_device_ids=true | all-gather | bytes 442368 | tf_op jit(solution)/shard_map/all_gather | solution.py:172
  292.9 16.5 while.79
  309.5 27.4 %all_gather.50 = bf16[1,1024,192]{1,2,0:T(8,128)(2,1)S(1)} all-gather(bf16[1,128,192]{1,2,0:T(8,128)(2,1)S(1)} %get-tuple-element.1696), channel_id=1, replica_groups=mesh['dp'=8,'tensor'=4] {'dp'}, dimensions={1}, use_global_device_ids=true | all-gather | bytes 442368 | tf_op jit(solution)/shard_map/all_gather | solution.py:173
  337.5 23.3 %while.80 = (s32[]{:T(128)}, f32[1,128,3,64]{1,3,2,0:T(8,128)}, s32[2]{0:T(128)S(1)}, bf16[1,1024,192]{1,2,0:T(8,128)(2,1)S(1)}, s32[1,1024]{1,0:T(1,128)S(1)}, ...) while((s32[]{:T(128)}, f32[1,128,3,64]{1,3,2,0:T(8,128)}, ...), condition=%wide.region_7.8_spmd.clone.clone.clone, body=%wide.region_6.7_spmd.clone.clone.clone.sunk | while | flops 51630604 | bytes 13485815 | solution.py:231
  363.6 28.8 %all-reduce.19.cloned.1.call-done = f32[128,768]{1,0:T(8,128)} async-done(((f32[128,768]{1,0:T(8,128)}), f32[128,768]{1,0:T(8,128)}) %all-reduce.19.cloned.1.call-update) | async-done | bytes 393232 | tf_op jit(solution)/shard_map/psum | solution.py:74
  394.9 15.3 scatter_fusion
  410.4 41.4 %all_to_all.48 = bf16[8,128,768]{2,1,0:T(8,128)(2,1)S(1)} all-to-all(bf16[8,128,768]{2,1,0:T(8,128)(2,1)S(1)} %bitcast.427), channel_id=1, replica_groups=mesh['dp'=8,'tensor'=4] {'dp'}, dimensions={0} | all-to-all | bytes 3145728 | tf_op jit(solution)/shard_map/all_to_all | solution.py:78
  461.8 38.2 %all-gather.5 = bf16[8,96,4]{1,2,0:T(4,128)(2,1)S(1)} all-gather(bf16[1,96,4]{1,2,0:T(4,128)(2,1)S(1)} %convert_bitcast_fusion.2), channel_id=1, replica_groups=mesh['dp'=8,'tensor'=4] {'dp'}, dimensions={0}, use_global_device_ids=true | all-gather | bytes 6912 | tf_op jit(solution)/shard_map/all_gather | solution.py:145
  511.3 36.2 %all-reduce.21.cloned.1.call-done = f32[128,768]{1,0:T(8,128)} async-done(((f32[128,768]{1,0:T(8,128)}), f32[128,768]{1,0:T(8,128)}) %all-reduce.21.cloned.1.call-update) | async-done | bytes 393232 | tf_op jit(solution)/shard_map/psum | solution.py:74
  573.3 32.7 %all-reduce.23.cloned.1.call-done = f32[128,768]{1,0:T(8,128)} async-done(((f32[128,768]{1,0:T(8,128)}), f32[128,768]{1,0:T(8,128)}) %all-reduce.23.cloned.1.call-update) | async-done | bytes 393232 | tf_op jit(solution)/shard_map/psum | solution.py:74
  611.3 23.8 %scatter_fusion.1 = bf16[4,128,768]{2,1,0:T(8,128)(2,1)S(1)} fusion(bf16[4,128,768]{2,1,0:T(8,128)(2,1)S(1)} %broadcast.995, s32[256]{0:T(256)S(1)} %bitcast.407, bf16[256,768]{1,0:T(8,128)(2,1)} %get-tuple-element.1693), kind=kCustom, calls=%fused_computation.13 | custom fusion | bytes 1181696 | tf_op jit(solution)/shard_map/scatter | solution.py:249
  635.2 41.5 %all_to_all.49 = bf16[8,128,768]{2,1,0:T(8,128)(2,1)S(1)} all-to-all(bf16[8,128,768]{2,1,0:T(8,128)(2,1)S(1)} %bitcast.428), channel_id=1, replica_groups=mesh['dp'=8,'tensor'=4] {'dp'}, dimensions={0} | all-to-all | bytes 3145728 | tf_op jit(solution)/shard_map/all_to_all | solution.py:78
  690.3 30.5 %all-to-all-done.3 = bf16[8,128,768]{2,1,0:T(8,128)(2,1)S(1)} async-done(((bf16[8,128,768]{2,1,0:T(8,128)(2,1)}), bf16[8,128,768]{2,1,0:T(8,128)(2,1)S(1)}, u32[]{:S(2)}, u32[]{:S(2)}) %all-to-all-start.3) | async-done | bytes 1572896 | tf_op jit(solution)/shard_map/all_to_all | solution.py:78
  728.4 31.1 %all-reduce.25.cloned.1.call-done = f32[128,768]{1,0:T(8,128)} async-done(((f32[128,768]{1,0:T(8,128)}), f32[128,768]{1,0:T(8,128)}) %all-reduce.25.cloned.1.call-update) | async-done | bytes 393232 | tf_op jit(solution)/shard_map/psum | solution.py:74
  763.8 68.8 %while.81 = (s32[]{:T(128)}, f32[1,128,3,64]{1,3,2,0:T(8,128)}, f32[3,2047]{1,0:T(4,128)}, f32[2,1,512,384]{2,0,3,1:T(2,128)}, s32[2]{0:T(128)}, /*index=5*/bf16...) while((s32[]{:T(128)}, f32[1,128,3,64]{1,3,2,0:T(8,128)}, ...), condition=%wide.region_39.40_spmd.clone.clone.clone, body=%wide.region_37.39_spmd.clone.clone.clone.sunk | while | flops 128530824 | bytes 32386260 | solution.py:379
  783.3 14.9 dynamic_update_slice.23
  836.9 64.8 %reduce-scatter.17.cloned.1.call-done = f32[1,128,384]{1,2,0:T(8,128)} async-done(((f32[1,1024,384]{1,2,0:T(8,128)}), f32[1,128,384]{1,2,0:T(8,128)}) %reduce-scatter.17.cloned.1.call-update) | async-done | bytes 196624 | tf_op jit(solution)/shard_map/reduce_scatter | solution.py:382
  906.4 29.8 %all-reduce.27.cloned.1.call-done = f32[128,768]{1,0:T(8,128)} async-done(((f32[128,768]{1,0:T(8,128)}), f32[128,768]{1,0:T(8,128)}) %all-reduce.27.cloned.1.call-update) | async-done | bytes 393232 | tf_op jit(solution)/shard_map/psum | solution.py:74
  957.9 18.0 %scatter_custom_fusion.3 = f32[8000,768]{1,0:T(8,128)} fusion(f32[8000,768]{1,0:T(8,128)} %fusion.115, s32[128]{0:T(128)} %copy-done.88, f32[128,768]{1,0:T(8,128)S(1)} %copy-done.22, f32[128,768]{1,0:T(8,128)S(1)} %copy-done.4, f32[128,768]{1,0:T(8,128)S(1)} %copy-done.37, f32[128]{0:T(128)S(1)} %multiply_multiply_fusion.11, f32[768]{0:T(1024)S(1)} %copy-done.58, ...), kind=kCustom, calls=%fused_computation.163 | custom fusion | flops 786432 | bytes 25760384 | tf_op jit(solution)/shard_map/scatter-add | solution.py:394
  975.8 24.7 %copy.283 = f32[8000,768]{0,1:T(8,128)} copy(f32[8000,768]{1,0:T(8,128)} %scatter_custom_fusion.3) | data formatting | bytes 49152000
  1010.1 21.5 %psum.84 = f32[3,32]{1,0:T(4,128)S(1)} all-reduce(f32[3,32]{1,0:T(4,128)S(1)} %fusion.79), channel_id=1, replica_groups=mesh['dp'=8,'tensor'=4] {'dp'}, use_global_device_ids=true, to_apply=%region_59.60 | all-reduce | flops 96 | bytes 768 | tf_op jit(solution)/shard_map/psum | solution.py:406
  1032.8 34.6 %reduce-scatter.23.cloned.1.call-done = f32[96,192]{1,0:T(8,128)} async-done(((f32[768,192]{1,0:T(8,128)}), f32[96,192]{1,0:T(8,128)}) %reduce-scatter.23.cloned.1.call-update) | async-done | bytes 73744
  1069.0 62.6 %reduce-scatter.27.cloned.1.call-done = f32[96,3]{1,0:T(8,128)} async-done(((f32[768,3]{1,0:T(8,128)}), f32[96,3]{1,0:T(8,128)}) %reduce-scatter.27.cloned.1.call-update) | async-done | bytes 1168
  1134.4 67.0 %reduce-scatter.21.cloned.1.call-done = f32[96,576]{1,0:T(8,128)} async-done(((f32[768,576]{1,0:T(8,128)}), f32[96,576]{1,0:T(8,128)}) %reduce-scatter.21.cloned.1.call-update) | async-done | bytes 221200
  1203.4 400.4 %reduce-scatter.19.cloned.1.call-done = f32[96,8000]{1,0:T(8,128)} async-done(((f32[768,8000]{1,0:T(8,128)}), f32[96,8000]{1,0:T(8,128)}) %reduce-scatter.19.cloned.1.call-update) | async-done | bytes 3072016
  1616.2 39.6 %all-reduce.8 = (f32[]{:T(128)}, f32[]{:T(128)}, f32[]{:T(128)}) all-reduce(f32[]{:T(128)S(6)} %add.875, f32[]{:T(128)S(6)} %div.261, f32[]{:T(128)S(6)} %div.262), channel_id=1, replica_groups=mesh['dp'=8,'tensor'=4] {'dp','tensor'}, use_global_device_ids=true, to_apply=%region_61.62 | all-reduce | flops 3 | bytes 24 | tf_op jit(solution)/shard_map/psum | solution.py:416
  (621 shorter events, 263.7 us)
Async XLA Ops:
  7.2 453.9 %copy-start = (s32[128]{0:T(128)S(1)}, s32[128]{0:T(128)}, u32[]{:S(2)}) copy-start(s32[128]{0:T(128)} %param.39) | copy-start | bytes 1540
  7.2 198.1 %all-gather.8.cloned.1.call-start = ((), (), s32[]{:S(2)}) async-start(), calls=%async_computation.10 | async-start | bytes 13934592 | tf_op jit(solution)/shard_map/all_gather | solution.py:142
  10.5 251.1 %all-reduce.17.cloned.1.call-start = ((), (), s32[]{:S(2)}) async-start(), calls=%async_computation.11 | async-start | bytes 786432 | tf_op jit(solution)/shard_map/psum | solution.py:74
  79.1 37.7 %copy-start.100 = (s32[2047]{0:T(1024)S(1)}, s32[2047]{0:T(1024)}, u32[]{:S(2)}) copy-start(s32[2047]{0:T(1024)} %param.43) | copy-start | bytes 24568
  80.0 182.7 %copy-start.14 = (bf16[3,768,192]{1,2,0:T(8,128)(2,1)}, bf16[3,768,192]{1,2,0:T(8,128)(2,1)S(1)}, u32[]{:S(2)}) copy-start(bf16[3,768,192]{1,2,0:T(8,128)(2,1)S(1)} %copy.256) | copy-start | bytes 2654212
  80.7 313.0 %copy-start.71 = (s32[1024]{0:T(1024)}, s32[1024]{0:T(1024)S(1)}, u32[]{:S(2)}) copy-start(s32[1024]{0:T(1024)S(1)} %pad_clamp_fusion.2) | copy-start | bytes 12292
  80.7 148.2 %copy-start.86 = (pred[128]{0:T(512)(128)(4,1)}, pred[128]{0:T(512)(128)(4,1)S(1)}, u32[]{:S(2)}) copy-start(pred[128]{0:T(512)(128)(4,1)S(1)} %get-tuple-element.1704) | copy-start | bytes 388
  81.4 181.4 %copy-start.57 = (f32[768]{0:T(1024)}, f32[768]{0:T(1024)S(1)}, u32[]{:S(2)}) copy-start(f32[768]{0:T(1024)S(1)} %get-tuple-element.1550) | copy-start | bytes 9220
  81.4 312.2 %copy-start.61 = (f32[768]{0:T(1024)}, f32[768]{0:T(1024)S(1)}, u32[]{:S(2)}) copy-start(f32[768]{0:T(1024)S(1)} %get-tuple-element.1549) | copy-start | bytes 9220
  81.4 467.3 %copy-start.63 = (f32[768]{0:T(1024)}, f32[768]{0:T(1024)S(1)}, u32[]{:S(2)}) copy-start(f32[768]{0:T(1024)S(1)} %get-tuple-element.1548) | copy-start | bytes 9220
  229.8 162.6 %all-reduce.19.cloned.1.call-start = ((), (), s32[]{:S(2)}) async-start(), calls=%async_computation.12 | async-start | bytes 786432 | tf_op jit(solution)/shard_map/psum | solution.py:74
  410.4 42.6 %copy-start.9 = (f32[768,384]{1,0:T(8,128)S(1)}, f32[768,384]{1,0:T(8,128)}, u32[]{:S(2)}) copy-start(f32[768,384]{1,0:T(8,128)} %param.56) | copy-start | bytes 3538948
  456.6 43.7 %copy-start.103 = (u32[32]{0:T(128)S(1)}, u32[32]{0:T(128)}, u32[]{:S(2)}) copy-start(u32[32]{0:T(128)} %constant.623) | copy-start | bytes 388
  456.6 48.0 %all-to-all-start.1 = ((bf16[8,128,768]{2,1,0:T(8,128)(2,1)}), bf16[8,128,768]{2,1,0:T(8,128)(2,1)S(1)}, u32[]{:S(2)}, u32[]{:S(2)}) async-start(bf16[8,128,768]{2,1,0:T(8,128)(2,1)} %bitcast.433), calls=%async_computation.1 | async-start | bytes 3145728 | tf_op jit(solution)/shard_map/all_to_all | solution.py:78
  460.3 87.1 %all-reduce.21.cloned.1.call-start = ((), (), s32[]{:S(2)}) async-start(), calls=%async_computation.13 | async-start | bytes 786432 | tf_op jit(solution)/shard_map/psum | solution.py:74
  501.6 62.2 %copy-start.82 = (f32[16]{0:T(128)}, f32[16]{0:T(128)S(1)}, u32[]{:S(2)}) copy-start(f32[16]{0:T(128)S(1)} %compare_convert_fusion.1) | copy-start | bytes 196
  511.1 95.0 %all-reduce.23.cloned.1.call-start = ((), (), s32[]{:S(2)}) async-start(), calls=%async_computation.14 | async-start | bytes 786432 | tf_op jit(solution)/shard_map/psum | solution.py:74
  511.3 52.5 %copy-start.74 = (s32[16]{0:T(128)}, s32[16]{0:T(128)S(1)}, u32[]{:S(2)}) copy-start(s32[16]{0:T(128)S(1)} %broadcast_subtract_fusion) | copy-start | bytes 196
  563.8 42.2 %copy-start.64 = (f32[768]{0:T(1024)S(1)}, f32[768]{0:T(1024)}, u32[]{:S(2)}) copy-start(f32[768]{0:T(1024)} %copy-done.63) | copy-start | bytes 9220
  635.2 41.5 %copy-start.33 = (f32[1024,384]{1,0:T(8,128)S(1)}, f32[1024,384]{1,0:T(8,128)}, u32[]{:S(2)}) copy-start(f32[1024,384]{1,0:T(8,128)} %copy-done.32) | copy-start | bytes 4718596
  635.2 41.5 %copy-start.41 = (f32[384,768]{1,0:T(8,128)S(1)}, f32[384,768]{1,0:T(8,128)}, u32[]{:S(2)}) copy-start(f32[384,768]{1,0:T(8,128)} %param.59) | copy-start | bytes 3538948
  680.7 40.1 %all-to-all-start.3 = ((bf16[8,128,768]{2,1,0:T(8,128)(2,1)}), bf16[8,128,768]{2,1,0:T(8,128)(2,1)S(1)}, u32[]{:S(2)}, u32[]{:S(2)}) async-start(bf16[8,128,768]{2,1,0:T(8,128)(2,1)} %bitcast.426), calls=%async_computation.3 | async-start | bytes 3145728 | tf_op jit(solution)/shard_map/all_to_all | solution.py:78
  684.3 75.3 %all-reduce.25.cloned.1.call-start = ((), (), s32[]{:S(2)}) async-start(), calls=%async_computation.15 | async-start | bytes 786432 | tf_op jit(solution)/shard_map/psum | solution.py:74
  728.1 173.6 %reduce-scatter.17.cloned.1.call-start = ((), (), s32[]{:S(2)}) async-start(), calls=%async_computation.16 | async-start | bytes 1769472 | tf_op jit(solution)/shard_map/reduce_scatter | solution.py:382
  836.0 66.7 %copy-start.15 = (bf16[3,768,192]{1,2,0:T(8,128)(2,1)S(1)}, bf16[3,768,192]{1,2,0:T(8,128)(2,1)}, u32[]{:S(2)}) copy-start(bf16[3,768,192]{1,2,0:T(8,128)(2,1)} %copy-done.14) | copy-start | bytes 2654212
  836.0 67.9 %copy-start.70 = (bf16[128,4]{0,1:T(4,128)(2,1)S(1)}, bf16[128,4]{0,1:T(4,128)(2,1)}, u32[]{:S(2)}) copy-start(bf16[128,4]{0,1:T(4,128)(2,1)} %copy-done.69) | copy-start | bytes 3076
  836.0 100.2 %all-reduce.27.cloned.1.call-start = ((), (), s32[]{:S(2)}) async-start(), calls=%async_computation.17 | async-start | bytes 786432 | tf_op jit(solution)/shard_map/psum | solution.py:74
  903.9 99.2 %reduce-scatter.25.cloned.1.call-start = ((), (), s32[]{:S(2)}) async-start(), calls=%async_computation.21 | async-start | bytes 442368
  905.0 162.4 %reduce-scatter.23.cloned.1.call-start = ((), (), s32[]{:S(2)}) async-start(), calls=%async_computation.20 | async-start | bytes 884736
  906.3 225.3 %reduce-scatter.27.cloned.1.call-start = ((), (), s32[]{:S(2)}) async-start(), calls=%async_computation.22 | async-start | bytes 442368
  938.4 263.1 %reduce-scatter.21.cloned.1.call-start = ((), (), s32[]{:S(2)}) async-start(), calls=%async_computation.19 | async-start | bytes 2211840
  946.7 657.1 %reduce-scatter.19.cloned.1.call-start = ((), (), s32[]{:S(2)}) async-start(), calls=%async_computation.18 | async-start | bytes 27869184
  (102 other events, 822.3 us)
Sparse Core Ops, SparseCore 0:
  10.8 194.4 all-gather.7
  229.9 31.6 all-reduce.16
  363.0 29.3 all-reduce.18
  511.2 36.2 all-reduce.20
  573.3 32.7 all-reduce.22
  728.2 31.2 all-reduce.24
  836.2 65.5 reduce-scatter.16
  904.7 31.4 all-reduce.26
  940.4 61.3 reduce-scatter.24
  1005.9 61.4 reduce-scatter.22
  1071.3 60.3 reduce-scatter.26
  1135.6 65.8 reduce-scatter.20
  1206.0 397.8 reduce-scatter.18
where the time goes:
time: 1700 us; the launch traced here: 1680 us
  waiting for transfers between devices  938 us (55%)
  blocking collectives  350 us (21%)
  local copies, waits for them, and re-layouts  219 us (13%)
  other arithmetic  82.9 us (5%)
  matrix products  54.8 us (3%)
  between operations  25.2 us (1%)
    unnamed x18, waiting for transfers between devices  565 us
    psum x6, waiting for transfers between devices, tensor_total(): return lax.psum(value, 'tensor')  190 us
    all_gather x1, waiting for transfers between devices, local(): lax.all_gather(embedding.astype(bf16), 'dp', axis=1, tiled=True)  88.3 us
    all_to_all x2, blocking collectives, route_exchange(): return lax.all_to_all(value, 'dp', split_axis=0, concat_axis=0, tiled=True)  82.9 us
    reduce_scatter x1, waiting for transfers between devices, local(): lax.psum_scatter(ordered, 'dp', scatter_dimension=1, tiled=True)  64.8 us
    unnamed x214, local copies, waits for them, and re-layouts  52.3 us
    all_gather x1, blocking collectives, local(): lax.all_gather(attn_proj.astype(bf16), 'dp', axis=1, tiled=True)  43 us
    psum x1, blocking collectives, local(): lax.psum((squares, loss_local / tensor_count, jnp.sum(weight) / tensor_co...  39.6 us
  transfers between devices with their start and end apart: 15, of which 13 were waited for; matrix products, arithmetic and copies ran while one was open for 5% of the time, Pallas kernels for 0%

commit v1 on v0

--- a/solution.py
+++ b/solution.py
@@ -91,6 +91,436 @@
     fixed_second = second / (1 - BETA2**STEP)
     weight = weight - rate * (fixed_first / (jnp.sqrt(fixed_second) + ADAM_EPS) + decay * weight)
     return (weight, first, second)
+
+
+def wide_norm_back(v, g, upstream):
+    size = v.shape[-1]
+    root = lax.rsqrt(jnp.mean(v * v, -1, keepdims=True) + NORM_EPS)
+    scaled = g * upstream
+    inner = jnp.sum(scaled * v, -1, keepdims=True)
+    return (root * scaled - v * (root * root * root * inner / size), jnp.sum(upstream * v * root, 0))
+
+
+def fast_local(
+    token_ids,
+    targets,
+    loss_offsets,
+    routes,
+    picture_start,
+    buckets,
+    embedding,
+    embedding_first,
+    embedding_second,
+    attn_proj,
+    attn_proj_first,
+    attn_proj_second,
+    out_proj,
+    out_proj_first,
+    out_proj_second,
+    router,
+    router_first,
+    router_second,
+    expert_in,
+    expert_in_first,
+    expert_in_second,
+    expert_out,
+    expert_out_first,
+    expert_out_second,
+    norm_gains,
+    norm_gains_first,
+    norm_gains_second,
+    position_bias,
+    position_bias_first,
+    position_bias_second,
+):
+    f32 = jnp.float32
+    bf16 = jnp.bfloat16
+    dp_count = lax.axis_size("dp")
+    tensor_count = lax.axis_size("tensor")
+    dp_place = lax.axis_index("dp")
+    tensor_place = lax.axis_index("tensor")
+    rows = token_ids.shape[0]
+    every = rows * dp_count
+    picks = loss_offsets.shape[0]
+    all_picks = picks * dp_count
+    scale = 1.0 / math.sqrt(HD)
+    vocab_rows, columns = embedding.shape
+    features = columns * dp_count
+    width = attn_proj.shape[2]
+    heads = width // HD
+    experts = router.shape[0]
+    both = ("dp", "tensor")
+    loss_hot = loss_offsets[:, None] == jnp.arange(rows, dtype=jnp.int32)[None, :]
+
+    def at_loss(values):
+        return jnp.sum(jnp.where(loss_hot, values[None, :], 0), 1)
+
+    packed = jnp.concatenate(
+        [token_ids, loss_offsets, at_loss(targets), at_loss(routes[:, 0]), at_loss(routes[:, 1])]
+    )
+    known = lax.all_gather(packed, "dp")
+    ids = known[:, :rows].reshape(every)
+    offsets, wanted, route_a, route_b = (
+        known[:, rows + k * picks : rows + (k + 1) * picks].reshape(all_picks) for k in range(4)
+    )
+    pick_block = jnp.arange(all_picks, dtype=jnp.int32) // picks
+    loss_rows = offsets + pick_block * rows
+    projection = lax.all_gather(attn_proj.astype(bf16), "dp", axis=1, tiled=True)
+    output_map = lax.all_gather(
+        lax.all_gather(out_proj.astype(bf16), "dp", axis=1, tiled=True),
+        "tensor",
+        axis=0,
+        tiled=True,
+    )
+    router_full = lax.all_gather(router.astype(bf16), "dp", axis=1, tiled=True)
+    gain = lax.all_gather(norm_gains.astype(bf16), "dp", axis=1, tiled=True).astype(f32)
+    own_gain = norm_gains.astype(bf16).astype(f32)
+    table_rows = lax.all_to_all(
+        embedding.astype(bf16), "dp", split_axis=0, concat_axis=1, tiled=True
+    )
+    place = ids - tensor_place * vocab_rows
+    owned = (place >= 0) & (place < vocab_rows)
+    looked = jnp.take(embedding, jnp.clip(place, 0, vocab_rows - 1), axis=0)
+    looked = jnp.where(owned[:, None], looked, 0.0).astype(bf16)
+    stream_in = lax.psum(
+        lax.all_to_all(looked, "dp", split_axis=0, concat_axis=1, tiled=True).astype(f32), "tensor"
+    )
+    in_columns = lax.psum(looked.astype(f32), "tensor")
+    root_in = lax.rsqrt(jnp.mean(stream_in * stream_in, -1, keepdims=True) + NORM_EPS)
+    normed_in = (stream_in * root_in * gain[0]).astype(bf16)
+    fresh = jnp.einsum("td,sde->ste", normed_in, projection, preferred_element_type=f32).astype(
+        bf16
+    )
+    loss_one = loss_hot.astype(bf16)
+    own_query = jnp.dot(loss_one, fresh[0], preferred_element_type=f32).astype(bf16)
+    own_stream = jnp.dot(
+        loss_one, stream_in.astype(bf16), preferred_element_type=f32
+    ).astype(bf16)
+    keys, values, query, stream_picked, root_all = (
+        lax.all_gather(part, "dp", axis=0, tiled=True)
+        for part in (fresh[1], fresh[2], own_query, own_stream, root_in)
+    )
+    stream_picked = stream_picked.astype(f32)
+    in_columns_normed = (in_columns * root_all * own_gain[0]).astype(bf16)
+    flipped = jnp.pad(jnp.flip(buckets), (0, 1)).astype(bf16)
+    period = 2 * every
+    shifted = jnp.tile(flipped, rows + 1)[: rows * (period + 1)].reshape(rows, period + 1)
+    shifted = shifted[:, : period - rows]
+    turn = (rows - 1 - offsets)[:, None] == jnp.arange(rows, dtype=jnp.int32)[None, :]
+    shifted = jnp.dot(turn.astype(bf16), shifted, preferred_element_type=f32)
+    bucket = jnp.concatenate(
+        [
+            shifted[
+                picks * k : picks * (k + 1),
+                rows * (dp_count - 1 - k) : rows * (dp_count - 1 - k) + every,
+            ]
+            for k in range(dp_count)
+        ]
+    ).astype(jnp.int32)
+    position = jnp.arange(every, dtype=jnp.int32)
+    key_picture = picture_of(position, picture_start[0], PIECE)
+    query_picture = picture_of(loss_rows, picture_start[0], PIECE)
+    allowed = (position[None, :] <= loss_rows[:, None]) | (
+        (key_picture[None, :] == query_picture[:, None]) & (query_picture[:, None] >= 0)
+    )
+    bucket_count = position_bias.shape[1]
+
+    def head(value, h):
+        return value[:, h * HD : (h + 1) * HD]
+
+    def scores_of(h):
+        raw = lax.dot_general(
+            head(query, h), head(keys, h), (((1,), (1,)), ((), ())), preferred_element_type=f32
+        )
+        bias = jnp.zeros(bucket.shape, f32)
+        for b in range(bucket_count):
+            bias = jnp.where(bucket == b, position_bias[h, b], bias)
+        return jnp.where(allowed, raw * scale + bias, NEGATIVE)
+
+    probs = []
+    for h in range(heads):
+        raw = scores_of(h)
+        terms = jnp.exp(raw - jnp.max(raw, -1, keepdims=True))
+        probs.append(terms / jnp.sum(terms, -1, keepdims=True))
+    attended = jnp.concatenate(
+        [
+            jnp.dot(probs[h].astype(bf16), head(values, h), preferred_element_type=f32)
+            for h in range(heads)
+        ],
+        1,
+    )
+    attended_low = attended.astype(bf16)
+    attended_all = lax.all_gather(attended_low, "tensor", axis=1, tiled=True)
+    stream_mid = stream_picked + jnp.dot(attended_all, output_map, preferred_element_type=f32)
+    normed_mid = normed(stream_mid, gain[1]).astype(bf16)
+    router_logits = jnp.dot(normed_mid, router_full.T, preferred_element_type=f32)
+    expert_ids = jnp.arange(experts, dtype=jnp.int32)[None, :]
+    hot_a = route_a[:, None] == expert_ids
+    hot_b = route_b[:, None] == expert_ids
+    logit_a = jnp.sum(jnp.where(hot_a, router_logits, 0.0), 1)
+    logit_b = jnp.sum(jnp.where(hot_b, router_logits, 0.0), 1)
+    logit_top = jnp.maximum(logit_a, logit_b)
+    gate_a, gate_b = jnp.exp(logit_a - logit_top), jnp.exp(logit_b - logit_top)
+    gate_a, gate_b = gate_a / (gate_a + gate_b), gate_b / (gate_a + gate_b)
+    spread = dp_count * tensor_count // experts
+    expert = (dp_place * tensor_count + tensor_place) // spread
+    gate = jnp.where(route_a == expert, gate_a, 0.0) + jnp.where(route_b == expert, gate_b, 0.0)
+    in_low = expert_in.astype(bf16)
+    out_low = expert_out.astype(bf16)
+    inner = jnp.dot(normed_mid, in_low, preferred_element_type=f32)
+    active = jax.nn.gelu(inner).astype(bf16)
+    piece = jnp.dot(active, out_low, preferred_element_type=f32).astype(bf16).astype(f32)
+    mixed = lax.psum(gate[:, None] * piece, both)
+    stream_out = stream_mid + mixed
+    normed_out = normed(stream_out, gain[2]).astype(bf16)
+    logits = lax.dot_general(
+        normed_out, table_rows, (((1,), (1,)), ((), ())), preferred_element_type=f32
+    )
+    share = table_rows.shape[0]
+    first_id = tensor_place * vocab_rows + dp_place * share
+    hit = jnp.arange(share, dtype=jnp.int32)[None, :] == (wanted - first_id)[:, None]
+    local_top = jnp.max(logits, -1)
+    stats = jnp.stack(
+        [
+            local_top,
+            jnp.sum(jnp.exp(logits - local_top[:, None]), -1),
+            jnp.sum(jnp.where(hit, logits, 0.0), -1),
+            jnp.sum(logits, -1),
+        ]
+    )
+    stats = lax.all_gather(stats, both)
+    peak = jnp.max(stats[:, 0], 0)
+    vocab_total = jnp.sum(stats[:, 1] * jnp.exp(stats[:, 0] - peak), 0)
+    target_logit = jnp.sum(stats[:, 2], 0)
+    logit_sum = jnp.sum(stats[:, 3], 0)
+    loss_total = peak + jnp.log(vocab_total)
+    weight = (query_picture < 0).astype(f32)
+    per_row = (
+        loss_total
+        - (1 - SMOOTH) * target_logit
+        - SMOOTH * logit_sum / VOCAB
+        + ZLOSS * loss_total * loss_total
+    )
+    loss_sum = jnp.sum(weight * per_row)
+    loss_count = jnp.sum(weight)
+    soft = jnp.exp(logits - loss_total[:, None])
+    d_logits = (
+        weight[:, None]
+        * (
+            (1 + 2 * ZLOSS * loss_total)[:, None] * soft
+            - (1 - SMOOTH) * hit.astype(f32)
+            - SMOOTH / VOCAB
+        )
+    ).astype(bf16)
+    d_logits_all = lax.all_gather(d_logits, "dp", axis=1, tiled=True)
+    d_normed_out = lax.psum(jnp.dot(d_logits, table_rows, preferred_element_type=f32), both)
+    d_stream_out, grad_final = wide_norm_back(stream_out, gain[2], d_normed_out)
+    d_piece = (gate[:, None] * d_stream_out).astype(bf16)
+    d_active = lax.dot_general(
+        d_piece, out_low, (((1,), (1,)), ((), ())), preferred_element_type=f32
+    )
+    unused, gelu_pull = jax.vjp(jax.nn.gelu, inner)
+    d_inner = gelu_pull(d_active)[0].astype(bf16)
+    grad_out = jnp.dot(active.T, d_piece, preferred_element_type=f32)
+    grad_in = jnp.dot(normed_mid.T, d_inner, preferred_element_type=f32)
+    sent_back = lax.dot_general(
+        d_inner, in_low, (((1,), (1,)), ((), ())), preferred_element_type=f32
+    ).astype(bf16)
+    gate_part = jnp.sum(d_stream_out * piece, -1)
+    gate_part = jnp.where(expert_ids == expert, gate_part[:, None], 0.0)
+    d_from_experts, d_gates = lax.psum((sent_back.astype(f32), gate_part), both)
+    d_gate_a = jnp.sum(jnp.where(hot_a, d_gates, 0.0), 1)
+    d_gate_b = jnp.sum(jnp.where(hot_b, d_gates, 0.0), 1)
+    d_mean = gate_a * d_gate_a + gate_b * d_gate_b
+    d_router_logits = (
+        jnp.where(hot_a, (gate_a * (d_gate_a - d_mean))[:, None], 0.0)
+        + jnp.where(hot_b, (gate_b * (d_gate_b - d_mean))[:, None], 0.0)
+    ).astype(bf16)
+
+    def own_columns(value):
+        return lax.dynamic_slice_in_dim(value, dp_place * columns, columns, value.ndim - 1)
+
+    grad_router = own_columns(
+        jnp.dot(d_router_logits.T, normed_mid, preferred_element_type=f32)
+    )
+    d_normed_mid = d_from_experts + jnp.dot(
+        d_router_logits, router_full, preferred_element_type=f32
+    )
+    d_from_mid, grad_middle = wide_norm_back(stream_mid, gain[1], d_normed_mid)
+    d_stream_mid = d_stream_out + d_from_mid
+    d_attn_low = d_stream_mid.astype(bf16)
+    grad_output_map = jnp.dot(
+        attended_low.T, own_columns(d_attn_low), preferred_element_type=f32
+    )
+    own_map = lax.dynamic_slice_in_dim(output_map, tensor_place * width, width, 0)
+    d_attended = lax.dot_general(
+        d_attn_low, own_map, (((1,), (1,)), ((), ())), preferred_element_type=f32
+    ).astype(bf16)
+    d_queries, d_keys, d_values, bias_terms = [], [], [], []
+    for h in range(heads):
+        d_head = head(d_attended, h)
+        d_probs = lax.dot_general(
+            d_head, head(values, h), (((1,), (1,)), ((), ())), preferred_element_type=f32
+        )
+        d_scores = probs[h] * (d_probs - jnp.sum(probs[h] * d_probs, -1, keepdims=True))
+        d_scores = d_scores.astype(bf16)
+        d_queries.append(
+            jnp.dot(d_scores, head(keys, h), preferred_element_type=f32) * scale
+        )
+        d_keys.append(
+            jnp.dot(d_scores.T, head(query, h), preferred_element_type=f32) * scale
+        )
+        d_values.append(
+            jnp.dot(probs[h].astype(bf16).T, d_head, preferred_element_type=f32)
+        )
+        wide = d_scores.astype(f32)
+        bias_terms.append(
+            jnp.stack([jnp.sum(jnp.where(bucket == b, wide, 0.0)) for b in range(bucket_count)])
+        )
+    sum_bias = jnp.stack(bias_terms)
+    d_query = jnp.concatenate(d_queries, 1).astype(bf16)
+    d_key = jnp.concatenate(d_keys, 1).astype(bf16)
+    d_value = jnp.concatenate(d_values, 1).astype(bf16)
+    back_hot = (loss_rows[None, :] == position[:, None]).astype(bf16)
+    in_picked = jnp.dot(
+        back_hot.T, in_columns_normed, preferred_element_type=f32
+    ).astype(bf16)
+    sum_proj = jnp.stack(
+        [
+            jnp.dot(in_picked.T, d_query, preferred_element_type=f32),
+            jnp.dot(in_columns_normed.T, d_key, preferred_element_type=f32),
+            jnp.dot(in_columns_normed.T, d_value, preferred_element_type=f32),
+        ]
+    )
+    d_query_all = jnp.dot(back_hot, d_query, preferred_element_type=f32).astype(bf16)
+    query_all = jnp.dot(back_hot, query, preferred_element_type=f32)
+    own_proj = attn_proj.astype(bf16)
+    d_columns = sum(
+        lax.dot_general(part, own_proj[s], (((1,), (1,)), ((), ())), preferred_element_type=f32)
+        for s, part in enumerate((d_query_all, d_key, d_value))
+    )
+    d_inner_in = jnp.sum(
+        d_query_all.astype(f32) * query_all
+        + d_key.astype(f32) * keys.astype(f32)
+        + d_value.astype(f32) * values.astype(f32),
+        -1,
+        keepdims=True,
+    )
+    d_columns, d_inner_in = lax.psum((d_columns, d_inner_in), "tensor")
+    grad_first = jnp.sum(d_columns * in_columns * root_all, 0)
+    own_stream_mid = own_columns(d_stream_mid)
+    stream_high = own_stream_mid.astype(bf16)
+    stream_low = (own_stream_mid - stream_high.astype(f32)).astype(bf16)
+    d_stream_in = (
+        root_all * own_gain[0] * d_columns
+        - in_columns * (root_all * root_all * d_inner_in / features)
+        + jnp.dot(back_hot, stream_high, preferred_element_type=f32)
+        + jnp.dot(back_hot, stream_low, preferred_element_type=f32)
+    )
+    sum_table = lax.dot_general(
+        d_logits_all, own_columns(normed_out), (((0,), (0,)), ((), ())), preferred_element_type=f32
+    )
+    d_high = d_stream_in.astype(bf16)
+    d_low = (d_stream_in - d_high.astype(f32)).astype(bf16)
+    id_hot = (jnp.arange(vocab_rows, dtype=jnp.int32)[:, None] == place[None, :]).astype(bf16)
+    scattered = jnp.dot(
+        id_hot, jnp.concatenate([d_high, d_low], 1), preferred_element_type=f32
+    )
+    sum_table = sum_table + scattered[:, :columns] + scattered[:, columns:]
+    sum_router = grad_router
+    sum_gains = jnp.stack([grad_first, own_columns(grad_middle), own_columns(grad_final)])
+    squares = (
+        jnp.sum(sum_table * sum_table)
+        + jnp.sum(sum_proj * sum_proj)
+        + jnp.sum(grad_output_map * grad_output_map)
+        + jnp.sum(grad_in * grad_in)
+        + jnp.sum(grad_out * grad_out)
+        + (jnp.sum(sum_router * sum_router) + jnp.sum(sum_gains * sum_gains)) / tensor_count
+        + jnp.sum(sum_bias * sum_bias) / dp_count
+    )
+    grad_norm = jnp.sqrt(lax.psum(squares, both))
+    clip = MAX_NORM / jnp.maximum(grad_norm, MAX_NORM)
+    params = (
+        embedding,
+        attn_proj,
+        out_proj,
+        router,
+        expert_in,
+        expert_out,
+        norm_gains,
+        position_bias,
+    )
+    firsts = (
+        embedding_first,
+        attn_proj_first,
+        out_proj_first,
+        router_first,
+        expert_in_first,
+        expert_out_first,
+        norm_gains_first,
+        position_bias_first,
+    )
+    seconds = (
+        embedding_second,
+        attn_proj_second,
+        out_proj_second,
+        router_second,
+        expert_in_second,
+        expert_out_second,
+        norm_gains_second,
+        position_bias_second,
+    )
+    grads = (
+        sum_table,
+        sum_proj,
+        grad_output_map,
+        sum_router,
+        grad_in,
+        grad_out,
+        sum_gains,
+        sum_bias,
+    )
+    results = []
+    for index in range(8):
+        results.extend(
+            adam_update(
+                params[index],
+                firsts[index],
+                seconds[index],
+                clip * grads[index],
+                RATES[index],
+                DECAYS[index],
+            )
+        )
+    return (
+        results[0],
+        results[1],
+        results[2],
+        results[3],
+        results[4],
+        results[5],
+        results[6],
+        results[7],
+        results[8],
+        results[9],
+        results[10],
+        results[11],
+        results[12],
+        results[13],
+        results[14],
+        results[15],
+        results[16],
+        results[17],
+        results[18],
+        results[19],
+        results[20],
+        results[21],
+        results[22],
+        results[23],
+        grad_norm,
+        loss_sum,
+        loss_count,
+    )
 
 
 def local(
@@ -554,4 +984,14 @@
         P(),
         P(),
     )
-    return jax.shard_map(local, mesh=mesh, in_specs=in_specs, out_specs=out_specs, check_vma=False)
+
+    def chosen(*arrays):
+        token_ids, routes, embedding, router = arrays[0], arrays[3], arrays[6], arrays[9 + 6]
+        rows = token_ids.shape[0]
+        dp_count, tensor_count = lax.axis_size("dp"), lax.axis_size("tensor")
+        single = rows * dp_count <= SEQ and arrays[4].shape[0] == 1
+        even = embedding.shape[0] % dp_count == 0
+        whole = dp_count * tensor_count % router.shape[0] == 0 and routes.shape[1] == 2
+        return (fast_local if single and even and whole else local)(*arrays)
+
+    return jax.shard_map(chosen, mesh=mesh, in_specs=in_specs, out_specs=out_specs, check_vma=False)

time: 1700 us -> 1100 us (0.65)
  waiting for transfers between devices: 938 us -> 334 us
  local copies, waits for them, and re-layouts: 219 us -> 119 us
  matrix products: 54.8 us -> 124 us
  blocking collectives: 350 us -> 417 us
    unnamed x18 -> x7, waiting for transfers between devices: 565 us -> 0.11 us
    psum x6 -> x5, waiting for transfers between devices: 190 us -> 333 us  [the longest x1 124 us: fast_local(): mixed = lax.psum(gate[:, None] * piece, both)]
    all_gather x6 -> x11, blocking collectives: 195 us -> 311 us  [the longest x5 137 us: fast_local(): lax.all_gather(part, 'dp', axis=0, tiled=True)]
    all_gather x1 -> x2, waiting for transfers between devices: 88.3 us -> 0.03 us  [the longest x1 0.02 us: fast_local(): d_logits_all = lax.all_gather(d_logits, 'dp', axis=1, tiled=True)]
    all_to_all x2 -> x1, blocking collectives: 82.9 us -> 10.4 us  [fast_local(): lax.all_to_all(looked, 'dp', split_axis=0, concat_axis=1, tiled=True)]
    dot_general x31 -> x47, matrix products: 51.1 us -> 122 us  [the longest x3 67.7 us: scores_of(): lax.dot_general(head(query, h), head(keys, h), (((1,), (1,)), ((), ())),...]
    reduce_scatter x1 -> x0, waiting for transfers between devices: 64.8 us -> none  [local(): lax.psum_scatter(ordered, 'dp', scatter_dimension=1, tiled=True)]
    another operation x7 -> x6, local copies, waits for them, and re-layouts: 4.24 us -> 67.7 us  [the longest x3 63.5 us: fast_local(): jnp.stack([jnp.sum(jnp.where(bucket == b, wide, 0.0)) for b in range(buck...]
  transfers between devices with their start and end apart: 15 -> 8, of which waited for: 13 -> 3; matrix products, arithmetic and copies ran while one was open for 5% -> 20% of each run, Pallas kernels for 0% -> 0%
where the time goes in v1:
time: 1100 us; the launch traced here: 1090 us
  blocking collectives  417 us (38%)
  waiting for transfers between devices  334 us (30%)
  matrix products  124 us (11%)
  local copies, waits for them, and re-layouts  119 us (11%)
  other arithmetic  67.7 us (6%)
  between operations  25.4 us (2%)
    all_gather x5, blocking collectives, fast_local(): lax.all_gather(part, 'dp', axis=0, tiled=True)  137 us
    psum x1, waiting for transfers between devices, fast_local(): mixed = lax.psum(gate[:, None] * piece, both)  124 us
    psum x1, waiting for transfers between devices, fast_local(): lax.psum(jnp.dot(d_logits, table_rows, preferred_element_type=f32), both)  122 us
    psum x1, waiting for transfers between devices, fast_local(): d_from_experts, d_gates = lax.psum((sent_back.astype(f32), gate_part), both)  87.1 us
    dot_general x3, matrix products, scores_of(): lax.dot_general(head(query, h), head(keys, h), (((1,), (1,)), ((), ())),...  67.7 us
    another operation x3, local copies, waits for them, and re-layouts, fast_local(): jnp.stack([jnp.sum(jnp.where(bucket == b, wide, 0.0)) for b in range(buck...  63.5 us
    all_gather x1, blocking collectives, fast_local(): lax.all_gather(out_proj.astype(bf16), 'dp', axis=1, tiled=True)  55.7 us
    all_gather x1, blocking collectives, fast_local(): stats = lax.all_gather(stats, both)  40.2 us
  transfers between devices with their start and end apart: 8, of which 3 were waited for; matrix products, arithmetic and copies ran while one was open for 20% of the time, Pallas kernels for 0%

profile of v1, /device:TPU:0, one launch (start us, length us, event | category | flops | bytes accessed | tf_op | source)
XLA Modules:
  0.0 1090.7 jit_solution(12020123117213397210)
XLA Ops:
  11.8 13.2 %all-reduce.1 = s32[1536]{0:T(1024)S(1)} all-reduce(s32[1536]{0:T(1024)S(1)} %dynamic-update-slice), channel_id=2, replica_groups=mesh['dp'=8,'tensor'=4] {'dp'}, use_global_device_ids=true, to_apply=%add.1 | all-reduce | flops 1536 | bytes 12288
  25.0 4.3 copy.117
  30.0 4.9 gather_fusion
  35.8 10.4 all_to_all.29
  48.3 4.9 all_to_all.23
  56.6 4.4 all-to-all-start.1
  61.2 55.7 %all_gather.57 = bf16[192,768]{0,1:T(8,128)(2,1)} all-gather(bf16[192,96]{0,1:T(8,128)(2,1)S(1)} %copy.123), channel_id=1, replica_groups=mesh['dp'=8,'tensor'=4] {'dp'}, dimensions={1}, use_global_device_ids=true | all-gather | bytes 331776 | tf_op jit(solution)/shard_map/all_gather | solution.py:170
  139.7 37.6 %all_gather.52 = bf16[3,768,192]{2,0,1:T(4,128)(2,1)} all-gather(bf16[3,96,192]{2,0,1:T(4,128)(2,1)S(1)} %copy.120), channel_id=1, replica_groups=mesh['dp'=8,'tensor'=4] {'dp'}, dimensions={1}, use_global_device_ids=true | all-gather | bytes 995328 | tf_op jit(solution)/shard_map/all_gather | solution.py:168
  180.8 18.1 %all-gather.5 = bf16[8,96,3]{1,2,0:T(4,128)(2,1)S(1)} all-gather(bf16[1,96,3]{1,2,0:T(4,128)(2,1)S(1)} %convert_bitcast_fusion.2), channel_id=1, replica_groups=mesh['dp'=8,'tensor'=4] {'dp'}, dimensions={0}, use_global_device_ids=true | all-gather | bytes 5184 | tf_op jit(solution)/shard_map/all_gather | solution.py:176
  200.8 16.5 %all-gather.6 = bf16[8,96,4]{1,2,0:T(4,128)(2,1)S(1)} all-gather(bf16[1,96,4]{1,2,0:T(4,128)(2,1)S(1)} %convert_bitcast_fusion.1), channel_id=1, replica_groups=mesh['dp'=8,'tensor'=4] {'dp'}, dimensions={0}, use_global_device_ids=true | all-gather | bytes 6912 | tf_op jit(solution)/shard_map/all_gather | solution.py:175
  223.9 26.8 %all-gather.1 = bf16[1,1024,192]{1,2,0:T(8,128)(2,1)S(1)} all-gather(bf16[1,128,192]{1,2,0:T(8,128)(2,1)S(1)} %get-tuple-element.270), channel_id=3, replica_groups=mesh['dp'=8,'tensor'=4] {'dp'}, dimensions={1}, use_global_device_ids=true | all-gather | bytes 442368 | tf_op jit(solution)/shard_map/all_gather | solution.py:200
  250.7 30.7 %all_gather.53 = bf16[128,192]{1,0:T(8,128)(2,1)S(1)} all-gather(bf16[16,192]{1,0:T(8,128)(2,1)S(1)} %convolution_convert_fusion.12), channel_id=1, replica_groups=mesh['dp'=8,'tensor'=4] {'dp'}, dimensions={0}, use_global_device_ids=true | all-gather | bytes 55296 | tf_op jit(solution)/shard_map/all_gather | solution.py:200
  281.7 23.3 %fusion.254 = (f32[128]{0:T(128)S(1)}, f32[128,1024]{1,0:T(8,128)S(1)}) fusion(pred[128,1024]{1,0:T(32,128)(4,1)S(1)} %copy-done.74, pred[128,1024]{1,0:T(32,128)(4,1)S(1)} %copy-done.94, pred[128,1024]{1,0:T(32,128)(4,1)S(1)} %copy-done.96, pred[128,1024]{1,0:T(32,128)(4,1)S(1)} %copy-done.98, pred[128,1024]{1,0:T(32,128)(4,1)S(1)} %copy-done.100, ...), kind=kOutput, calls=%fused_computation.572 | convolution fusion | flops 22019968 | bytes 4888704 | tf_op jit(solution)/shard_map/dot_general | solution.py:232
  305.5 26.7 %all-gather.2 = bf16[1,1024,192]{1,2,0:T(8,128)(2,1)S(1)} all-gather(bf16[1,128,192]{1,2,0:T(8,128)(2,1)S(1)} %get-tuple-element.269), channel_id=4, replica_groups=mesh['dp'=8,'tensor'=4] {'dp'}, dimensions={1}, use_global_device_ids=true | all-gather | bytes 442368 | tf_op jit(solution)/shard_map/all_gather | solution.py:200
  332.3 21.9 %fusion.255 = (f32[128]{0:T(128)S(1)}, f32[128,1024]{1,0:T(8,128)S(1)}) fusion(pred[128,1024]{1,0:T(32,128)(4,1)S(1)} %copy-done.74, pred[128,1024]{1,0:T(32,128)(4,1)S(1)} %copy-done.94, pred[128,1024]{1,0:T(32,128)(4,1)S(1)} %copy-done.96, pred[128,1024]{1,0:T(32,128)(4,1)S(1)} %copy-done.98, pred[128,1024]{1,0:T(32,128)(4,1)S(1)} %copy-done.100, ...), kind=kOutput, calls=%fused_computation.573 | convolution fusion | flops 22019968 | bytes 4888704 | tf_op jit(solution)/shard_map/dot_general | solution.py:232
  354.5 22.5 %fusion.256 = (f32[128]{0:T(128)S(1)}, f32[128,1024]{1,0:T(8,128)S(1)}) fusion(pred[128,1024]{1,0:T(32,128)(4,1)S(1)} %copy-done.74, pred[128,1024]{1,0:T(32,128)(4,1)S(1)} %copy-done.94, pred[128,1024]{1,0:T(32,128)(4,1)S(1)} %copy-done.96, pred[128,1024]{1,0:T(32,128)(4,1)S(1)} %copy-done.98, pred[128,1024]{1,0:T(32,128)(4,1)S(1)} %copy-done.100, ...), kind=kOutput, calls=%fused_computation.574 | convolution fusion | flops 22019968 | bytes 4888704 | tf_op jit(solution)/shard_map/dot_general | solution.py:232
  379.2 6.2 all_gather.56
  385.4 32.7 %all_gather.50 = bf16[128,768]{1,0:T(8,128)(2,1)} all-gather(bf16[16,768]{1,0:T(8,128)(2,1)S(1)} %convolution_convert_fusion.8), channel_id=1, replica_groups=mesh['dp'=8,'tensor'=4] {'dp'}, dimensions={0}, use_global_device_ids=true | all-gather | bytes 221184 | tf_op jit(solution)/shard_map/all_gather | solution.py:200
  423.8 124.4 %all-reduce.11.cloned.1.call-done = f32[128,768]{1,0:T(8,128)} async-done(((f32[128,768]{1,0:T(8,128)}), f32[128,768]{1,0:T(8,128)}) %all-reduce.11.cloned.1.call-update) | async-done | bytes 393232 | tf_op jit(solution)/shard_map/psum | solution.py:273
  554.1 40.2 %all-gather.7 = f32[32,4,128]{2,1,0:T(4,128)S(1)} all-gather(f32[1,4,128]{2,1,0:T(4,128)S(1)} %maximum_bitcast_fusion), channel_id=5, replica_groups=mesh['dp'=8,'tensor'=4] {'dp','tensor'}, dimensions={0}, use_global_device_ids=true | all-gather | bytes 67584 | tf_op jit(solution)/shard_map/all_gather | solution.py:291
  603.6 121.9 %all-reduce.13.cloned.1.call-done = f32[128,768]{1,0:T(8,128)} async-done(((f32[128,768]{1,0:T(8,128)}), f32[128,768]{1,0:T(8,128)}) %all-reduce.13.cloned.1.call-update) | async-done | bytes 393232 | tf_op jit(solution)/shard_map/psum | solution.py:316
  731.6 39.3 %psum.67 = f32[128,4]{0,1:T(4,128)S(1)} all-reduce(f32[128,4]{0,1:T(4,128)S(1)} %broadcast_select_fusion), channel_id=1, replica_groups=mesh['dp'=8,'tensor'=4] {'dp','tensor'}, use_global_device_ids=true, to_apply=%region_26.27 | all-reduce | flops 512 | bytes 4096 | tf_op jit(solution)/shard_map/psum | solution.py:331
  771.0 87.1 %all-reduce.15.cloned.1.call-done = f32[128,768]{1,0:T(8,128)} async-done(((f32[128,768]{1,0:T(8,128)}), f32[128,768]{1,0:T(8,128)}) %all-reduce.15.cloned.1.call-update) | async-done | bytes 393232 | tf_op jit(solution)/shard_map/psum | solution.py:331
  879.5 19.7 %all-gather.8 = f32[8,1,128]{2,1,0:T(1,128)S(1)} all-gather(f32[1,1,128]{2,1,0:T(1,128)} %get-tuple-element.377), channel_id=6, replica_groups=mesh['dp'=8,'tensor'=4] {'dp'}, dimensions={0}, use_global_device_ids=true | all-gather | bytes 4608 | tf_op jit(solution)/shard_map/all_gather | solution.py:200
  914.2 21.0 %stack.461 = f32[32]{0:T(128)} concatenate(f32[1]{0:T(128)} %bitcast.210, f32[1]{0:T(128)} %bitcast.211, f32[1]{0:T(128)} %bitcast.212, f32[1]{0:T(128)} %bitcast.213, f32[1]{0:T(128)} %bitcast.214, f32[1]{0:T(128)} %bitcast.215, f32[1]{0:T(128)} %bitcast.216, f32[1]{0:T(128)} %bitcast.217, f32[1]{0:T(128)} %bitcast.218, f32[1]{0:T(128)} %bitcast.219, f32[1]{0:T(128)} %bitcast.220, ...), dimensions={0} | concatenate | bytes 256 | tf_op jit(solution)/shard_map/stack | solution.py:378
  935.2 21.2 %stack.427 = f32[32]{0:T(128)} concatenate(f32[1]{0:T(128)} %bitcast.177, f32[1]{0:T(128)} %bitcast.178, f32[1]{0:T(128)} %bitcast.179, f32[1]{0:T(128)} %bitcast.180, f32[1]{0:T(128)} %bitcast.181, f32[1]{0:T(128)} %bitcast.182, f32[1]{0:T(128)} %bitcast.183, f32[1]{0:T(128)} %bitcast.184, f32[1]{0:T(128)} %bitcast.185, f32[1]{0:T(128)} %bitcast.186, f32[1]{0:T(128)} %bitcast.187, ...), dimensions={0} | concatenate | bytes 256 | tf_op jit(solution)/shard_map/stack | solution.py:378
  956.3 21.3 %stack.393 = f32[32]{0:T(128)} concatenate(f32[1]{0:T(128)} %bitcast.144, f32[1]{0:T(128)} %bitcast.145, f32[1]{0:T(128)} %bitcast.146, f32[1]{0:T(128)} %bitcast.147, f32[1]{0:T(128)} %bitcast.148, f32[1]{0:T(128)} %bitcast.149, f32[1]{0:T(128)} %bitcast.150, f32[1]{0:T(128)} %bitcast.151, f32[1]{0:T(128)} %bitcast.152, f32[1]{0:T(128)} %bitcast.153, f32[1]{0:T(128)} %bitcast.154, ...), dimensions={0} | concatenate | bytes 256 | tf_op jit(solution)/shard_map/stack | solution.py:378
  982.0 5.8 psum.70
  1004.3 9.1 fusion
  1013.5 6.6 multiply_reduce_fusion
  1024.1 37.0 %psum.71 = f32[]{:T(128)} all-reduce(f32[]{:T(128)S(6)} %add.479), channel_id=1, replica_groups=mesh['dp'=8,'tensor'=4] {'dp','tensor'}, use_global_device_ids=true, to_apply=%region_144.145 | all-reduce | flops 1 | bytes 8 | tf_op jit(solution)/shard_map/psum | solution.py:441
  1068.2 7.5 multiply_subtract_fusion
  (599 shorter events, 142.3 us)
Async XLA Ops:
  7.2 212.6 %all-reduce.9.cloned.1.call-start = ((), (), s32[]{:S(2)}) async-start(), calls=%async_computation.2 | async-start | bytes 786432 | tf_op jit(solution)/shard_map/psum | solution.py:185
  56.6 494.3 %all-to-all-start.1 = ((bf16[8,1000,96]{1,2,0:T(8,128)(2,1)}), bf16[8,1000,96]{1,2,0:T(8,128)(2,1)}, u32[]{:S(2)}, u32[]{:S(2)}) async-start(bf16[8,1000,96]{1,2,0:T(8,128)(2,1)} %copy.126), calls=%async_computation.1 | async-start | bytes 3145728 | tf_op jit(solution)/shard_map/all_to_all | solution.py:178
  61.0 64.8 %copy-start.164 = (s32[2047]{0:T(1024)S(1)}, s32[2047]{0:T(1024)}, u32[]{:S(2)}) copy-start(s32[2047]{0:T(1024)} %param.35) | copy-start | bytes 24568
  61.0 357.1 %all-gather.12.cloned.1.call-start = ((), (), s32[]{:S(2)}) async-start(), calls=%async_computation.3 | async-start | bytes 1474560 | tf_op jit(solution)/shard_map/all_gather | solution.py:169
  118.8 429.4 %all-reduce.11.cloned.1.call-start = ((), (), s32[]{:S(2)}) async-start(), calls=%async_computation.4 | async-start | bytes 786432 | tf_op jit(solution)/shard_map/psum | solution.py:273
  138.8 215.7 %copy-start.40 = (pred[128,1024]{1,0:T(32,128)(4,1)}, pred[128,1024]{1,0:T(32,128)(4,1)S(1)}, u32[]{:S(2)}) copy-start(pred[128,1024]{1,0:T(32,128)(4,1)S(1)} %get-tuple-element.249) | copy-start | bytes 393220
  138.8 215.7 %copy-start.42 = (pred[128,1024]{1,0:T(32,128)(4,1)}, pred[128,1024]{1,0:T(32,128)(4,1)S(1)}, u32[]{:S(2)}) copy-start(pred[128,1024]{1,0:T(32,128)(4,1)S(1)} %get-tuple-element.250) | copy-start | bytes 393220
  138.8 215.7 %copy-start.44 = (pred[128,1024]{1,0:T(32,128)(4,1)}, pred[128,1024]{1,0:T(32,128)(4,1)S(1)}, u32[]{:S(2)}) copy-start(pred[128,1024]{1,0:T(32,128)(4,1)S(1)} %get-tuple-element.251) | copy-start | bytes 393220
  199.5 154.9 %copy-start.158 = (s32[128]{0:T(128)}, s32[128]{0:T(128)S(1)}, u32[]{:S(2)}) copy-start(s32[128]{0:T(128)S(1)} %get-tuple-element.225) | copy-start | bytes 1540
  200.1 132.2 %copy-start.195 = (s32[1024]{0:T(1024)}, s32[1024]{0:T(1024)S(1)}, u32[]{:S(2)}) copy-start(s32[1024]{0:T(1024)S(1)} %convert_add_fusion) | copy-start | bytes 12292
  219.8 61.6 %copy-start.106 = (pred[128,1024]{1,0:T(32,128)(4,1)S(1)}, pred[128,1024]{1,0:T(32,128)(4,1)}, u32[]{:S(2)}) copy-start(pred[128,1024]{1,0:T(32,128)(4,1)} %get-tuple-element.242) | copy-start | bytes 393220
  219.8 61.6 %copy-start.108 = (pred[128,1024]{1,0:T(32,128)(4,1)S(1)}, pred[128,1024]{1,0:T(32,128)(4,1)}, u32[]{:S(2)}) copy-start(pred[128,1024]{1,0:T(32,128)(4,1)} %get-tuple-element.243) | copy-start | bytes 393220
  219.8 61.6 %copy-start.110 = (pred[128,1024]{1,0:T(32,128)(4,1)S(1)}, pred[128,1024]{1,0:T(32,128)(4,1)}, u32[]{:S(2)}) copy-start(pred[128,1024]{1,0:T(32,128)(4,1)} %get-tuple-element.244) | copy-start | bytes 393220
  221.5 60.0 %copy-start.54 = (pred[128,1024]{1,0:T(32,128)(4,1)S(1)}, pred[128,1024]{1,0:T(32,128)(4,1)}, u32[]{:S(2)}) copy-start(pred[128,1024]{1,0:T(32,128)(4,1)} %get-tuple-element.256) | copy-start | bytes 393220
  221.5 60.0 %copy-start.56 = (pred[128,1024]{1,0:T(32,128)(4,1)S(1)}, pred[128,1024]{1,0:T(32,128)(4,1)}, u32[]{:S(2)}) copy-start(pred[128,1024]{1,0:T(32,128)(4,1)} %get-tuple-element.257) | copy-start | bytes 393220
  221.5 60.0 %copy-start.58 = (pred[128,1024]{1,0:T(32,128)(4,1)S(1)}, pred[128,1024]{1,0:T(32,128)(4,1)}, u32[]{:S(2)}) copy-start(pred[128,1024]{1,0:T(32,128)(4,1)} %get-tuple-element.258) | copy-start | bytes 393220
  221.6 60.0 %copy-start.60 = (pred[128,1024]{1,0:T(32,128)(4,1)S(1)}, pred[128,1024]{1,0:T(32,128)(4,1)}, u32[]{:S(2)}) copy-start(pred[128,1024]{1,0:T(32,128)(4,1)} %get-tuple-element.259) | copy-start | bytes 393220
  250.7 103.8 %copy-start.76 = (bf16[1,1024,192]{1,2,0:T(8,128)(2,1)}, bf16[1,1024,192]{1,2,0:T(8,128)(2,1)S(1)}, u32[]{:S(2)}) copy-start(bf16[1,1024,192]{1,2,0:T(8,128)(2,1)S(1)} %all-gather.1) | copy-start | bytes 1179652
  281.5 73.0 %copy-start.129 = (bf16[128,192]{1,0:T(8,128)(2,1)}, bf16[128,192]{1,0:T(8,128)(2,1)S(1)}, u32[]{:S(2)}) copy-start(bf16[128,192]{1,0:T(8,128)(2,1)S(1)} %all_gather.53) | copy-start | bytes 147460
  305.5 71.8 %copy-start.7 = (f32[128,1024]{1,0:T(8,128)}, f32[128,1024]{1,0:T(8,128)S(1)}, u32[]{:S(2)}) copy-start(f32[128,1024]{1,0:T(8,128)S(1)} %fusion.126) | copy-start | bytes 1572868
  423.1 302.4 %all-reduce.13.cloned.1.call-start = ((), (), s32[]{:S(2)}) async-start(), calls=%async_computation.6 | async-start | bytes 786432 | tf_op jit(solution)/shard_map/psum | solution.py:316
  598.7 126.8 %copy-start.180 = (f32[128]{0:T(128)S(1)}, f32[128]{0:T(128)}, u32[]{:S(2)}) copy-start(f32[128]{0:T(128)} %copy-done.179) | copy-start | bytes 1540
  601.7 125.7 %copy-start.203 = (f32[128]{0:T(128)S(1)}, f32[128]{0:T(128)}, u32[]{:S(2)}) copy-start(f32[128]{0:T(128)} %copy-done.202) | copy-start | bytes 1540
  601.8 256.3 %all-reduce.15.cloned.1.call-start = ((), (), s32[]{:S(2)}) async-start(), calls=%async_computation.7 | async-start | bytes 786432 | tf_op jit(solution)/shard_map/psum | solution.py:331
  603.6 125.4 %copy-start.166 = (f32[128]{0:T(128)S(1)}, f32[128]{0:T(128)}, u32[]{:S(2)}) copy-start(f32[128]{0:T(128)} %copy-done.165) | copy-start | bytes 1540
  730.4 127.7 %copy-start.192 = (f32[128]{0:T(128)S(1)}, f32[128]{0:T(128)}, u32[]{:S(2)}) copy-start(f32[128]{0:T(128)} %copy-done.191) | copy-start | bytes 1540
  731.5 260.6 %all-reduce.17.cloned.1.call-start = ((), (), s32[]{:S(2)}) async-start(), calls=%async_computation.8 | async-start | bytes 1572864 | tf_op jit(solution)/shard_map/psum | solution.py:188
  771.0 90.8 %copy-start.182 = (f32[128]{0:T(128)}, f32[128]{0:T(128)S(1)}, u32[]{:S(2)}) copy-start(f32[128]{0:T(128)S(1)} %get-tuple-element.278) | copy-start | bytes 1540
  771.0 90.8 %copy-start.183 = (f32[128]{0:T(128)}, f32[128]{0:T(128)S(1)}, u32[]{:S(2)}) copy-start(f32[128]{0:T(128)S(1)} %get-tuple-element.279) | copy-start | bytes 1540
  877.7 135.8 %all-gather.14.cloned.1.call-start = ((), (), s32[]{:S(2)}) async-start(), calls=%async_computation.5 | async-start | bytes 2304000 | tf_op jit(solution)/shard_map/all_gather | solution.py:315
  911.0 68.7 %copy-start.35 = (bf16[1,1024,192]{1,2,0:T(8,128)(2,1)S(1)}, bf16[1,1024,192]{1,2,0:T(8,128)(2,1)}, u32[]{:S(2)}) copy-start(bf16[1,1024,192]{1,2,0:T(8,128)(2,1)} %copy-done.33) | copy-start | bytes 1179652
  911.0 68.7 %copy-start.160 = (s32[128]{0:T(128)S(1)}, s32[128]{0:T(128)}, u32[]{:S(2)}) copy-start(s32[128]{0:T(128)} %copy-done.158) | copy-start | bytes 1540
  (184 other events, 2744.2 us)
Sparse Core Ops, SparseCore 0:
  47.1 30.5 all-reduce.8
  118.9 16.7 all-gather.11
  423.3 124.9 all-reduce.10
  601.9 123.5 all-reduce.12
  731.6 126.4 all-reduce.14
  877.8 33.7 all-reduce.16
  913.8 49.1 all-gather.13

commit v2 on v1

--- a/solution.py
+++ b/solution.py
@@ -1,7 +1,10 @@
+import functools
 import math
 
 import jax
 import jax.numpy as jnp
+from jax.experimental import pallas as pl
+from jax.experimental.pallas import tpu as pltpu
 from jax import lax
 from jax.sharding import PartitionSpec as P
 
@@ -91,6 +94,684 @@
     fixed_second = second / (1 - BETA2**STEP)
     weight = weight - rate * (fixed_first / (jnp.sqrt(fixed_second) + ADAM_EPS) + decay * weight)
     return (weight, first, second)
+
+
+MESH = pl.DeviceIdType.MESH
+VMEM_BYTES = 48 * 1024 * 1024
+WHOLE = pl.BlockSpec(memory_space=pltpu.VMEM)
+DMA = pltpu.SemaphoreType.DMA
+F32 = jnp.float32
+BF16 = jnp.bfloat16
+
+
+def greet(axes):
+    barrier = pltpu.get_barrier_semaphore()
+    total = 0
+    for axis in axes:
+        count, here = lax.axis_size(axis), lax.axis_index(axis)
+        for step in range(1, count):
+            pl.semaphore_signal(
+                barrier, inc=1, device_id={axis: lax.rem(here + step, count)}, device_id_type=MESH
+            )
+        total += count - 1
+    return barrier, total
+
+
+def met(greeting):
+    pl.semaphore_wait(*greeting)
+
+
+class Exchange:
+    def __init__(self, axis, source, dest, sems):
+        self.axis, self.count, self.here = axis, lax.axis_size(axis), lax.axis_index(axis)
+        self.source, self.dest, self.sems = source, dest, sems
+
+    def copy(self, step):
+        target = lax.rem(self.here + step, self.count)
+        return pltpu.make_async_remote_copy(
+            src_ref=self.source(target),
+            dst_ref=self.dest.at[self.here],
+            send_sem=self.sems.at[0, step],
+            recv_sem=self.sems.at[1, step],
+            device_id={self.axis: target},
+            device_id_type=MESH,
+        )
+
+    def start(self):
+        for step in range(1, self.count):
+            self.copy(step).start()
+        return self
+
+    def arrive(self):
+        for step in range(1, self.count):
+            self.copy(step).wait_recv()
+
+    def finish(self):
+        for step in range(1, self.count):
+            self.copy(step).wait_send()
+
+
+def scatter_rows(axis, source, dest, sems):
+    count = dest.shape[0]
+    height = dest.shape[1]
+    return Exchange(
+        axis,
+        lambda target: source.at[pl.ds(pl.multiple_of(target * height, height), height)],
+        dest,
+        sems,
+    ).start()
+
+
+def share_block(axis, dest, sems):
+    here = lax.axis_index(axis)
+    return Exchange(axis, lambda target: dest.at[here], dest, sems).start()
+
+
+def sems_of(axis_size):
+    return DMA((2, axis_size))
+
+
+def gather_kernel(axis, count, *refs):
+    parts, outs, own, sems = refs[:count], refs[count : 2 * count], refs[-2], refs[-1]
+    greeting = greet((axis,))
+    here = lax.axis_index(axis)
+    mine = [
+        pltpu.make_async_copy(part, out.at[here], own.at[k])
+        for k, (part, out) in enumerate(zip(parts, outs))
+    ]
+    for copy in mine:
+        copy.start()
+    met(greeting)
+    moves = [
+        Exchange(axis, lambda target, part=part: part, out, sems.at[k]).start()
+        for k, (part, out) in enumerate(zip(parts, outs))
+    ]
+    for move in moves:
+        move.arrive()
+    for copy in mine:
+        copy.wait()
+    for move in moves:
+        move.finish()
+
+
+def gather_blocks(parts, axis, number, name):
+    size = lax.axis_size(axis)
+    count = len(parts)
+    return pl.pallas_call(
+        functools.partial(gather_kernel, axis, count),
+        out_shape=[jax.ShapeDtypeStruct((size,) + p.shape, p.dtype) for p in parts],
+        in_specs=[WHOLE] * count,
+        out_specs=[WHOLE] * count,
+        scratch_shapes=[DMA((count,)), DMA((count, 2, size))],
+        compiler_params=pltpu.CompilerParams(
+            collective_id=number, has_side_effects=True, vmem_limit_bytes=VMEM_BYTES
+        ),
+        name=name,
+    )(*parts)
+
+
+def lookup_kernel(looked, rows_out, columns_out, first, second, sems_a, sems_b, sems_c, sems_d):
+    greeting = greet(("tensor", "dp"))
+    here, block = lax.axis_index("tensor"), lax.axis_index("dp")
+    met(greeting)
+    split = Exchange("tensor", lambda target: looked.at[target], first, sems_a).start()
+    first[here] = looked[here]
+    split.arrive()
+    total = first[0].astype(F32)
+    for k in range(1, first.shape[0]):
+        total = total + first[k].astype(F32)
+    columns_out[here] = total.astype(BF16)
+    to_rows = Exchange("dp", lambda target: columns_out.at[here, target], second, sems_b).start()
+    to_columns = share_block("tensor", columns_out, sems_c)
+    second[block] = columns_out[here, block]
+    to_rows.arrive()
+    rows_out[here] = second[...]
+    to_all = share_block("tensor", rows_out, sems_d)
+    to_all.arrive()
+    to_columns.arrive()
+    for move in (split, to_rows, to_columns, to_all):
+        move.finish()
+
+
+def exchange_lookups(looked):
+    tensor, blocks, part, columns = looked.shape
+    shape = jax.ShapeDtypeStruct(looked.shape, BF16)
+    return pl.pallas_call(
+        lookup_kernel,
+        out_shape=[shape, shape],
+        in_specs=[WHOLE],
+        out_specs=[WHOLE] * 2,
+        scratch_shapes=[
+            pltpu.VMEM((tensor, blocks, part, columns), BF16),
+            pltpu.VMEM((blocks, part, columns), BF16),
+            sems_of(tensor),
+            sems_of(blocks),
+            sems_of(tensor),
+            sems_of(tensor),
+        ],
+        compiler_params=pltpu.CompilerParams(
+            collective_id=2, has_side_effects=True, vmem_limit_bytes=VMEM_BYTES
+        ),
+        name="exchange_lookups",
+    )(looked)
+
+
+def dot_nt(a, b):
+    return lax.dot_general(a, b, (((1,), (1,)), ((), ())), preferred_element_type=F32)
+
+
+def dot_nn(a, b):
+    return jnp.dot(a, b, preferred_element_type=F32)
+
+
+def root_of(v):
+    return lax.rsqrt(jnp.mean(v * v, -1, keepdims=True) + NORM_EPS)
+
+
+def gelu_parts(x):
+    slope = math.sqrt(2.0 / math.pi)
+    t = jnp.tanh(slope * (x + 0.044715 * (x * x * x)))
+    value = 0.5 * x * (1.0 + t)
+    grad = 0.5 * (1.0 + t) + 0.5 * x * (1.0 - t * t) * (slope * (1.0 + 3 * 0.044715 * x * x))
+    return value, grad
+
+
+def lanes(shape):
+    return lax.broadcasted_iota(jnp.int32, shape, len(shape) - 1)
+
+
+def own_rows(count):
+    here = lax.axis_index("dp")
+    return pl.ds(pl.multiple_of(here * count, count), count)
+
+
+def tensor_sum(total, buffer, sems):
+    here = lax.axis_index("tensor")
+    buffer[here] = total
+    move = share_block("tensor", buffer, sems)
+    move.arrive()
+    total = buffer[0]
+    for k in range(1, buffer.shape[0]):
+        total = total + buffer[k]
+    return total, move
+
+
+def experts_kernel(
+    experts,
+    attended,
+    stream,
+    output_map,
+    router,
+    gains,
+    routes,
+    expert_in,
+    expert_out,
+    normed_out,
+    normed_mid_out,
+    stream_mid_own,
+    stream_out_own,
+    gates_out,
+    inner_out,
+    active_out,
+    piece_out,
+    heads,
+    stream_mid,
+    arrived,
+    summed,
+    sems_a,
+    sems_b,
+    sems_c,
+    sems_d,
+):
+    greeting = greet(("tensor", "dp"))
+    block, here = lax.axis_index("dp"), lax.axis_index("tensor")
+    blocks, picks = arrived.shape[0], arrived.shape[1]
+    width = attended.shape[1]
+    heads[here] = attended[...]
+    met(greeting)
+    to_heads = share_block("tensor", heads, sems_a)
+    to_heads.arrive()
+    middle = stream[...].astype(F32)
+    for k in range(heads.shape[0]):
+        middle = middle + dot_nn(heads[k], output_map[pl.ds(k * width, width), :])
+    stream_mid[...] = middle
+    stream_mid_own[...] = stream_mid[own_rows(picks), :]
+    normed_mid = (middle * root_of(middle) * gains[1:2, :]).astype(BF16)
+    normed_mid_out[...] = normed_mid
+    inner = dot_nn(normed_mid, expert_in[...].astype(BF16))
+    active = gelu_parts(inner)[0].astype(BF16)
+    piece_out[...] = dot_nn(active, expert_out[...].astype(BF16)).astype(BF16)
+    to_owner = scatter_rows("dp", piece_out, arrived, sems_b)
+    inner_out[...] = inner
+    active_out[...] = active
+    router_logits = dot_nt(normed_mid, router[...])
+    lane = lanes(router_logits.shape)
+    hot_a = lane == routes[:, 0:1]
+    hot_b = lane == routes[:, 1:2]
+    logit_a = jnp.sum(jnp.where(hot_a, router_logits, 0.0), 1, keepdims=True)
+    logit_b = jnp.sum(jnp.where(hot_b, router_logits, 0.0), 1, keepdims=True)
+    logit_top = jnp.maximum(logit_a, logit_b)
+    gate_a, gate_b = jnp.exp(logit_a - logit_top), jnp.exp(logit_b - logit_top)
+    both = gate_a + gate_b
+    gates_out[...] = jnp.where(hot_a, gate_a / both, 0.0) + jnp.where(hot_b, gate_b / both, 0.0)
+    arrived[block] = piece_out[own_rows(picks), :]
+    own_gates = gates_out[own_rows(picks), :]
+    to_owner.arrive()
+    spread = blocks // experts
+    mixed = jnp.zeros(stream_out_own.shape, F32)
+    for e in range(experts):
+        part = arrived[e * spread].astype(F32)
+        for k in range(1, spread):
+            part = part + arrived[e * spread + k].astype(F32)
+        mixed = mixed + own_gates[:, e : e + 1] * part
+    mixed, to_sum = tensor_sum(mixed, summed, sems_c)
+    final = stream_mid_own[...] + mixed
+    stream_out_own[...] = final
+    normed_out[block] = (final * root_of(final) * gains[2:3, :]).astype(BF16)
+    to_all = share_block("dp", normed_out, sems_d)
+    to_all.arrive()
+    for move in (to_heads, to_owner, to_sum, to_all):
+        move.finish()
+
+
+def run_experts(experts, blocks, tensor, attended, stream, output_map, router, gains, routes, expert_in, expert_out):
+    count, features = stream.shape
+    picks = count // blocks
+    hidden = expert_in.shape[1]
+    out = jax.ShapeDtypeStruct
+    return pl.pallas_call(
+        functools.partial(experts_kernel, experts),
+        out_shape=[
+            out((blocks, picks, features), BF16),
+            out((count, features), BF16),
+            out((picks, features), F32),
+            out((picks, features), F32),
+            out((count, router.shape[0]), F32),
+            out((count, hidden), F32),
+            out((count, hidden), BF16),
+            out((count, features), BF16),
+        ],
+        in_specs=[WHOLE] * 8,
+        out_specs=[WHOLE] * 8,
+        scratch_shapes=[
+            pltpu.VMEM((tensor,) + attended.shape, BF16),
+            pltpu.VMEM((count, features), F32),
+            pltpu.VMEM((blocks, picks, features), BF16),
+            pltpu.VMEM((tensor, picks, features), F32),
+            sems_of(tensor),
+            sems_of(blocks),
+            sems_of(tensor),
+            sems_of(blocks),
+        ],
+        compiler_params=pltpu.CompilerParams(
+            collective_id=3, has_side_effects=True, vmem_limit_bytes=VMEM_BYTES
+        ),
+        name="experts_forward",
+    )(attended, stream, output_map, router, gains, routes, expert_in, expert_out)
+
+
+def norm_back_rows(v, g, upstream):
+    root = root_of(v)
+    scaled = g * upstream
+    inner = jnp.sum(scaled * v, -1, keepdims=True)
+    back = root * scaled - v * (root * root * root * inner / v.shape[-1])
+    return back, jnp.sum(upstream * v * root, 0, keepdims=True)
+
+
+def merge_stats(parts):
+    peak = parts[0][0:1]
+    for part in parts[1:]:
+        peak = jnp.maximum(peak, part[0:1])
+    total = sum(part[1:2] * jnp.exp(part[0:1] - peak) for part in parts)
+    target = sum(part[2:3] for part in parts)
+    plain = sum(part[3:4] for part in parts)
+    return jnp.concatenate([peak, total, target, plain, parts[0][4:8]], 0)
+
+
+def backward_kernel(
+    experts,
+    normed_out,
+    table,
+    wanted,
+    weight,
+    gates,
+    routes,
+    router,
+    gains,
+    stream_out_own,
+    stream_mid_own,
+    normed_mid,
+    inner,
+    active,
+    piece,
+    expert_in,
+    expert_out,
+    d_logits_all,
+    d_middle,
+    gain_parts,
+    grad_in,
+    grad_out,
+    losses,
+    stats_a,
+    stats_b,
+    sent,
+    arrived,
+    summed,
+    d_final,
+    sent_wide,
+    arrived_wide,
+    summed_wide,
+    sems_a,
+    sems_b,
+    sems_c,
+    sems_d,
+    sems_e,
+    sems_f,
+    sems_g,
+    sems_h,
+    sems_i,
+    sems_j,
+):
+    greeting = greet(("tensor", "dp"))
+    block, here = lax.axis_index("dp"), lax.axis_index("tensor")
+    blocks, picks, features = arrived.shape
+    count = blocks * picks
+    out = jnp.concatenate([normed_out[k] for k in range(blocks)], 0)
+    logits = dot_nn(out, table[...])
+    share = logits.shape[1]
+    hit = lanes(logits.shape) == wanted[...]
+    local_top = jnp.max(logits, -1, keepdims=True)
+    local = (
+        local_top,
+        jnp.sum(jnp.exp(logits - local_top), -1, keepdims=True),
+        jnp.sum(jnp.where(hit, logits, 0.0), -1, keepdims=True),
+        jnp.sum(logits, -1, keepdims=True),
+    )
+    lane = lanes((count, 128))
+    packed = jnp.zeros((count, 128), F32)
+    for k, column in enumerate(local):
+        packed = jnp.where(lane == k, column, packed)
+    stats_a[here] = packed.T[0:8, :]
+    met(greeting)
+    moves = [share_block("tensor", stats_a, sems_a)]
+    moves[-1].arrive()
+    stats_b[block] = merge_stats([stats_a[k] for k in range(stats_a.shape[0])])
+    moves.append(share_block("dp", stats_b, sems_b))
+    moves[-1].arrive()
+    merged_rows = merge_stats([stats_b[k] for k in range(blocks)])
+    loss_total = merged_rows[0:1] + jnp.log(merged_rows[1:2])
+    row_weight = weight[...]
+    per_row = (
+        loss_total
+        - (1 - SMOOTH) * merged_rows[2:3]
+        - SMOOTH * merged_rows[3:4] / VOCAB
+        + ZLOSS * loss_total * loss_total
+    )
+    losses[0:1, :] = row_weight * per_row
+    losses[1:2, :] = row_weight
+    sublane = lax.broadcasted_iota(jnp.int32, (128, count), 0)
+    columns = jnp.where(sublane == 0, loss_total, jnp.where(sublane == 1, row_weight, 0.0)).T
+    total_column, weight_column = columns[:, 0:1], columns[:, 1:2]
+    d_logits = (
+        weight_column
+        * (
+            (1 + 2 * ZLOSS * total_column) * jnp.exp(logits - total_column)
+            - jnp.where(hit, 1 - SMOOTH, 0.0)
+            - SMOOTH / VOCAB
+        )
+    ).astype(BF16)
+    d_logits_all[block] = d_logits
+    sent[...] = dot_nt(d_logits, table[...]).astype(BF16)
+    moves.append(scatter_rows("dp", sent, arrived, sems_c))
+    arrived[block] = sent[own_rows(picks), :]
+    moves[-1].arrive()
+    total = arrived[0].astype(F32)
+    for k in range(1, blocks):
+        total = total + arrived[k].astype(F32)
+    d_normed, to_sum = tensor_sum(total, summed, sems_d)
+    moves.append(to_sum)
+    d_stream_out, grad_final = norm_back_rows(stream_out_own[...], gains[2:3, :], d_normed)
+    d_final[block] = d_stream_out.astype(BF16)
+    moves.append(share_block("dp", d_final, sems_e))
+    moves[-1].arrive()
+    moves.append(share_block("dp", d_logits_all, sems_f))
+    upstream = jnp.concatenate([d_final[k] for k in range(blocks)], 0).astype(F32)
+    expert = block // (blocks // experts)
+    gate = jnp.sum(jnp.where(lane == expert, gates[...], 0.0), 1, keepdims=True)
+    d_piece = (gate * upstream).astype(BF16)
+    d_active = dot_nt(d_piece, expert_out[...].astype(BF16))
+    d_inner = (d_active * gelu_parts(inner[...])[1]).astype(BF16)
+    sent_wide[:, 0:features] = dot_nt(d_inner, expert_in[...].astype(BF16)).astype(BF16)
+    gate_part = jnp.sum(upstream * piece[...].astype(F32), 1, keepdims=True)
+    high = gate_part.astype(BF16).astype(F32)
+    sent_wide[:, features:] = jnp.where(
+        lane == expert, high, jnp.where(lane == expert + 64, gate_part - high, 0.0)
+    ).astype(BF16)
+    moves.append(scatter_rows("dp", sent_wide, arrived_wide, sems_g))
+    arrived_wide[block] = sent_wide[own_rows(picks), :]
+    grad_out[...] = dot_nn(active[...].T, d_piece)
+    grad_in[...] = dot_nn(normed_mid[...].T, d_inner)
+    moves[-1].arrive()
+    total = arrived_wide[0].astype(F32)
+    for k in range(1, blocks):
+        total = total + arrived_wide[k].astype(F32)
+    total, to_sum = tensor_sum(total, summed_wide, sems_h)
+    moves.append(to_sum)
+    tail = total[:, features:]
+    d_gates = tail + pltpu.roll(tail, 64, 1)
+    own_routes = routes[own_rows(picks), :]
+    own_gates = gates[own_rows(picks), :]
+    slim = lanes(tail.shape)
+    chosen = (slim == own_routes[:, 0:1]) | (slim == own_routes[:, 1:2])
+    d_gates = jnp.where(chosen, d_gates, 0.0)
+    mean = jnp.sum(own_gates * d_gates, 1, keepdims=True)
+    d_router = jnp.where(chosen, own_gates * (d_gates - mean), 0.0).astype(BF16)
+    d_normed_mid = total[:, 0:features] + dot_nn(d_router, router[...])
+    d_from_mid, grad_middle = norm_back_rows(stream_mid_own[...], gains[1:2, :], d_normed_mid)
+    d_middle[block, :, 0:features] = (d_stream_out + d_from_mid).astype(BF16)
+    d_middle[block, :, features:] = d_router
+    gain_parts[block, 0:1, :] = grad_middle
+    gain_parts[block, 1:2, :] = grad_final
+    moves.append(share_block("dp", d_middle, sems_i))
+    moves.append(share_block("dp", gain_parts, sems_j))
+    moves[-2].arrive()
+    moves[-1].arrive()
+    moves[5].arrive()
+    for move in moves:
+        move.finish()
+
+
+def run_backward(experts, blocks, tensor, *operands):
+    normed_out, table, expert_in = operands[0], operands[1], operands[14]
+    picks, features = normed_out.shape[1:]
+    count = blocks * picks
+    share = table.shape[1]
+    wide = features + 128
+    out = jax.ShapeDtypeStruct
+    return pl.pallas_call(
+        functools.partial(backward_kernel, experts),
+        out_shape=[
+            out((blocks, count, share), BF16),
+            out((blocks, picks, wide), BF16),
+            out((blocks, 2, features), F32),
+            out(expert_in.shape, F32),
+            out(expert_in.shape[::-1], F32),
+            out((2, count), F32),
+        ],
+        in_specs=[WHOLE] * len(operands),
+        out_specs=[WHOLE] * 6,
+        scratch_shapes=[
+            pltpu.VMEM((tensor, 8, 128), F32),
+            pltpu.VMEM((blocks, 8, 128), F32),
+            pltpu.VMEM((count, features), BF16),
+            pltpu.VMEM((blocks, picks, features), BF16),
+            pltpu.VMEM((tensor, picks, features), F32),
+            pltpu.VMEM((blocks, picks, features), BF16),
+            pltpu.VMEM((count, wide), BF16),
+            pltpu.VMEM((blocks, picks, wide), BF16),
+            pltpu.VMEM((tensor, picks, wide), F32),
+            sems_of(tensor),
+            sems_of(blocks),
+            sems_of(blocks),
+            sems_of(tensor),
+            sems_of(blocks),
+            sems_of(blocks),
+            sems_of(blocks),
+            sems_of(tensor),
+            sems_of(blocks),
+            sems_of(blocks),
+        ],
+        compiler_params=pltpu.CompilerParams(
+            collective_id=4, has_side_effects=True, vmem_limit_bytes=VMEM_BYTES
+        ),
+        name="loss_and_experts_backward",
+    )(*operands)
+
+
+def head_of(ref, h):
+    return ref[:, h * HD : (h + 1) * HD]
+
+
+def attention_kernel(
+    query,
+    keys,
+    values,
+    flipped,
+    offsets,
+    positions,
+    query_picture,
+    key_picture,
+    table,
+    attended_low,
+    probs,
+    bucket,
+    shifted,
+    bias,
+):
+    count, every = bucket.shape
+    heads, bucket_count = table.shape
+    rows = 128
+    blocks = every // rows
+    picks = count // blocks
+    period = flipped.shape[1]
+    spread = jnp.broadcast_to(flipped[...], (rows, period))
+    turned = pltpu.roll(spread, period - rows + 1, 1, stride=1, stride_axis=0).astype(BF16)
+    chosen = (lanes((count, rows)) == offsets[...]).astype(F32).astype(BF16)
+    shifted[...] = dot_nn(chosen, turned).astype(jnp.int32)
+    for k in range(blocks):
+        first = rows * (blocks - 1 - k)
+        bucket[k * picks : (k + 1) * picks, :] = shifted[
+            k * picks : (k + 1) * picks, first : first + every
+        ]
+
+    def fill(k, carry):
+        here = pl.ds(pl.multiple_of(k * picks, picks), picks)
+        block = bucket[here, :]
+        terms = [jnp.zeros(block.shape, F32)] * heads
+        for b in range(bucket_count):
+            same = block == b
+            terms = [jnp.where(same, table[h, b], terms[h]) for h in range(heads)]
+        for h in range(heads):
+            bias[h, here, :] = terms[h]
+        return carry
+
+    lax.fori_loop(0, blocks, fill, 0)
+    key_position = lanes((count, every))
+    picture = query_picture[...]
+    allowed = (key_position <= positions[...]) | (
+        (key_picture[...] == picture) & (picture >= 0)
+    )
+    for h in range(heads):
+        raw = dot_nt(head_of(query, h), head_of(keys, h)) * (1.0 / math.sqrt(HD)) + bias[h]
+        raw = jnp.where(allowed, raw, NEGATIVE)
+        terms = jnp.exp(raw - jnp.max(raw, -1, keepdims=True))
+        soft = terms / jnp.sum(terms, -1, keepdims=True)
+        probs[h] = soft
+        attended_low[:, h * HD : (h + 1) * HD] = dot_nn(
+            soft.astype(BF16), head_of(values, h)
+        ).astype(BF16)
+
+
+def run_attention(query, keys, values, flipped, offsets, positions, query_picture, key_picture, table):
+    count, width = query.shape
+    every = keys.shape[0]
+    heads = table.shape[0]
+    out = jax.ShapeDtypeStruct
+    smem = pl.BlockSpec(memory_space=pltpu.SMEM)
+    return pl.pallas_call(
+        attention_kernel,
+        out_shape=[
+            out((count, width), BF16),
+            out((heads, count, every), F32),
+            out((count, every), jnp.int32),
+        ],
+        in_specs=[WHOLE] * 8 + [smem],
+        out_specs=[WHOLE] * 3,
+        scratch_shapes=[
+            pltpu.VMEM((count, flipped.shape[1]), jnp.int32),
+            pltpu.VMEM((heads, count, every), F32),
+        ],
+        compiler_params=pltpu.CompilerParams(vmem_limit_bytes=VMEM_BYTES),
+        name="attention",
+    )(query, keys, values, flipped, offsets, positions, query_picture, key_picture, table)
+
+
+def attention_back_kernel(
+    upstream, output_map, query, keys, values, probs, bucket, d_query, d_key, d_value, bias_rows, spare
+):
+    heads, count, every = probs.shape
+    picks = 16
+    scale = 1.0 / math.sqrt(HD)
+    d_attended = dot_nt(upstream[...], output_map[...]).astype(BF16)
+    for h in range(heads):
+        span = slice(h * HD, (h + 1) * HD)
+        soft = probs[h]
+        d_head = d_attended[:, span]
+        d_probs = dot_nt(d_head, head_of(values, h))
+        d_scores = soft * (d_probs - jnp.sum(soft * d_probs, -1, keepdims=True))
+        d_scores = d_scores.astype(BF16)
+        spare[h] = d_scores.astype(F32)
+        d_query[:, span] = (dot_nn(d_scores, head_of(keys, h)) * scale).astype(BF16)
+        d_key[:, span] = (dot_nn(d_scores.T, head_of(query, h)) * scale).astype(BF16)
+        d_value[:, span] = dot_nn(soft.astype(BF16).T, d_head).astype(BF16)
+    bias_rows[...] = jnp.zeros(bias_rows.shape, F32)
+    bucket_count = bias_rows.shape[1]
+
+    def collect(k, carry):
+        here = pl.ds(pl.multiple_of(k * picks, picks), picks)
+        block = bucket[here, :]
+        parts = [spare[h, here, :] for h in range(heads)]
+        for b in range(bucket_count):
+            same = block == b
+            for h in range(heads):
+                kept = jnp.where(same, parts[h], 0.0)
+                kept = kept[0:8] + kept[8:16]
+                slim = kept[:, 0:128]
+                for c in range(1, every // 128):
+                    slim = slim + kept[:, c * 128 : (c + 1) * 128]
+                bias_rows[h, b] += slim
+        return carry
+
+    lax.fori_loop(0, count // picks, collect, 0)
+
+
+def run_attention_back(upstream, output_map, query, keys, values, probs, bucket, bucket_count):
+    heads, count, every = probs.shape
+    out = jax.ShapeDtypeStruct
+    return pl.pallas_call(
+        attention_back_kernel,
+        out_shape=[
+            out(query.shape, BF16),
+            out(keys.shape, BF16),
+            out(keys.shape, BF16),
+            out((heads, bucket_count, 8, 128), F32),
+        ],
+        in_specs=[WHOLE] * 7,
+        out_specs=[WHOLE] * 4,
+        scratch_shapes=[pltpu.VMEM((heads, count, every), F32)],
+        compiler_params=pltpu.CompilerParams(vmem_limit_bytes=VMEM_BYTES),
+        name="attention_backward",
+    )(upstream, output_map, query, keys, values, probs, bucket)
 
 
 def wide_norm_back(v, g, upstream):
@@ -158,7 +839,8 @@
     packed = jnp.concatenate(
         [token_ids, loss_offsets, at_loss(targets), at_loss(routes[:, 0]), at_loss(routes[:, 1])]
     )
-    known = lax.all_gather(packed, "dp")
+    packed = jnp.pad(packed, (0, 256 - packed.shape[0])).reshape(2, 128)
+    known = gather_blocks((packed,), "dp", 1, "gather_integers")[0].reshape(dp_count, 256)
     ids = known[:, :rows].reshape(every)
     offsets, wanted, route_a, route_b = (
         known[:, rows + k * picks : rows + (k + 1) * picks].reshape(all_picks) for k in range(4)
@@ -178,14 +860,18 @@
     table_rows = lax.all_to_all(
         embedding.astype(bf16), "dp", split_axis=0, concat_axis=1, tiled=True
     )
+    part = rows // tensor_count
+    sorted_ids = jnp.swapaxes(ids.reshape(dp_count, tensor_count, part), 0, 1).reshape(every)
+    place = sorted_ids - tensor_place * vocab_rows
+    owned = (place >= 0) & (place < vocab_rows)
+    looked = jnp.take(embedding.astype(bf16), jnp.clip(place, 0, vocab_rows - 1), axis=0)
+    looked = jnp.where(owned[:, None], looked, 0.0).astype(bf16)
+    stream_parts, column_parts = exchange_lookups(
+        looked.reshape(tensor_count, dp_count, part, columns)
+    )
+    stream_in = jnp.swapaxes(stream_parts, 1, 2).reshape(rows, features).astype(f32)
+    in_columns = jnp.swapaxes(column_parts, 0, 1).reshape(every, columns).astype(f32)
     place = ids - tensor_place * vocab_rows
-    owned = (place >= 0) & (place < vocab_rows)
-    looked = jnp.take(embedding, jnp.clip(place, 0, vocab_rows - 1), axis=0)
-    looked = jnp.where(owned[:, None], looked, 0.0).astype(bf16)
-    stream_in = lax.psum(
-        lax.all_to_all(looked, "dp", split_axis=0, concat_axis=1, tiled=True).astype(f32), "tensor"
-    )
-    in_columns = lax.psum(looked.astype(f32), "tensor")
     root_in = lax.rsqrt(jnp.mean(stream_in * stream_in, -1, keepdims=True) + NORM_EPS)
     normed_in = (stream_in * root_in * gain[0]).astype(bf16)
     fresh = jnp.einsum("td,sde->ste", normed_in, projection, preferred_element_type=f32).astype(
@@ -196,191 +882,99 @@
     own_stream = jnp.dot(
         loss_one, stream_in.astype(bf16), preferred_element_type=f32
     ).astype(bf16)
-    keys, values, query, stream_picked, root_all = (
-        lax.all_gather(part, "dp", axis=0, tiled=True)
-        for part in (fresh[1], fresh[2], own_query, own_stream, root_in)
-    )
-    stream_picked = stream_picked.astype(f32)
+    shared = jnp.concatenate([fresh[1], fresh[2]], 1)
+    shared, query, stream_picked, root_all = gather_blocks(
+        (shared, own_query, own_stream, root_in.reshape(1, rows)), "dp", 5, "gather_keys"
+    )
+    shared = shared.reshape(every, 2 * width)
+    keys, values = shared[:, :width], shared[:, width:]
+    query = query.reshape(all_picks, width)
+    stream_picked = stream_picked.reshape(all_picks, features)
+    root_all = root_all.reshape(every, 1)
     in_columns_normed = (in_columns * root_all * own_gain[0]).astype(bf16)
-    flipped = jnp.pad(jnp.flip(buckets), (0, 1)).astype(bf16)
-    period = 2 * every
-    shifted = jnp.tile(flipped, rows + 1)[: rows * (period + 1)].reshape(rows, period + 1)
-    shifted = shifted[:, : period - rows]
-    turn = (rows - 1 - offsets)[:, None] == jnp.arange(rows, dtype=jnp.int32)[None, :]
-    shifted = jnp.dot(turn.astype(bf16), shifted, preferred_element_type=f32)
-    bucket = jnp.concatenate(
-        [
-            shifted[
-                picks * k : picks * (k + 1),
-                rows * (dp_count - 1 - k) : rows * (dp_count - 1 - k) + every,
-            ]
-            for k in range(dp_count)
-        ]
-    ).astype(jnp.int32)
+    flipped = jnp.pad(jnp.flip(buckets), (0, 1)).astype(f32)[None, :]
     position = jnp.arange(every, dtype=jnp.int32)
     key_picture = picture_of(position, picture_start[0], PIECE)
     query_picture = picture_of(loss_rows, picture_start[0], PIECE)
-    allowed = (position[None, :] <= loss_rows[:, None]) | (
-        (key_picture[None, :] == query_picture[:, None]) & (query_picture[:, None] >= 0)
-    )
     bucket_count = position_bias.shape[1]
-
-    def head(value, h):
-        return value[:, h * HD : (h + 1) * HD]
-
-    def scores_of(h):
-        raw = lax.dot_general(
-            head(query, h), head(keys, h), (((1,), (1,)), ((), ())), preferred_element_type=f32
-        )
-        bias = jnp.zeros(bucket.shape, f32)
-        for b in range(bucket_count):
-            bias = jnp.where(bucket == b, position_bias[h, b], bias)
-        return jnp.where(allowed, raw * scale + bias, NEGATIVE)
-
-    probs = []
-    for h in range(heads):
-        raw = scores_of(h)
-        terms = jnp.exp(raw - jnp.max(raw, -1, keepdims=True))
-        probs.append(terms / jnp.sum(terms, -1, keepdims=True))
-    attended = jnp.concatenate(
-        [
-            jnp.dot(probs[h].astype(bf16), head(values, h), preferred_element_type=f32)
-            for h in range(heads)
-        ],
-        1,
-    )
-    attended_low = attended.astype(bf16)
-    attended_all = lax.all_gather(attended_low, "tensor", axis=1, tiled=True)
-    stream_mid = stream_picked + jnp.dot(attended_all, output_map, preferred_element_type=f32)
-    normed_mid = normed(stream_mid, gain[1]).astype(bf16)
-    router_logits = jnp.dot(normed_mid, router_full.T, preferred_element_type=f32)
-    expert_ids = jnp.arange(experts, dtype=jnp.int32)[None, :]
-    hot_a = route_a[:, None] == expert_ids
-    hot_b = route_b[:, None] == expert_ids
-    logit_a = jnp.sum(jnp.where(hot_a, router_logits, 0.0), 1)
-    logit_b = jnp.sum(jnp.where(hot_b, router_logits, 0.0), 1)
-    logit_top = jnp.maximum(logit_a, logit_b)
-    gate_a, gate_b = jnp.exp(logit_a - logit_top), jnp.exp(logit_b - logit_top)
-    gate_a, gate_b = gate_a / (gate_a + gate_b), gate_b / (gate_a + gate_b)
-    spread = dp_count * tensor_count // experts
-    expert = (dp_place * tensor_count + tensor_place) // spread
-    gate = jnp.where(route_a == expert, gate_a, 0.0) + jnp.where(route_b == expert, gate_b, 0.0)
-    in_low = expert_in.astype(bf16)
-    out_low = expert_out.astype(bf16)
-    inner = jnp.dot(normed_mid, in_low, preferred_element_type=f32)
-    active = jax.nn.gelu(inner).astype(bf16)
-    piece = jnp.dot(active, out_low, preferred_element_type=f32).astype(bf16).astype(f32)
-    mixed = lax.psum(gate[:, None] * piece, both)
-    stream_out = stream_mid + mixed
-    normed_out = normed(stream_out, gain[2]).astype(bf16)
-    logits = lax.dot_general(
-        normed_out, table_rows, (((1,), (1,)), ((), ())), preferred_element_type=f32
+    attended_low, probs, bucket = run_attention(
+        query,
+        keys,
+        values,
+        flipped,
+        offsets[:, None],
+        loss_rows[:, None],
+        query_picture[:, None],
+        key_picture[None, :],
+        position_bias,
+    )
+    route_pair = jnp.stack([route_a, route_b], 1)
+    router_wide = jnp.pad(router_full, ((0, 128 - experts), (0, 0)))
+    (
+        normed_out,
+        normed_mid,
+        stream_mid_own,
+        stream_out_own,
+        gates,
+        inner,
+        active,
+        piece,
+    ) = run_experts(
+        experts,
+        dp_count,
+        tensor_count,
+        attended_low,
+        stream_picked,
+        output_map,
+        router_wide,
+        gain,
+        route_pair,
+        expert_in,
+        expert_out,
     )
     share = table_rows.shape[0]
     first_id = tensor_place * vocab_rows + dp_place * share
-    hit = jnp.arange(share, dtype=jnp.int32)[None, :] == (wanted - first_id)[:, None]
-    local_top = jnp.max(logits, -1)
-    stats = jnp.stack(
-        [
-            local_top,
-            jnp.sum(jnp.exp(logits - local_top[:, None]), -1),
-            jnp.sum(jnp.where(hit, logits, 0.0), -1),
-            jnp.sum(logits, -1),
-        ]
-    )
-    stats = lax.all_gather(stats, both)
-    peak = jnp.max(stats[:, 0], 0)
-    vocab_total = jnp.sum(stats[:, 1] * jnp.exp(stats[:, 0] - peak), 0)
-    target_logit = jnp.sum(stats[:, 2], 0)
-    logit_sum = jnp.sum(stats[:, 3], 0)
-    loss_total = peak + jnp.log(vocab_total)
     weight = (query_picture < 0).astype(f32)
-    per_row = (
-        loss_total
-        - (1 - SMOOTH) * target_logit
-        - SMOOTH * logit_sum / VOCAB
-        + ZLOSS * loss_total * loss_total
-    )
-    loss_sum = jnp.sum(weight * per_row)
-    loss_count = jnp.sum(weight)
-    soft = jnp.exp(logits - loss_total[:, None])
-    d_logits = (
-        weight[:, None]
-        * (
-            (1 + 2 * ZLOSS * loss_total)[:, None] * soft
-            - (1 - SMOOTH) * hit.astype(f32)
-            - SMOOTH / VOCAB
-        )
-    ).astype(bf16)
-    d_logits_all = lax.all_gather(d_logits, "dp", axis=1, tiled=True)
-    d_normed_out = lax.psum(jnp.dot(d_logits, table_rows, preferred_element_type=f32), both)
-    d_stream_out, grad_final = wide_norm_back(stream_out, gain[2], d_normed_out)
-    d_piece = (gate[:, None] * d_stream_out).astype(bf16)
-    d_active = lax.dot_general(
-        d_piece, out_low, (((1,), (1,)), ((), ())), preferred_element_type=f32
-    )
-    unused, gelu_pull = jax.vjp(jax.nn.gelu, inner)
-    d_inner = gelu_pull(d_active)[0].astype(bf16)
-    grad_out = jnp.dot(active.T, d_piece, preferred_element_type=f32)
-    grad_in = jnp.dot(normed_mid.T, d_inner, preferred_element_type=f32)
-    sent_back = lax.dot_general(
-        d_inner, in_low, (((1,), (1,)), ((), ())), preferred_element_type=f32
-    ).astype(bf16)
-    gate_part = jnp.sum(d_stream_out * piece, -1)
-    gate_part = jnp.where(expert_ids == expert, gate_part[:, None], 0.0)
-    d_from_experts, d_gates = lax.psum((sent_back.astype(f32), gate_part), both)
-    d_gate_a = jnp.sum(jnp.where(hot_a, d_gates, 0.0), 1)
-    d_gate_b = jnp.sum(jnp.where(hot_b, d_gates, 0.0), 1)
-    d_mean = gate_a * d_gate_a + gate_b * d_gate_b
-    d_router_logits = (
-        jnp.where(hot_a, (gate_a * (d_gate_a - d_mean))[:, None], 0.0)
-        + jnp.where(hot_b, (gate_b * (d_gate_b - d_mean))[:, None], 0.0)
-    ).astype(bf16)
+    d_logits_all, d_middle, gain_parts, grad_in, grad_out, losses = run_backward(
+        experts,
+        dp_count,
+        tensor_count,
+        normed_out,
+        table_rows.T,
+        (wanted - first_id)[:, None],
+        weight[None, :],
+        gates,
+        route_pair,
+        router_wide,
+        gain,
+        stream_out_own,
+        stream_mid_own,
+        normed_mid,
+        inner,
+        active,
+        piece,
+        expert_in,
+        expert_out,
+    )
+    loss_sum, loss_count = jnp.sum(losses[0]), jnp.sum(losses[1])
+    d_middle = d_middle.reshape(all_picks, features + 128)
+    d_attn_low, d_router_logits = d_middle[:, :features], d_middle[:, features:]
 
     def own_columns(value):
         return lax.dynamic_slice_in_dim(value, dp_place * columns, columns, value.ndim - 1)
 
-    grad_router = own_columns(
-        jnp.dot(d_router_logits.T, normed_mid, preferred_element_type=f32)
-    )
-    d_normed_mid = d_from_experts + jnp.dot(
-        d_router_logits, router_full, preferred_element_type=f32
-    )
-    d_from_mid, grad_middle = wide_norm_back(stream_mid, gain[1], d_normed_mid)
-    d_stream_mid = d_stream_out + d_from_mid
-    d_attn_low = d_stream_mid.astype(bf16)
+    grad_router = jnp.dot(
+        d_router_logits.T, own_columns(normed_mid), preferred_element_type=f32
+    )[:experts]
+    grad_middle, grad_final = jnp.sum(gain_parts[:, 0], 0), jnp.sum(gain_parts[:, 1], 0)
     grad_output_map = jnp.dot(
         attended_low.T, own_columns(d_attn_low), preferred_element_type=f32
     )
     own_map = lax.dynamic_slice_in_dim(output_map, tensor_place * width, width, 0)
-    d_attended = lax.dot_general(
-        d_attn_low, own_map, (((1,), (1,)), ((), ())), preferred_element_type=f32
-    ).astype(bf16)
-    d_queries, d_keys, d_values, bias_terms = [], [], [], []
-    for h in range(heads):
-        d_head = head(d_attended, h)
-        d_probs = lax.dot_general(
-            d_head, head(values, h), (((1,), (1,)), ((), ())), preferred_element_type=f32
-        )
-        d_scores = probs[h] * (d_probs - jnp.sum(probs[h] * d_probs, -1, keepdims=True))
-        d_scores = d_scores.astype(bf16)
-        d_queries.append(
-            jnp.dot(d_scores, head(keys, h), preferred_element_type=f32) * scale
-        )
-        d_keys.append(
-            jnp.dot(d_scores.T, head(query, h), preferred_element_type=f32) * scale
-        )
-        d_values.append(
-            jnp.dot(probs[h].astype(bf16).T, d_head, preferred_element_type=f32)
-        )
-        wide = d_scores.astype(f32)
-        bias_terms.append(
-            jnp.stack([jnp.sum(jnp.where(bucket == b, wide, 0.0)) for b in range(bucket_count)])
-        )
-    sum_bias = jnp.stack(bias_terms)
-    d_query = jnp.concatenate(d_queries, 1).astype(bf16)
-    d_key = jnp.concatenate(d_keys, 1).astype(bf16)
-    d_value = jnp.concatenate(d_values, 1).astype(bf16)
+    d_query, d_key, d_value, bias_rows = run_attention_back(
+        d_attn_low, own_map, query, keys, values, probs, bucket, bucket_count
+    )
+    sum_bias = jnp.sum(bias_rows, (2, 3))
     back_hot = (loss_rows[None, :] == position[:, None]).astype(bf16)
     in_picked = jnp.dot(
         back_hot.T, in_columns_normed, preferred_element_type=f32
@@ -408,18 +1002,15 @@
     )
     d_columns, d_inner_in = lax.psum((d_columns, d_inner_in), "tensor")
     grad_first = jnp.sum(d_columns * in_columns * root_all, 0)
-    own_stream_mid = own_columns(d_stream_mid)
-    stream_high = own_stream_mid.astype(bf16)
-    stream_low = (own_stream_mid - stream_high.astype(f32)).astype(bf16)
+    own_stream_mid = own_columns(d_attn_low)
     d_stream_in = (
         root_all * own_gain[0] * d_columns
         - in_columns * (root_all * root_all * d_inner_in / features)
-        + jnp.dot(back_hot, stream_high, preferred_element_type=f32)
-        + jnp.dot(back_hot, stream_low, preferred_element_type=f32)
-    )
-    sum_table = lax.dot_general(
-        d_logits_all, own_columns(normed_out), (((0,), (0,)), ((), ())), preferred_element_type=f32
-    )
+        + jnp.dot(back_hot, own_stream_mid, preferred_element_type=f32)
+    )
+    own_out = own_columns(normed_out.reshape(all_picks, features))
+    sum_table = jnp.einsum("kqv,qd->kvd", d_logits_all, own_out, preferred_element_type=f32)
+    sum_table = sum_table.reshape(vocab_rows, columns)
     d_high = d_stream_in.astype(bf16)
     d_low = (d_stream_in - d_high.astype(f32)).astype(bf16)
     id_hot = (jnp.arange(vocab_rows, dtype=jnp.int32)[:, None] == place[None, :]).astype(bf16)
@@ -992,6 +1583,8 @@
         single = rows * dp_count <= SEQ and arrays[4].shape[0] == 1
         even = embedding.shape[0] % dp_count == 0
         whole = dp_count * tensor_count % router.shape[0] == 0 and routes.shape[1] == 2
-        return (fast_local if single and even and whole else local)(*arrays)
+        whole = whole and dp_count % router.shape[0] == 0
+        tiles = rows == 128 and arrays[2].shape[0] * dp_count == 128
+        return (fast_local if single and even and whole and tiles else local)(*arrays)
 
     return jax.shard_map(chosen, mesh=mesh, in_specs=in_specs, out_specs=out_specs, check_vma=False)

time: 1100 us -> 504 us (0.46)
  waiting for transfers between devices: 334 us -> 15.8 us
  blocking collectives: 417 us -> 153 us
  Pallas kernels: 0 us -> 195 us
  matrix products: 124 us -> 25.4 us
  local copies, waits for them, and re-layouts: 119 us -> 53.9 us
  other arithmetic: 67.7 us -> 31.3 us
    psum x5 -> x1, waiting for transfers between devices: 333 us -> 15.8 us  [fast_local(): d_columns, d_inner_in = lax.psum((d_columns, d_inner_in), 'tensor')]
    pallas_call x0 -> x7, Pallas kernels: none -> 195 us  [the longest x1 93.6 us: run_backward(): pl.pallas_call(functools.partial(backward_kernel, experts), out_shape=[ou...]
    all_gather x7 -> x0, blocking collectives: 183 us -> none  [the longest x5 137 us: fast_local(): lax.all_gather(part, 'dp', axis=0, tiled=True)]
    dot_general x35 -> x3, matrix products: 102 us -> 5.25 us  [the longest x1 2.37 us: fast_local(): jnp.einsum('kqv,qd->kvd', d_logits_all, own_out, preferred_element_type=f32)]
    another operation x5 -> x4, local copies, waits for them, and re-layouts: 66.4 us -> 0.35 us  [the longest x3 0.27 us: fast_local(): route_pair = jnp.stack([route_a, route_b], 1)]
    psum x1 -> x0, blocking collectives: 39.3 us -> none  [fast_local(): d_from_experts, d_gates = lax.psum((sent_back.astype(f32), gate_part), both)]
    all_gather x1, blocking collectives: 55.7 us -> 32.7 us  [fast_local(): lax.all_gather(out_proj.astype(bf16), 'dp', axis=1, tiled=True)]
    unnamed x1 -> x0, blocking collectives: 13.2 us -> none
  transfers between devices with their start and end apart: 8 -> 3, of which waited for: 3 -> 1; matrix products, arithmetic and copies ran while one was open for 20% -> 8% of each run, Pallas kernels for 0% -> 19%
where the time goes in v2:
time: 504 us; the launch traced here: 503 us
  Pallas kernels  195 us (39%)
  blocking collectives  153 us (30%)
  local copies, waits for them, and re-layouts  53.9 us (11%)
  other arithmetic  31.3 us (6%)
  matrix products  25.4 us (5%)
  between operations  22.8 us (5%)
  waiting for transfers between devices  15.8 us (3%)
  starting transfers between devices  5.87 us (1%)
    pallas_call x1, Pallas kernels, run_backward(): pl.pallas_call(functools.partial(backward_kernel, experts), out_shape=[ou...  93.6 us
    pallas_call x2, Pallas kernels, gather_blocks(): pl.pallas_call(functools.partial(gather_kernel, axis, count), out_shape=[...  52.8 us
    psum x1, blocking collectives, fast_local(): grad_norm = jnp.sqrt(lax.psum(squares, both))  39.5 us
    all_gather x1, blocking collectives, fast_local(): lax.all_gather(attn_proj.astype(bf16), 'dp', axis=1, tiled=True)  38 us
    all_gather x1, blocking collectives, fast_local(): lax.all_gather(out_proj.astype(bf16), 'dp', axis=1, tiled=True)  32.7 us
    unnamed x198, local copies, waits for them, and re-layouts  28.7 us
    pallas_call x1, Pallas kernels, run_experts(): pl.pallas_call(functools.partial(experts_kernel, experts), out_shape=[out...  22.8 us
    all_gather x1, blocking collectives, fast_local(): lax.all_gather(norm_gains.astype(bf16), 'dp', axis=1, tiled=True)  19.5 us
  transfers between devices with their start and end apart: 3, of which 1 were waited for; matrix products, arithmetic and copies ran while one was open for 8% of the time, Pallas kernels for 19%

profile of v2, /device:TPU:0, one launch (start us, length us, event | category | flops | bytes accessed | tf_op | source)
XLA Modules:
  0.0 502.8 jit_solution(11509629880970784059)
XLA Ops:
  8.2 32.7 %all_gather.17 = bf16[192,768]{0,1:T(8,128)(2,1)S(1)} all-gather(bf16[192,96]{0,1:T(8,128)(2,1)S(1)} %copy.186), channel_id=1, replica_groups=mesh['dp'=8,'tensor'=4] {'dp'}, dimensions={1}, use_global_device_ids=true | all-gather | bytes 331776 | tf_op jit(solution)/shard_map/all_gather | solution.py:852
  41.9 3.4 copy.177
  45.3 3.0 copy.190
  48.3 5.8 %all-to-all-start = ((bf16[8,1000,96]{1,2,0:T(8,128)(2,1)}), bf16[8,1000,96]{1,2,0:T(8,128)(2,1)}, u32[]{:S(2)}, u32[]{:S(2)}) async-start(bf16[8,1000,96]{1,2,0:T(8,128)(2,1)} %copy.190), calls=%async_computation | async-start | bytes 3145728 | tf_op jit(solution)/shard_map/all_to_all | solution.py:860
  54.5 31.4 %gather_integers.1 = s32[8,2,128]{2,1,0:T(2,128)S(1)} custom-call(s32[2,128]{1,0:T(2,128)S(1)} %pad_bitcast_fusion.refs_0_), custom_call_target="tpu_custom_call" | custom-call | tf_op jit(solution)/shard_map/gather_integers/pallas_call | solution.py:200
  87.4 38.0 %all_gather.16 = bf16[3,768,192]{2,0,1:T(4,128)(2,1)} all-gather(bf16[3,96,192]{2,0,1:T(4,128)(2,1)S(1)} %copy.180), channel_id=1, replica_groups=mesh['dp'=8,'tensor'=4] {'dp'}, dimensions={1}, use_global_device_ids=true | all-gather | bytes 995328 | tf_op jit(solution)/shard_map/all_gather | solution.py:850
  125.4 2.6 copy.181
  128.1 3.2 gather_fusion
  131.8 13.7 %exchange_lookups.1 = (bf16[4,8,32,96]{3,2,1,0:T(8,128)(2,1)S(1)}, bf16[4,8,32,96]{3,2,1,0:T(8,128)(2,1)S(1)}) custom-call(bf16[4,8,32,96]{3,2,1,0:T(8,128)(2,1)S(1)} %select_select_fusion.looked), custom_call_target="tpu_custom_call" | custom-call | tf_op jit(solution)/shard_map/exchange_lookups/pallas_call | solution.py:239
  146.0 19.5 %all-gather = bf16[8,96,3]{1,2,0:T(4,128)(2,1)S(1)} all-gather(bf16[1,96,3]{1,2,0:T(4,128)(2,1)S(1)} %convert_bitcast_fusion.2), channel_id=1, replica_groups=mesh['dp'=8,'tensor'=4] {'dp'}, dimensions={0}, use_global_device_ids=true | all-gather | bytes 5184 | tf_op jit(solution)/shard_map/all_gather | solution.py:858
  169.7 16.5 %all-gather.1 = bf16[8,96,4]{1,2,0:T(4,128)(2,1)S(1)} all-gather(bf16[1,96,4]{1,2,0:T(4,128)(2,1)S(1)} %convert_bitcast_fusion.1), channel_id=1, replica_groups=mesh['dp'=8,'tensor'=4] {'dp'}, dimensions={0}, use_global_device_ids=true | all-gather | bytes 6912 | tf_op jit(solution)/shard_map/all_gather | solution.py:857
  189.0 21.4 %gather_keys.1 = (bf16[8,128,384]{2,1,0:T(8,128)(2,1)S(1)}, bf16[8,16,192]{2,1,0:T(8,128)(2,1)S(1)}, bf16[8,16,768]{2,1,0:T(8,128)(2,1)S(1)}, f32[8,1,128]{2,1,0:T(1,128)S(1)}) custom-call(bf16[128,384]{1,0:T(8,128)(2,1)S(1)} %pad_maximum_fusion.1.refs_0_, bf16[16,192]{1,0:T(8,128)(2,1)S(1)} %convolution_convert_fusion.3.refs_1_, ...), custom_call_target="tpu_custom_call" | custom-call | tf_op jit(solution)/shard_map/gather_keys/pallas_call | solution.py:200
  211.3 6.0 %attention.1 = (bf16[128,192]{1,0:T(8,128)(2,1)S(1)}, f32[3,128,1024]{2,1,0:T(8,128)S(1)}, s32[128,1024]{1,0:T(8,128)S(1)}) custom-call(bf16[128,192]{1,0:T(8,128)(2,1)S(1)} %bitcast.128, bf16[1024,192]{1,0:T(8,128)(2,1)S(1)} %get-tuple-element.117.keys, bf16[1024,192]{1,0:T(8,128)(2,1)S(1)} %get-tuple-element.116.values, f32[1,2048]{1,0:T(1,128)S(1)} %bitcast.140, ...), custom_call_target="tpu_custom_call" | custom-call | tf_op jit(solution)/shard_map/attention/pallas_call | solution.py:701
  225.5 22.8 %experts_forward.1 = (bf16[8,16,768]{2,1,0:T(8,128)(2,1)S(1)}, bf16[128,768]{1,0:T(8,128)(2,1)S(1)}, f32[16,768]{1,0:T(8,128)S(1)}, f32[16,768]{1,0:T(8,128)S(1)...) custom-call(bf16[128,192]{1,0:T(8,128)(2,1)S(1)} %copy-done.26, ...), custom_call_target="tpu_custom_call" | custom-call | tf_op jit(solution)/shard_map/experts_forward/pallas_call | solution.py:382
  262.8 93.6 %loss_and_experts_backward.1 = (bf16[8,128,1000]{2,1,0:T(8,128)(2,1)}, bf16[8,16,896]{2,1,0:T(8,128)(2,1)S(1)}, f32[8,2,768]{2,1,0:T(2,128)S(1)}, f32[768,384]{1...) custom-call(bf16[8,16,768]{2,1,0:T(8,128)(2,1)S(1)} %copy-done.22, bf16[768,1000]{1,0:T(8,128)(2,1)} %bitcast.30.table, ...), custom_call_target="tpu_custom_call" | custom-call | tf_op jit(solution)/shard_map/loss_and_experts_backward/pallas_call | solution.py:591
  360.4 5.9 %attention_backward.1 = (bf16[128,192]{1,0:T(8,128)(2,1)S(1)}, bf16[1024,192]{1,0:T(8,128)(2,1)S(1)}, bf16[1024,192]{1,0:T(8,128)(2,1)S(1)}, f32[3,32,8,128]{3,2,1,0:T(8,128)S(1)}) custom-call(bf16[128,768]{1,0:T(8,128)(2,1)S(1)} %slice.122.upstream, bf16[192,768]{1,0:T(8,128)(2,1)S(1)} %copy-done.16, bf16[128,192]{1,0:T(8,128)(2,1)S(1)} %bitcast.129, ...), custom_call_target="tpu_custom_call" | custom-call | tf_op jit(solution)/shard_map/attention_backward/pallas_call | solution.py:761
  369.6 6.5 %psum.22 = f32[1024,1]{0,1:T(1,128)S(1)} all-reduce(f32[1024,1]{0,1:T(1,128)S(1)} %bitcast.159), channel_id=1, replica_groups=mesh['dp'=8,'tensor'=4] {'tensor'}, use_global_device_ids=true, to_apply=%region_6.7 | all-reduce | flops 1024 | bytes 8192 | tf_op jit(solution)/shard_map/psum | solution.py:1003
  378.5 2.4 fusion.29
  380.9 3.4 copy.195
  384.3 4.7 reshape.430
  395.3 15.8 %all-reduce.5.cloned.1.call-done = f32[1024,96]{0,1:T(8,128)} async-done(((f32[1024,96]{0,1:T(8,128)}), f32[1024,96]{0,1:T(8,128)}) %all-reduce.5.cloned.1.call-update) | async-done | bytes 393232 | tf_op jit(solution)/shard_map/psum | solution.py:1003
  411.1 1.9 multiply_reduce_fusion.4
  413.0 2.0 convolution_bitcast_fusion
  415.9 1.9 convolution_bitcast_fusion.2
  417.8 1.5 subtract_convert_fusion
  419.3 8.3 %fusion = f32[8000,192]{0,1:T(8,128)S(1)} fusion(s32[1024]{0:T(1024)} %get-tuple-element.129, bf16[1024,96]{0,1:T(8,128)(2,1)S(1)} %get-tuple-element.114, bf16[1024,96]{0,1:T(8,128)(2,1)S(1)} %get-tuple-element.115), kind=kOutput, calls=%fused_computation.2 | convolution fusion | flops 3154706432 | bytes 6541312 | tf_op jit(solution)/shard_map/dot_general | solution.py:1017
  427.7 3.0 multiply_reduce_fusion
  437.9 39.5 %psum.23 = f32[]{:T(128)} all-reduce(f32[]{:T(128)S(6)} %add.331), channel_id=1, replica_groups=mesh['dp'=8,'tensor'=4] {'dp','tensor'}, use_global_device_ids=true, to_apply=%region_19.20 | all-reduce | flops 1 | bytes 8 | tf_op jit(solution)/shard_map/psum | solution.py:1032
  478.2 2.5 multiply_subtract_fusion.3
  480.7 3.8 multiply_subtract_fusion.2
  484.6 2.4 multiply_subtract_fusion.1
  489.0 4.5 multiply_subtract_fusion
  (285 shorter events, 56.3 us)
Async XLA Ops:
  7.2 214.3 %all-gather.4.cloned.1.call-start = ((), (), s32[]{:S(2)}) async-start(), calls=%async_computation.1 | async-start | bytes 1474560 | tf_op jit(solution)/shard_map/all_gather | solution.py:851
  48.3 38.4 %copy-start.61 = (f32[3,96,192]{2,1,0:T(8,128)S(1)}, f32[3,96,192]{2,1,0:T(8,128)}, u32[]{:S(2)}) copy-start(f32[3,96,192]{2,1,0:T(8,128)} %param.39) | copy-start | bytes 663556
  48.3 205.9 %all-to-all-start = ((bf16[8,1000,96]{1,2,0:T(8,128)(2,1)}), bf16[8,1000,96]{1,2,0:T(8,128)(2,1)}, u32[]{:S(2)}, u32[]{:S(2)}) async-start(bf16[8,1000,96]{1,2,0:T(8,128)(2,1)} %copy.190), calls=%async_computation | async-start | bytes 3145728 | tf_op jit(solution)/shard_map/all_to_all | solution.py:860
  54.1 357.0 %all-reduce.5.cloned.1.call-start = ((), (), s32[]{:S(2)}) async-start(), calls=%async_computation.2 | async-start | bytes 786432 | tf_op jit(solution)/shard_map/psum | solution.py:1003
  131.3 14.7 %copy-start.72 = (f32[3,96]{1,0:T(4,128)S(1)}, f32[3,96]{1,0:T(4,128)}, u32[]{:S(2)}) copy-start(f32[3,96]{1,0:T(4,128)} %param.54) | copy-start | bytes 3460
  145.7 20.6 %copy-start.76 = (f32[4,96]{1,0:T(4,128)S(1)}, f32[4,96]{1,0:T(4,128)}, u32[]{:S(2)}) copy-start(f32[4,96]{1,0:T(4,128)} %param.45) | copy-start | bytes 4612
  210.4 6.9 %copy-start.29 = (bf16[8,16,192]{2,1,0:T(8,128)(2,1)}, bf16[8,16,192]{2,1,0:T(8,128)(2,1)S(1)}, u32[]{:S(2)}) copy-start(bf16[8,16,192]{2,1,0:T(8,128)(2,1)S(1)} %get-tuple-element.55) | copy-start | bytes 147460
  210.5 11.0 %copy-start.1 = (f32[384,768]{1,0:T(8,128)S(1)}, f32[384,768]{1,0:T(8,128)}, u32[]{:S(2)}) copy-start(f32[384,768]{1,0:T(8,128)} %expert_out.3) | copy-start | bytes 3538948
  210.8 9.2 %copy-start.95 = (s32[128]{0:T(128)S(1)}, s32[128]{0:T(128)}, u32[]{:S(2)}) copy-start(s32[128]{0:T(128)} %reshape.431) | copy-start | bytes 1540
  210.8 9.7 %copy-start.86 = (s32[1,128]{1,0:T(1,128)S(1)}, s32[1,128]{1,0:T(1,128)}, u32[]{:S(2)}) copy-start(s32[1,128]{1,0:T(1,128)} %reshape.428) | copy-start | bytes 1540
  210.8 10.2 %copy-start.91 = (bf16[3,96]{1,0:T(4,128)(2,1)S(1)}, bf16[3,96]{1,0:T(4,128)(2,1)}, u32[]{:S(2)}) copy-start(bf16[3,96]{1,0:T(4,128)(2,1)} %convert_element_type.144) | copy-start | bytes 1732
  210.8 10.7 %copy-start = (f32[768,384]{1,0:T(8,128)S(1)}, f32[768,384]{1,0:T(8,128)}, u32[]{:S(2)}) copy-start(f32[768,384]{1,0:T(8,128)} %expert_in.3) | copy-start | bytes 3538948
  225.5 28.7 %copy-start.28 = (s32[128,1]{1,0:T(8,128)S(1)}, s32[128,1]{1,0:T(8,128)}, u32[]{:S(2)}) copy-start(s32[128,1]{1,0:T(8,128)} %sub.121.wanted) | copy-start | bytes 1540
  262.8 96.1 %copy-start.27 = (bf16[128,192]{1,0:T(8,128)(2,1)S(1)}, bf16[128,192]{1,0:T(8,128)(2,1)}, u32[]{:S(2)}) copy-start(bf16[128,192]{1,0:T(8,128)(2,1)} %copy-done.25) | copy-start | bytes 147460
  262.8 97.5 %copy-start.13 = (f32[3,128,1024]{2,1,0:T(8,128)S(1)}, f32[3,128,1024]{2,1,0:T(8,128)}, u32[]{:S(2)}) copy-start(f32[3,128,1024]{2,1,0:T(8,128)} %copy-done.12) | copy-start | bytes 4718596
  262.8 97.5 %copy-start.16 = (bf16[192,768]{1,0:T(8,128)(2,1)S(1)}, bf16[192,768]{1,0:T(8,128)(2,1)}, u32[]{:S(2)}) copy-start(bf16[192,768]{1,0:T(8,128)(2,1)} %constant_dynamic-slice_fusion.output_map) | copy-start | bytes 884740
  262.8 97.5 %copy-start.19 = (s32[128,1024]{1,0:T(8,128)S(1)}, s32[128,1024]{1,0:T(8,128)}, u32[]{:S(2)}) copy-start(s32[128,1024]{1,0:T(8,128)} %copy-done.18) | copy-start | bytes 1572868
  262.8 97.5 %copy-start.30 = (bf16[8,16,192]{2,1,0:T(8,128)(2,1)S(1)}, bf16[8,16,192]{2,1,0:T(8,128)(2,1)}, u32[]{:S(2)}) copy-start(bf16[8,16,192]{2,1,0:T(8,128)(2,1)} %copy-done.29) | copy-start | bytes 147460
  357.5 8.9 %copy-start.46 = (f32[8,2,768]{2,1,0:T(2,128)}, f32[8,2,768]{2,1,0:T(2,128)S(1)}, u32[]{:S(2)}) copy-start(f32[8,2,768]{2,1,0:T(2,128)S(1)} %get-tuple-element.78) | copy-start | bytes 147460
  357.5 8.9 %copy-start.51 = (f32[2,128]{1,0:T(2,128)}, f32[2,128]{1,0:T(2,128)S(1)}, u32[]{:S(2)}) copy-start(f32[2,128]{1,0:T(2,128)S(1)} %get-tuple-element.80) | copy-start | bytes 3076
  357.5 8.9 %copy-start.17 = (bf16[128,768]{1,0:T(8,128)(2,1)}, bf16[128,768]{1,0:T(8,128)(2,1)S(1)}, u32[]{:S(2)}) copy-start(bf16[128,768]{1,0:T(8,128)(2,1)S(1)} %slice.122.upstream) | copy-start | bytes 589828
  360.4 6.8 %copy-start.78 = (s32[128]{0:T(128)S(1)}, s32[128]{0:T(128)}, u32[]{:S(2)}) copy-start(s32[128]{0:T(128)} %fusion.52) | copy-start | bytes 1540
  368.8 7.2 %copy-start.60 = (bf16[3,96,192]{2,1,0:T(8,128)(2,1)S(1)}, bf16[3,96,192]{2,1,0:T(8,128)(2,1)}, u32[]{:S(2)}) copy-start(bf16[3,96,192]{2,1,0:T(8,128)(2,1)} %copy-done.59) | copy-start | bytes 331780
  369.5 7.9 %copy-start.8 = (bf16[1024,192]{1,0:T(8,128)(2,1)S(1)}, bf16[1024,192]{1,0:T(8,128)(2,1)}, u32[]{:S(2)}) copy-start(bf16[1024,192]{1,0:T(8,128)(2,1)} %copy-done.7) | copy-start | bytes 1179652
  419.3 8.4 %copy-start.55 = (f32[8000,96]{0,1:T(8,128)S(1)}, f32[8000,96]{0,1:T(8,128)}, u32[]{:S(2)}) copy-start(f32[8000,96]{0,1:T(8,128)} %reshape.430) | copy-start | bytes 9216004
  427.7 7.0 %copy-start.81 = (f32[96]{0:T(128)S(1)}, f32[96]{0:T(128)}, u32[]{:S(2)}) copy-start(f32[96]{0:T(128)} %get-tuple-element.118) | copy-start | bytes 1156
  427.7 7.0 %copy-start.82 = (f32[1,96]{1,0:T(1,128)S(1)}, f32[1,96]{1,0:T(1,128)}, u32[]{:S(2)}) copy-start(f32[1,96]{1,0:T(1,128)} %get-tuple-element.136) | copy-start | bytes 1156
  427.7 9.6 %copy-start.52 = (f32[2,128]{1,0:T(2,128)S(1)}, f32[2,128]{1,0:T(2,128)}, u32[]{:S(2)}) copy-start(f32[2,128]{1,0:T(2,128)} %copy-done.51) | copy-start | bytes 3076
  478.2 6.3 %copy-start.63 = (f32[384,768]{1,0:T(8,128)S(1)}, f32[384,768]{1,0:T(8,128)}, u32[]{:S(2)}) copy-start(f32[384,768]{1,0:T(8,128)} %param.52) | copy-start | bytes 3538948
  478.2 6.3 %copy-start.64 = (f32[384,768]{1,0:T(8,128)S(1)}, f32[384,768]{1,0:T(8,128)}, u32[]{:S(2)}) copy-start(f32[384,768]{1,0:T(8,128)} %param.53) | copy-start | bytes 3538948
  480.7 7.5 %copy-start.57 = (f32[8000,96]{0,1:T(8,128)S(1)}, f32[8000,96]{0,1:T(8,128)}, u32[]{:S(2)}) copy-start(f32[8000,96]{0,1:T(8,128)} %param.37) | copy-start | bytes 9216004
  480.7 7.5 %copy-start.58 = (f32[8000,96]{0,1:T(8,128)S(1)}, f32[8000,96]{0,1:T(8,128)}, u32[]{:S(2)}) copy-start(f32[8000,96]{0,1:T(8,128)} %param.38) | copy-start | bytes 9216004
  (67 other events, 159.6 us)
Sparse Core Ops, SparseCore 0:
  42.0 18.5 all-gather.3
  378.6 32.4 all-reduce.4

commit v3 on v0

--- a/solution.py
+++ b/solution.py
@@ -1,7 +1,11 @@
+import functools
 import math
+import types
 
 import jax
 import jax.numpy as jnp
+from jax.experimental import pallas as pl
+from jax.experimental.pallas import tpu as pltpu
 from jax import lax
 from jax.sharding import PartitionSpec as P
 
@@ -91,6 +95,1186 @@
     fixed_second = second / (1 - BETA2**STEP)
     weight = weight - rate * (fixed_first / (jnp.sqrt(fixed_second) + ADAM_EPS) + decay * weight)
     return (weight, first, second)
+
+
+MESH = pl.DeviceIdType.MESH
+DP = "dp"
+OUTSIDE = "_hbm"
+TENSOR = "tensor"
+UPDATE_BYTES = 20 * 1024 * 1024
+VMEM_BYTES = 33 * 1024 * 1024
+WHOLE = pl.BlockSpec(memory_space=pltpu.VMEM)
+DMA = pltpu.SemaphoreType.DMA
+F32 = jnp.float32
+BF16 = jnp.bfloat16
+STRIP = 256
+
+
+def greet_everyone():
+    barrier = pltpu.get_barrier_semaphore()
+    tensor = lax.axis_size(TENSOR)
+    total = lax.axis_size(DP) * tensor
+    here = lax.axis_index(DP) * tensor + lax.axis_index(TENSOR)
+
+    def signal(step, carry):
+        other = lax.rem(here + step, total)
+        pl.semaphore_signal(
+            barrier,
+            inc=1,
+            device_id={DP: other // tensor, TENSOR: lax.rem(other, tensor)},
+            device_id_type=MESH,
+        )
+        return carry
+
+    lax.fori_loop(1, total, signal, 0)
+    return barrier, total - 1
+
+
+class Move:
+    def __init__(self, axis, source, dest, sems, steps=None):
+        self.axis, self.count, self.here = axis, lax.axis_size(axis), lax.axis_index(axis)
+        self.source, self.dest, self.sems = source, dest, sems
+        self.steps = range(1, self.count) if steps is None else steps
+
+    def copy(self, step):
+        target = lax.rem(self.here + step, self.count)
+        return pltpu.make_async_remote_copy(
+            src_ref=self.source(target),
+            dst_ref=self.dest.at[self.here],
+            send_sem=self.sems.at[0, step],
+            recv_sem=self.sems.at[1, step],
+            device_id={self.axis: target},
+            device_id_type=MESH,
+        )
+
+    def start(self):
+        for step in self.steps:
+            self.copy(step).start()
+        return self
+
+    def arrive(self):
+        for step in self.steps:
+            self.copy(step).wait_recv()
+
+    def finish(self):
+        for step in self.steps:
+            self.copy(step).wait_send()
+
+
+def scatter_rows(axis, source, dest, sems):
+    height = dest.shape[1]
+    return Move(
+        axis,
+        lambda target: source.at[pl.ds(pl.multiple_of(target * height, height), height)],
+        dest,
+        sems,
+    ).start()
+
+
+def share_block(axis, dest, sems):
+    here = lax.axis_index(axis)
+    return Move(axis, lambda target: dest.at[here], dest, sems).start()
+
+
+class PairGather:
+    def __init__(self, buffer, sems):
+        self.buffer, self.sems = buffer, sems
+        self.count, self.here = lax.axis_size(DP), lax.axis_index(DP)
+        self.partner = self.here + 1 - 2 * lax.rem(self.here, 2)
+        self.half = self.count // 2
+
+    def copy(self, block, target, slot):
+        return pltpu.make_async_remote_copy(
+            src_ref=self.buffer.at[block],
+            dst_ref=self.buffer.at[block],
+            send_sem=self.sems.at[0, slot],
+            recv_sem=self.sems.at[1, slot],
+            device_id={DP: target},
+            device_id_type=MESH,
+        )
+
+    def direct(self, step):
+        return self.copy(self.here, lax.rem(self.here + 2 * step, self.count), step)
+
+    def onward(self, step):
+        block = lax.rem(self.here + self.count - 2 * step, self.count)
+        return self.copy(block, self.partner, self.half + step)
+
+    def start(self):
+        for step in range(1, self.half):
+            self.direct(step).start()
+        self.onward(0).start()
+        return self
+
+    def forward_one(self, step):
+        self.direct(step).wait_recv()
+        self.onward(step).start()
+
+    def forward(self):
+        for step in range(1, self.half):
+            self.forward_one(step)
+
+    def arrive(self):
+        for step in range(self.half):
+            self.onward(step).wait_recv()
+
+    def finish(self):
+        for step in range(1, self.half):
+            self.direct(step).wait_send()
+        for step in range(self.half):
+            self.onward(step).wait_send()
+
+
+class Relay:
+    def __init__(self, buffer, dp_sems, sems):
+        self.buffer, self.sems = buffer, sems
+        self.here = lax.axis_index(TENSOR)
+        self.gather = PairGather(buffer.at[self.here], dp_sems)
+        self.far = lax.rem(self.here + 2, 4)
+        self.near = self.here + 1 - 2 * lax.rem(self.here, 2)
+        self.blocks, self.block = lax.axis_size(DP), lax.axis_index(DP)
+        self.half = self.blocks // 2
+        partner = self.gather.partner
+        own = [lax.rem(self.block + self.blocks - 2 * k, self.blocks) for k in range(self.half)]
+        other = [lax.rem(partner + self.blocks - 2 * k, self.blocks) for k in range(self.half)]
+        self.order = own + other
+
+    def copy(self, kind, index):
+        source = self.far if kind == 2 else self.here
+        block = self.order[index]
+        return pltpu.make_async_remote_copy(
+            src_ref=self.buffer.at[source, block],
+            dst_ref=self.buffer.at[source, block],
+            send_sem=self.sems.at[0, kind, index],
+            recv_sem=self.sems.at[1, kind, index],
+            device_id={TENSOR: self.far if kind == 0 else self.near},
+            device_id_type=MESH,
+        )
+
+    def send(self, index):
+        self.copy(0, index).start()
+        self.copy(1, index).start()
+
+    def start(self):
+        self.gather.start()
+        self.send(0)
+        return self
+
+    def pass_on(self):
+        for step in range(1, self.half):
+            self.gather.forward_one(step)
+            self.send(step)
+        for step in range(self.half):
+            self.gather.onward(step).wait_recv()
+            self.send(self.half + step)
+
+    def spread(self):
+        for index in range(self.blocks):
+            self.copy(0, index).wait_recv()
+            self.copy(2, index).start()
+
+    def arrive(self):
+        for index in range(self.blocks):
+            self.copy(1, index).wait_recv()
+            self.copy(2, index).wait_recv()
+
+    def finish(self):
+        self.gather.finish()
+        for index in range(self.blocks):
+            for kind in range(3):
+                self.copy(kind, index).wait_send()
+
+
+class Everyone:
+    def __init__(self, buffer, sems):
+        self.buffer, self.sems = buffer, sems
+        self.tensor = lax.axis_size(TENSOR)
+        self.total = lax.axis_size(DP) * self.tensor
+        self.here = lax.axis_index(DP) * self.tensor + lax.axis_index(TENSOR)
+
+    def copy(self, step):
+        other = lax.rem(self.here + step, self.total)
+        return pltpu.make_async_remote_copy(
+            src_ref=self.buffer.at[self.here],
+            dst_ref=self.buffer.at[self.here],
+            send_sem=self.sems.at[0, step],
+            recv_sem=self.sems.at[1, step],
+            device_id={DP: other // self.tensor, TENSOR: lax.rem(other, self.tensor)},
+            device_id_type=MESH,
+        )
+
+    def each(self, act):
+        def one(step, carry):
+            act(self.copy(step))
+            return carry
+
+        lax.fori_loop(1, self.total, one, 0)
+
+    def start(self):
+        self.each(lambda copy: copy.start())
+        return self
+
+    def arrive(self):
+        self.each(lambda copy: copy.wait_recv())
+
+    def finish(self):
+        self.each(lambda copy: copy.wait_send())
+
+
+def dot_nt(a, b):
+    return lax.dot_general(a, b, (((1,), (1,)), ((), ())), preferred_element_type=F32)
+
+
+def dot_nn(a, b):
+    return jnp.dot(a, b, preferred_element_type=F32)
+
+
+def root_of(v):
+    return lax.rsqrt(jnp.mean(v * v, -1, keepdims=True) + NORM_EPS)
+
+
+def low(v):
+    return v.astype(BF16).astype(F32)
+
+
+def gelu_value(x):
+    slope = math.sqrt(2.0 / math.pi)
+    return 0.5 * x * (1.0 + jnp.tanh(slope * (x + 0.044715 * (x * x * x))))
+
+
+def gelu_slope(x):
+    slope = math.sqrt(2.0 / math.pi)
+    t = jnp.tanh(slope * (x + 0.044715 * (x * x * x)))
+    return 0.5 * (1.0 + t) + 0.5 * x * (1.0 - t * t) * (slope * (1.0 + 3 * 0.044715 * x * x))
+
+
+def lanes(shape):
+    return lax.broadcasted_iota(jnp.int32, shape, len(shape) - 1)
+
+
+def sublanes(shape):
+    return lax.broadcasted_iota(jnp.int32, shape, len(shape) - 2)
+
+
+def tensor_sum(total, buffer, sems):
+    here = lax.axis_index(TENSOR)
+    buffer[here] = total
+    move = share_block(TENSOR, buffer, sems)
+    move.arrive()
+    total = buffer[0]
+    for k in range(1, buffer.shape[0]):
+        total = total + buffer[k]
+    return total, move
+
+
+def norm_back_rows(v, g, upstream):
+    root = root_of(v)
+    scaled = g * upstream
+    inner = jnp.sum(scaled * v, -1, keepdims=True)
+    back = root * scaled - v * (root * root * root * inner / v.shape[-1])
+    return back, jnp.sum(upstream * v * root, 0, keepdims=True)
+
+
+def merge_stats(parts):
+    peak = parts[0][0:1]
+    for part in parts[1:]:
+        peak = jnp.maximum(peak, part[0:1])
+    total = sum(part[1:2] * jnp.exp(part[0:1] - peak) for part in parts)
+    target = sum(part[2:3] for part in parts)
+    plain = sum(part[3:4] for part in parts)
+    return jnp.concatenate([peak, total, target, plain, parts[0][4:8]], 0)
+
+
+def sum_blocks(ref):
+    total = ref[0].astype(F32)
+    for k in range(1, ref.shape[0]):
+        total = total + ref[k].astype(F32)
+    return total
+
+
+def across(ref, axis):
+    return jnp.concatenate([ref[k] for k in range(ref.shape[0])], axis)
+
+
+def squared(value):
+    return jnp.sum(value * value, keepdims=True)
+
+
+def step_kernel(names, small, weights, experts, vocab_rows, starts, *refs):
+    r = types.SimpleNamespace(**dict(zip(names, refs, strict=True)))
+    block, here = lax.axis_index(DP), lax.axis_index(TENSOR)
+    blocks, tensor = lax.axis_size(DP), lax.axis_size(TENSOR)
+    rows = r.own_ids.shape[1]
+    every = rows * blocks
+    picks = r.own_offsets.shape[1]
+    count = picks * blocks
+    columns, width = r.proj_weight.shape[1:]
+    features = columns * blocks
+    heads = width // HD
+    share = r.pages.shape[2]
+    group = blocks // tensor
+    scale = 1.0 / math.sqrt(HD)
+    own_rows = pl.ds(pl.multiple_of(block * picks, picks), picks)
+    moves = []
+
+    def keep(move):
+        moves.append(move)
+        return move
+
+    def load(name, sems, k):
+        copy = pltpu.make_async_copy(getattr(r, name + OUTSIDE), getattr(r, name), sems.at[k])
+        copy.start()
+        return copy
+
+    loads = [load(name, r.load_sems, k) for k, name in enumerate(small)]
+    greeting = greet_everyone()
+    held = [load(name, r.held_sems, k) for k, name in enumerate(weights)]
+    proj_load, map_load, table_load, in_load, out_load = held[:5]
+    for copy in loads:
+        copy.wait()
+
+    ids = r.own_ids[...].astype(F32)
+    offset_row = jnp.concatenate(
+        [r.own_offsets[...].astype(F32), jnp.zeros((1, rows - picks), F32)], 1
+    )
+    slot = lanes((rows, rows))
+    loss_hot = (sublanes((rows, rows)).astype(F32) == offset_row) & (slot < picks)
+    targets = r.own_targets[...]
+    upper = targets // 256
+    facts = jnp.concatenate(
+        [
+            upper.astype(F32),
+            (targets - upper * 256).astype(F32),
+            r.own_routes[...].astype(F32),
+            jnp.zeros((4, rows), F32),
+        ],
+        0,
+    )
+    facts = dot_nn(facts.astype(BF16), loss_hot.astype(F32).astype(BF16))
+    known = jnp.concatenate(
+        [
+            offset_row,
+            facts[0:1] * 256.0 + facts[1:2],
+            facts[2:4],
+            ids,
+            jnp.zeros((3, rows), F32),
+        ],
+        0,
+    )
+    r.known[block] = known
+    own_router = r.own_router[...]
+    own_small = jnp.concatenate(
+        [own_router, jnp.zeros((4 - experts, columns), F32), r.own_gains[...], jnp.zeros((1, columns), F32)]
+        if experts < 4
+        else [own_router, r.own_gains[...], jnp.zeros((1, columns), F32)],
+        0,
+    )
+    r.small[block] = jnp.concatenate([own_small, jnp.zeros((8, 128 - columns), F32)], 1)
+    map_load.wait()
+    r.maps[here, block] = r.map_weight[...].T.astype(BF16)
+    proj_load.wait()
+    for s in range(3):
+        r.proj[block, :, s * width : (s + 1) * width] = r.proj_weight[s].astype(BF16)
+    pl.semaphore_wait(*greeting)
+    to_known = keep(share_block(DP, r.known, r.sem_known))
+    to_small = keep(share_block(DP, r.small, r.sem_small))
+    to_proj = keep(PairGather(r.proj, r.sem_proj).start())
+
+    table_load.wait()
+    for k in range(blocks):
+        stop = min(vocab_rows, (k + 1) * share)
+        span = max(0, stop - k * share)
+        if span > 0:
+            r.pages[k, :, 0:span] = r.table_weight[:, k * share : stop].astype(BF16)
+        if span < share:
+            r.pages[k, :, span:share] = jnp.zeros((columns, share - span), BF16)
+    r.table[block] = r.pages[block]
+
+    def pages_move(steps):
+        return keep(
+            Move(DP, lambda target: r.pages.at[target], r.table, r.sem_pages, steps).start()
+        )
+
+    to_known.arrive()
+    base = (here * vocab_rows).astype(F32)
+    for k in range(blocks):
+        r.id_row[:, k * rows : (k + 1) * rows] = r.known[k][4:5, :] - base
+    chunk = group * rows
+    id_high = jnp.floor(r.id_row[...] * (1.0 / STRIP))
+    r.id_high[...] = id_high
+    r.id_place[...] = r.id_row[...] - id_high * STRIP
+    strips_of_page = share // STRIP
+    for step in range(1, tensor + 1):
+        target = lax.rem(here + step, tensor)
+        at = pl.ds(pl.multiple_of(target * chunk, chunk), chunk)
+        hot = sublanes((STRIP, chunk)).astype(F32) == r.id_place[:, at]
+        hot = hot.astype(F32).astype(BF16)
+        number = r.id_high[:, at]
+
+        def look(k, total, hot=hot, number=number):
+            strips = jnp.concatenate(
+                [r.pages[k, :, n * STRIP : (n + 1) * STRIP] for n in range(strips_of_page)], 0
+            )
+            found = dot_nn(strips, hot)
+            for n in range(strips_of_page):
+                mine = number == (k * strips_of_page + n).astype(F32)
+                total = total + jnp.where(mine, found[n * columns : (n + 1) * columns], 0.0)
+            return total
+
+        found = lax.fori_loop(0, blocks, look, jnp.zeros((columns, chunk), F32))
+        for b in range(group):
+            r.looked[target, b] = found[:, b * rows : (b + 1) * rows].astype(BF16)
+        if step == tensor - 1:
+            to_total = keep(
+                Move(TENSOR, lambda target: r.looked.at[target], r.first, r.sem_first).start()
+            )
+    to_proj.forward()
+    r.first[here] = r.looked[here]
+    to_total.arrive()
+    for b in range(group):
+        r.streams[here, block, :, b * rows : (b + 1) * rows] = sum_blocks(r.first.at[:, b]).astype(
+            BF16
+        )
+    to_streams = keep(Relay(r.streams, r.sem_stream, r.sem_streams).start())
+    to_maps = keep(Relay(r.maps, r.sem_map, r.sem_maps).start())
+    to_streams.pass_on()
+    to_maps.pass_on()
+    pages_now = [pages_move((1, 7, 2, 6) if blocks == 8 else None)]
+    to_small.arrive()
+    gain_columns = [low(r.small[k].T[0:columns, 4:5]) for k in range(blocks)]
+    small_rows = jnp.concatenate([r.small[k][:, 0:columns] for k in range(blocks)], 1)
+    gains = low(small_rows)
+    r.router[...] = jnp.concatenate(
+        [
+            jnp.where(sublanes(gains.shape) < experts, gains, 0.0),
+            jnp.zeros((128 - gains.shape[0], features), F32),
+        ],
+        0,
+    ).astype(BF16)
+    r.gains[...] = gains
+    r.id_low[...] = (
+        (sublanes((STRIP, every)).astype(F32) == r.id_place[...]).astype(F32).astype(BF16).T
+    )
+
+    def column_of(field):
+        table = jnp.concatenate(
+            [r.known[k][field : field + 1, :] for k in range(blocks)]
+            + ([jnp.zeros((8 - blocks, rows), F32)] if blocks < 8 else []),
+            0,
+        ).T
+        return jnp.concatenate([table[0:picks, k : k + 1] for k in range(blocks)], 0)
+
+    offsets, wanted, route_a, route_b = (
+        column_of(field).astype(jnp.int32) for field in range(4)
+    )
+    positions = offsets + sublanes((count, 1)) // picks * rows
+    period = 2 * every
+    bucket_row = jnp.concatenate(
+        [r.own_buckets[...].astype(F32), jnp.zeros((1, 1), F32)], 1
+    )
+    strips = [bucket_row[:, k * rows : (k + 1) * rows] for k in range(period // rows)]
+    mirror = (lanes((rows, rows)) + sublanes((rows, rows)) == rows - 1).astype(F32).astype(BF16)
+    strips = dot_nn(jnp.concatenate(strips, 0).astype(BF16), mirror)
+    flipped = jnp.concatenate(
+        [strips[k : k + 1, :] for k in reversed(range(period // rows))], 1
+    )
+    spread = jnp.broadcast_to(flipped, (rows, period))
+    turned = pltpu.roll(spread, period - rows, 1, stride=1, stride_axis=0).astype(BF16)
+    chosen = (lanes((count, rows)) == offsets).astype(F32).astype(BF16)
+    r.shifted[...] = dot_nn(chosen, turned).astype(jnp.int32)
+    for k in range(blocks):
+        begin = rows * (blocks - 1 - k)
+        r.bucket[k * picks : (k + 1) * picks, :] = r.shifted[
+            k * picks : (k + 1) * picks, begin : begin + every
+        ]
+    bucket_count = r.position_bias.shape[1]
+
+    def fill(k, carry):
+        at = pl.ds(pl.multiple_of(k * picks, picks), picks)
+        numbers = r.bucket[at, :]
+        terms = [jnp.zeros(numbers.shape, F32)] * heads
+        for b in range(bucket_count):
+            same = numbers == b
+            terms = [jnp.where(same, r.position_bias[h, b], terms[h]) for h in range(heads)]
+        for h in range(heads):
+            r.bias[h, at, :] = terms[h]
+        return carry
+
+    lax.fori_loop(0, blocks, fill, 0)
+
+    def picture_at(place):
+        inside = jnp.full(place.shape, -1, jnp.int32)
+        for n in range(starts):
+            begin = r.picture_start[0, n]
+            inside = jnp.where((place >= begin) & (place < begin + PIECE), n, inside)
+        return inside
+
+    key_position = lanes((count, every))
+    query_picture = picture_at(positions)
+    allowed = (key_position <= positions) | (
+        (picture_at(lanes((1, every))) == query_picture) & (query_picture >= 0)
+    )
+    to_streams.spread()
+    to_proj.arrive()
+    all_proj = across(r.proj, 0)
+    key_proj, value_proj = (
+        all_proj[:, k * width : (k + 1) * width].astype(F32).T.astype(BF16) for k in (1, 2)
+    )
+    gain_column = jnp.concatenate(gain_columns, 0)
+    back_hot = (key_position == positions).astype(F32).astype(BF16)
+    stream = jnp.zeros((count, features), F32)
+    normed_loss = jnp.zeros((count, features), F32)
+    to_streams.arrive()
+    for k in range(tensor):
+        part = slice(k * chunk, (k + 1) * chunk)
+        low_part = across(r.streams.at[k], 0)
+        wide_part = low_part.astype(F32)
+        root = lax.rsqrt(jnp.mean(wide_part * wide_part, 0, keepdims=True) + NORM_EPS)
+        r.roots[:, part] = root
+        normed_in = (wide_part * root * gain_column).astype(BF16)
+        r.keys[:, part] = dot_nn(key_proj, normed_in).astype(BF16)
+        r.values[:, part] = dot_nn(value_proj, normed_in).astype(BF16)
+        stream = stream + dot_nt(back_hot[:, part], low_part)
+        normed_loss = normed_loss + dot_nt(back_hot[:, part], normed_in)
+    query = dot_nn(normed_loss.astype(BF16), all_proj[:, 0:width]).astype(BF16)
+    to_maps.spread()
+
+    def head(value, h):
+        return value[:, h * HD : (h + 1) * HD]
+
+    def tall(ref, h):
+        return ref[h * HD : (h + 1) * HD, :]
+
+    for h in range(heads):
+        raw = dot_nn(head(query, h), tall(r.keys, h)) * scale + r.bias[h]
+        raw = jnp.where(allowed, raw, NEGATIVE)
+        terms = jnp.exp(raw - jnp.max(raw, -1, keepdims=True))
+        r.probs[h] = terms / jnp.sum(terms, -1, keepdims=True)
+    attended = jnp.concatenate(
+        [dot_nt(r.probs[h].astype(BF16), tall(r.values, h)).astype(BF16) for h in range(heads)],
+        1,
+    )
+    r.heads[here] = attended
+    to_heads = keep(share_block(TENSOR, r.heads, r.sem_heads))
+    in_load.wait()
+    out_load.wait()
+    in_low, out_low = r.in_weight[...].astype(BF16), r.out_weight[...].astype(BF16)
+    to_maps.arrive()
+    to_heads.arrive()
+
+    middle = stream
+    for k in range(tensor):
+        full = jnp.concatenate([r.maps[k, i] for i in range(blocks)], 0)
+        middle = middle + dot_nt(r.heads[k], full)
+    r.middle[...] = middle
+    gain_middle, gain_final = r.gains[5:6, :], r.gains[6:7, :]
+    normed_mid = (middle * root_of(middle) * gain_middle).astype(BF16)
+    inner = dot_nn(normed_mid, in_low)
+    active = gelu_value(inner).astype(BF16)
+    r.piece[...] = dot_nn(active, out_low).astype(BF16)
+    to_rows = keep(scatter_rows(DP, r.piece, r.arrived, r.sem_piece))
+    router_logits = dot_nt(normed_mid, r.router[...])
+    lane = lanes(router_logits.shape)
+    hot_a, hot_b = lane == route_a, lane == route_b
+    logit_a = jnp.sum(jnp.where(hot_a, router_logits, 0.0), 1, keepdims=True)
+    logit_b = jnp.sum(jnp.where(hot_b, router_logits, 0.0), 1, keepdims=True)
+    logit_top = jnp.maximum(logit_a, logit_b)
+    gate_a, gate_b = jnp.exp(logit_a - logit_top), jnp.exp(logit_b - logit_top)
+    both = gate_a + gate_b
+    r.gates[...] = jnp.where(hot_a, gate_a / both, 0.0) + jnp.where(hot_b, gate_b / both, 0.0)
+    own_gates = r.gates[own_rows, :]
+    own_middle = r.middle[own_rows, :]
+    if blocks == 8:
+        pages_now.append(pages_move((3,)))
+    r.arrived[block] = r.piece[own_rows, :]
+    to_rows.arrive()
+    depth = blocks // experts
+    mixed = jnp.zeros((picks, features), F32)
+    for e in range(experts):
+        part = r.arrived[e * depth].astype(F32)
+        for k in range(1, depth):
+            part = part + r.arrived[e * depth + k].astype(F32)
+        mixed = mixed + own_gates[:, e : e + 1] * part
+    mixed, to_sum = tensor_sum(mixed, r.summed, r.sem_summed)
+    keep(to_sum)
+    own_final = own_middle + mixed
+    r.final[block] = (own_final * root_of(own_final) * gain_final).astype(BF16)
+    to_final = keep(share_block(DP, r.final, r.sem_final))
+    if blocks == 8:
+        pages_now.append(pages_move((5, 4)))
+    to_final.arrive()
+    for move in pages_now:
+        move.arrive()
+
+    out = across(r.final, 0)
+    table = across(r.table, 0)
+    logits = dot_nn(out, table)
+    slot = lanes(logits.shape) + block * share
+    logits = jnp.where(slot < vocab_rows, logits, NEGATIVE)
+    hit = slot == wanted - here * vocab_rows
+    local_top = jnp.max(logits, -1, keepdims=True)
+    local_stats = (
+        local_top,
+        jnp.sum(jnp.exp(logits - local_top), -1, keepdims=True),
+        jnp.sum(jnp.where(hit & (slot < vocab_rows), logits, 0.0), -1, keepdims=True),
+        jnp.sum(jnp.where(slot < vocab_rows, logits, 0.0), -1, keepdims=True),
+    )
+    packed = jnp.zeros((count, 128), F32)
+    for k, column in enumerate(local_stats):
+        packed = jnp.where(lane == k, column, packed)
+    r.stats_a[here] = packed.T[0:8, :]
+    to_stats = keep(share_block(TENSOR, r.stats_a, r.sem_stats_a))
+    to_stats.arrive()
+    r.stats_b[block] = merge_stats([r.stats_a[k] for k in range(tensor)])
+    to_stats = keep(share_block(DP, r.stats_b, r.sem_stats_b))
+    weight = (query_picture < 0).astype(F32)
+    weight_row = jnp.where(lane == 0, weight, 0.0).T[0:1, :]
+    to_stats.arrive()
+    stats = merge_stats([r.stats_b[k] for k in range(blocks)])
+    log_total = stats[0:1] + jnp.log(stats[1:2])
+    per_row = (
+        log_total
+        - (1 - SMOOTH) * stats[2:3]
+        - SMOOTH * stats[3:4] / VOCAB
+        + ZLOSS * log_total * log_total
+    )
+    loss_sum = jnp.sum(weight_row * per_row, keepdims=True)
+    loss_count = jnp.sum(weight_row, keepdims=True)
+    total_column = jnp.where(sublanes((128, count)) == 0, log_total, 0.0).T[:, 0:1]
+    d_logits = weight * (
+        (1 + 2 * ZLOSS * total_column) * jnp.exp(logits - total_column)
+        - jnp.where(hit, 1 - SMOOTH, 0.0)
+        - SMOOTH / VOCAB
+    )
+    d_logits = jnp.where(slot < vocab_rows, d_logits, 0.0).astype(BF16)
+    r.d_logits_parts = [r.d_logits.at[k] for k in range(r.d_logits.shape[0])]
+    piece_rows = r.d_logits.shape[2]
+    for k, part in enumerate(r.d_logits_parts):
+        part[block] = d_logits[k * piece_rows : (k + 1) * piece_rows]
+    logit_moves = [
+        keep(PairGather(part, r.sem_logits.at[k])) for k, part in enumerate(r.d_logits_parts)
+    ]
+    r.sent[...] = dot_nt(d_logits, table).astype(BF16)
+    to_rows = keep(scatter_rows(DP, r.sent, r.arrived_b, r.sem_sent))
+    r.arrived_b[block] = r.sent[own_rows, :]
+    to_rows.arrive()
+    logit_moves[0].start()
+    d_normed, to_sum = tensor_sum(sum_blocks(r.arrived_b), r.summed_b, r.sem_summed_b)
+    keep(to_sum)
+    d_final, grad_final = norm_back_rows(own_final, gain_final, d_normed)
+    r.d_final[block] = d_final.astype(BF16)
+    to_final = keep(share_block(DP, r.d_final, r.sem_d_final))
+    to_final.arrive()
+    logit_moves[0].forward()
+    logit_moves[1].start()
+    upstream = across(r.d_final, 0).astype(F32)
+    expert = block // depth
+    gate = jnp.sum(jnp.where(lane == expert, r.gates[...], 0.0), 1, keepdims=True)
+    d_piece = (gate * upstream).astype(BF16)
+    d_inner = (dot_nt(d_piece, out_low) * gelu_slope(inner)).astype(BF16)
+    r.wide[:, 0:features] = dot_nt(d_inner, in_low).astype(BF16)
+    gate_part = jnp.sum(upstream * r.piece[...].astype(F32), 1, keepdims=True)
+    high = low(gate_part)
+    r.wide[:, features:] = jnp.where(
+        lane == expert, high, jnp.where(lane == expert + 64, gate_part - high, 0.0)
+    ).astype(BF16)
+    to_rows = keep(scatter_rows(DP, r.wide, r.arrived_c, r.sem_wide))
+    r.arrived_c[block] = r.wide[own_rows, :]
+    grad_out = dot_nn(active.T, d_piece)
+    grad_in = dot_nn(normed_mid.T, d_inner)
+    r.grad_out[...] = grad_out
+    r.grad_in[...] = grad_in
+    squares = squared(grad_out) + squared(grad_in)
+    to_rows.arrive()
+    logit_moves[1].forward()
+    logit_moves[2].start()
+    total, to_sum = tensor_sum(sum_blocks(r.arrived_c), r.summed_c, r.sem_summed_c)
+    keep(to_sum)
+    tail = total[:, features:]
+    d_gates = tail + pltpu.roll(tail, 64, 1)
+    own_known = known.T[0:picks].astype(jnp.int32)
+    slim = lanes(tail.shape)
+    named = (slim == own_known[:, 2:3]) | (slim == own_known[:, 3:4])
+    d_gates = jnp.where(named, d_gates, 0.0)
+    mean = jnp.sum(own_gates * d_gates, 1, keepdims=True)
+    d_router = jnp.where(named, own_gates * (d_gates - mean), 0.0).astype(BF16)
+    d_normed_mid = total[:, 0:features] + dot_nn(d_router, r.router[...])
+    d_from_mid, grad_middle = norm_back_rows(own_middle, gain_middle, d_normed_mid)
+    r.d_middle[block, :, 0:features] = (d_final + d_from_mid).astype(BF16)
+    r.d_middle[block, :, features:] = d_router
+    r.gain_parts[block, 0:1, :] = grad_middle
+    r.gain_parts[block, 1:2, :] = grad_final
+    to_middle = keep(share_block(DP, r.d_middle, r.sem_d_middle))
+    to_gains = keep(share_block(DP, r.gain_parts, r.sem_gains))
+    logit_moves[2].forward()
+    logit_moves[3].start()
+    stream_c = jnp.concatenate([r.streams[k, block] for k in range(tensor)], 1).astype(F32)
+    roots = r.roots[...]
+    gain_column = low(r.small[block].T[0:columns, 4:5])
+    normed_c = (stream_c * roots * gain_column).astype(BF16)
+    normed_loss = dot_nt(normed_c, back_hot).astype(BF16)
+    query_wide = dot_nn(query.T, back_hot)
+    to_middle.arrive()
+
+    d_middle = across(r.d_middle, 0)
+    d_attn = d_middle[:, 0:features]
+    own_map = jnp.concatenate([r.maps[here, i] for i in range(blocks)], 0)
+    d_attended = dot_nn(d_attn, own_map).astype(BF16)
+    d_query = []
+    for h in range(heads):
+        soft = r.probs[h]
+        d_head = head(d_attended, h)
+        d_probs = dot_nn(d_head, tall(r.values, h))
+        d_scores = soft * (d_probs - jnp.sum(soft * d_probs, -1, keepdims=True))
+        d_scores = d_scores.astype(BF16)
+        r.bias[h] = d_scores.astype(F32)
+        d_query.append((dot_nt(d_scores, tall(r.keys, h)) * scale).astype(BF16))
+        r.d_keys[h * HD : (h + 1) * HD, :] = (
+            dot_nn(head(query, h).T, d_scores) * scale
+        ).astype(BF16)
+        r.d_values[h * HD : (h + 1) * HD, :] = dot_nn(d_head.T, soft.astype(BF16)).astype(BF16)
+    d_query = jnp.concatenate(d_query, 1)
+    d_query_wide = dot_nn(d_query.T, back_hot).astype(BF16)
+    own_proj = r.proj[block]
+    d_columns = (
+        dot_nn(own_proj[:, 0:width], d_query_wide)
+        + dot_nn(own_proj[:, width : 2 * width], r.d_keys[...])
+        + dot_nn(own_proj[:, 2 * width :], r.d_values[...])
+    )
+    inner_row = jnp.sum(
+        d_query_wide.astype(F32) * query_wide
+        + r.d_keys[...].astype(F32) * r.keys[...].astype(F32)
+        + r.d_values[...].astype(F32) * r.values[...].astype(F32),
+        0,
+        keepdims=True,
+    )
+    inner_high = low(inner_row)
+    extra = sublanes((16, every))
+    r.part[0:columns, :] = d_columns.astype(BF16)
+    r.part[columns:, :] = jnp.where(
+        extra == 0, inner_high, jnp.where(extra == 1, inner_row - inner_high, 0.0)
+    ).astype(BF16)
+    to_part = keep(
+        Move(
+            TENSOR,
+            lambda target: r.part.at[:, pl.ds(pl.multiple_of(target * chunk, chunk), chunk)],
+            r.part_in,
+            r.sem_part,
+        ).start()
+    )
+    r.part_in[here] = r.part[:, pl.ds(pl.multiple_of(here * chunk, chunk), chunk)]
+    grad_proj = (
+        dot_nn(normed_loss, d_query),
+        dot_nt(normed_c, r.d_keys[...]),
+        dot_nt(normed_c, r.d_values[...]),
+    )
+    for s in range(3):
+        r.grad_proj[s] = grad_proj[s]
+        squares = squares + squared(grad_proj[s])
+    to_part.arrive()
+    r.part_all[here] = sum_blocks(r.part_in).astype(BF16)
+    to_parts = keep(share_block(TENSOR, r.part_all, r.sem_part_all))
+    r.bias_rows[...] = jnp.zeros(r.bias_rows.shape, F32)
+
+    def collect(k, carry):
+        at = pl.ds(pl.multiple_of(k * picks, picks), picks)
+        numbers = r.bucket[at, :]
+        parts = [r.bias[h, at, :] for h in range(heads)]
+        for b in range(bucket_count):
+            same = numbers == b
+            for h in range(heads):
+                kept = jnp.where(same, parts[h], 0.0)
+                kept = kept[0:8] + kept[8:16]
+                narrow = kept[:, 0:128]
+                for c in range(1, every // 128):
+                    narrow = narrow + kept[:, c * 128 : (c + 1) * 128]
+                r.bias_rows[h, b] += narrow
+        return carry
+
+    lax.fori_loop(0, count // picks, collect, 0)
+    grad_bias = jnp.sum(r.bias_rows[...], 2)
+    r.grad_bias[...] = grad_bias
+    grad_bias = jnp.sum(grad_bias, -1, keepdims=True)
+    squares = squares + jnp.sum(grad_bias * grad_bias, keepdims=True)[0] / blocks
+    pick_own = lanes((columns, features)) == sublanes((columns, features)) + block * columns
+    pick_own = pick_own.astype(F32).astype(BF16)
+    d_attn_t = dot_nt(pick_own, d_attn).astype(BF16)
+    out_t = dot_nt(pick_own, out).astype(BF16)
+    middle_t = dot_nt(pick_own, normed_mid).astype(BF16)
+    grad_map = dot_nt(attended.T, d_attn_t)
+    r.grad_map[...] = grad_map
+    squares = squares + squared(grad_map)
+    grad_router = dot_nt(d_middle[:, features:].T, middle_t)[0:8]
+    residual = dot_nn(d_attn_t, back_hot)
+    logit_moves[3].forward()
+    to_gains.arrive()
+    gain_sum = r.gain_parts[0]
+    for k in range(1, blocks):
+        gain_sum = gain_sum + r.gain_parts[k]
+    gain_sum = jnp.concatenate([gain_sum, jnp.zeros((6, features), F32)], 0)
+    gain_sum = pltpu.roll(gain_sum, lax.rem(features - block * columns, features), 1)
+    to_parts.arrive()
+    parts = across(r.part_all, 1).astype(F32)
+    d_columns = parts[0:columns]
+    inner_row = parts[columns : columns + 1] + parts[columns + 1 : columns + 2]
+    grad_first = jnp.sum(d_columns * stream_c * roots, 1, keepdims=True)
+    grad_first = jnp.broadcast_to(grad_first, (columns, 128)).T[0:1, :]
+    small = jnp.concatenate(
+        [
+            grad_router[0:4],
+            grad_first,
+            gain_sum[0:2, 0:columns],
+            jnp.zeros((1, columns), F32),
+        ],
+        0,
+    )
+    r.grad_small[:, 0:columns] = small
+    r.grad_small[:, columns:] = jnp.zeros((8, 128 - columns), F32)
+    squares = squares + squared(small) / tensor
+    d_stream = (
+        roots * gain_column * d_columns
+        - stream_c * (roots * roots * inner_row / features)
+        + residual
+    )
+    d_high = d_stream.astype(BF16)
+    d_low = (d_stream - d_high.astype(F32)).astype(BF16)
+    low_half = d_stream.astype(BF16)
+    full = vocab_rows // STRIP
+    ends = [(k, min(STRIP, vocab_rows - k * STRIP)) for k in range(full - full % 4, -(-vocab_rows // STRIP))]
+
+    def strip_mask(number):
+        return (r.id_high[...] == number).astype(F32).astype(BF16)
+
+    def scatter_four(k, carry):
+        masked = [low_half * strip_mask((k * 4 + n).astype(F32)) for n in range(4)]
+        found = dot_nn(jnp.concatenate(masked, 0), r.id_low[...])
+        begin = pl.multiple_of(k * 4 * STRIP, STRIP)
+        for n in range(4):
+            r.grad_table[:, pl.ds(begin + n * STRIP, STRIP)] = found[
+                n * columns : (n + 1) * columns
+            ]
+        return carry
+
+    lax.fori_loop(0, full // 4, scatter_four, 0)
+    masked = jnp.concatenate([low_half * strip_mask(float(k)) for k, size in ends], 0)
+    found = dot_nn(masked, r.id_low[...])
+    for n, (k, size) in enumerate(ends):
+        r.grad_table[:, k * STRIP : k * STRIP + size] = found[
+            n * columns : (n + 1) * columns, 0:size
+        ]
+    for move in logit_moves:
+        move.arrive()
+
+    def page_strips(k, total):
+        begin = pl.multiple_of(k * share, share)
+        return total + add_page(k, pl.ds(begin, share))
+
+    def add_page(k, where, size=share):
+        page = jnp.concatenate([part[k] for part in r.d_logits_parts], 0)
+        value = r.grad_table[:, where] + dot_nn(out_t, page)[:, 0:size]
+        r.grad_table[:, where] = value
+        return squared(value)
+
+    whole = vocab_rows // share
+    squares = squares + lax.fori_loop(0, whole, page_strips, jnp.zeros((1, 1), F32))
+    if vocab_rows > whole * share:
+        squares = squares + add_page(
+            whole, slice(whole * share, vocab_rows), vocab_rows - whole * share
+        )
+    r.squares[block * tensor + here] = jnp.broadcast_to(squares, (1, 128))
+    to_squares = keep(Everyone(r.squares, r.sem_squares).start())
+    to_squares.arrive()
+    norm = jnp.sqrt(sum_blocks(r.squares))
+    r.norm[...] = norm[:, 0:1]
+    r.clip[...] = (MAX_NORM / jnp.maximum(norm, MAX_NORM))[:, 0:1]
+    r.loss_sum[...] = loss_sum
+    r.loss_count[...] = loss_count
+    for copy in held[5:]:
+        copy.wait()
+    for move in moves:
+        move.finish()
+
+
+def run_step(blocks, tensor, experts, small, held, scalars):
+    rows = small["own_ids"].shape[1]
+    every = rows * blocks
+    picks = small["own_offsets"].shape[1]
+    count = picks * blocks
+    columns, width = held["proj_weight"].shape[1:]
+    features = columns * blocks
+    hidden = held["in_weight"].shape[1]
+    vocab_rows = held["table_weight"].shape[1]
+    heads, bucket_count = scalars["position_bias"].shape
+    share = -(-vocab_rows // (blocks * STRIP)) * STRIP
+    group = blocks // tensor
+    chunk = group * rows
+    wide = features + 128
+    outputs = dict(
+        grad_table=(columns, vocab_rows),
+        grad_proj=(3, columns, width),
+        grad_map=(width, columns),
+        grad_small=(8, 128),
+        grad_in=(features, hidden),
+        grad_out=(hidden, features),
+        grad_bias=(heads, bucket_count, 128),
+        norm=(1, 1),
+        clip=(1, 1),
+        loss_sum=(1, 1),
+        loss_count=(1, 1),
+    )
+    scratch = dict(
+        known=((blocks, 8, rows), F32),
+        small=((blocks, 8, 128), F32),
+        proj=((blocks, columns, 3 * width), BF16),
+        maps=((tensor, blocks, columns, width), BF16),
+        pages=((blocks, columns, share), BF16),
+        table=((blocks, columns, share), BF16),
+        id_row=((1, every), F32),
+        id_high=((1, every), F32),
+        id_place=((1, every), F32),
+        id_low=((every, STRIP), BF16),
+        looked=((tensor, group, columns, rows), BF16),
+        first=((tensor, group, columns, rows), BF16),
+        router=((128, features), BF16),
+        gains=((8, features), F32),
+        roots=((1, every), F32),
+        streams=((tensor, blocks, columns, chunk), BF16),
+        shifted=((count, 2 * every), jnp.int32),
+        bucket=((count, every), jnp.int32),
+        bias=((heads, count, every), F32),
+        keys=((width, every), BF16),
+        values=((width, every), BF16),
+        probs=((heads, count, every), F32),
+        heads=((tensor, count, width), BF16),
+        middle=((count, features), F32),
+        piece=((count, features), BF16),
+        gates=((count, 128), F32),
+        arrived=((blocks, picks, features), BF16),
+        summed=((tensor, picks, features), F32),
+        final=((blocks, picks, features), BF16),
+        stats_a=((tensor, 8, 128), F32),
+        stats_b=((blocks, 8, 128), F32),
+        d_logits=((4, blocks, count // 4, share), BF16),
+        sent=((count, features), BF16),
+        arrived_b=((blocks, picks, features), BF16),
+        summed_b=((tensor, picks, features), F32),
+        d_final=((blocks, picks, features), BF16),
+        wide=((count, wide), BF16),
+        arrived_c=((blocks, picks, wide), BF16),
+        summed_c=((tensor, picks, wide), F32),
+        d_middle=((blocks, picks, wide), BF16),
+        gain_parts=((blocks, 2, features), F32),
+        d_keys=((width, every), BF16),
+        d_values=((width, every), BF16),
+        part=((columns + 16, every), BF16),
+        part_in=((tensor, columns + 16, chunk), BF16),
+        part_all=((tensor, columns + 16, chunk), BF16),
+        bias_rows=((heads, bucket_count, 8, 128), F32),
+        squares=((blocks * tensor, 1, 128), F32),
+    )
+    scratch.update({name: (array.shape, array.dtype) for name, array in small.items()})
+    outputs.update({name: array.shape for name, array in held.items()})
+    dp, ten = (2, blocks), (2, tensor)
+    sems = dict(
+        load_sems=(len(small),),
+        held_sems=(len(held),),
+        sem_squares=(2, blocks * tensor),
+        sem_logits=(4, 2, blocks),
+        sem_known=dp,
+        sem_small=dp,
+        sem_proj=dp,
+        sem_map=dp,
+        sem_pages=dp,
+        sem_piece=dp,
+        sem_final=dp,
+        sem_stats_b=dp,
+        sem_sent=dp,
+        sem_d_final=dp,
+        sem_wide=dp,
+        sem_d_middle=dp,
+        sem_gains=dp,
+        sem_first=ten,
+        sem_stream=dp,
+        sem_streams=(2, 3, blocks),
+        sem_maps=(2, 3, blocks),
+        sem_heads=ten,
+        sem_summed=ten,
+        sem_stats_a=ten,
+        sem_summed_b=ten,
+        sem_summed_c=ten,
+        sem_part=ten,
+        sem_part_all=ten,
+    )
+    copied = {**small, **held}
+    names = tuple(name + OUTSIDE for name in copied) + tuple(scalars)
+    names += tuple(outputs) + tuple(scratch) + tuple(sems)
+    starts = scalars["picture_start"].shape[1]
+    results = pl.pallas_call(
+        functools.partial(
+            step_kernel, names, tuple(small), tuple(held), experts, vocab_rows, starts
+        ),
+        out_shape=[
+            jax.ShapeDtypeStruct(shape, F32) if shape == (1, 1) else pltpu.VMEM(shape, F32)
+            for shape in outputs.values()
+        ],
+        in_specs=[pl.BlockSpec(memory_space=pltpu.HBM)] * len(copied)
+        + [pl.BlockSpec(memory_space=pltpu.SMEM)] * len(scalars),
+        out_specs=[WHOLE] * len(outputs),
+        scratch_shapes=[pltpu.VMEM(*spec) for spec in scratch.values()]
+        + [DMA(shape) for shape in sems.values()],
+        compiler_params=pltpu.CompilerParams(
+            collective_id=0, has_side_effects=True, vmem_limit_bytes=VMEM_BYTES
+        ),
+        name="training_step",
+    )(*copied.values(), *scalars.values())
+    return dict(zip(outputs, results))
+
+
+def update_piece(weight, first, second, grad, rate, decay):
+    first = BETA1 * first + (1 - BETA1) * grad
+    second = BETA2 * second + (1 - BETA2) * (grad * grad)
+    spread = second * lax.rsqrt(second) * math.sqrt(1 / (1 - BETA2**STEP)) + ADAM_EPS
+    step = first / spread
+    return weight * (1 - rate * decay) - (rate / (1 - BETA1**STEP)) * step, first, second
+
+
+def update_kernel(jobs, clip, *refs):
+    grads, refs = refs[: len(jobs)], refs[len(jobs) :]
+    total = 3 * len(jobs)
+    olds, outs, news, done = refs[:total], refs[total : 2 * total], refs[2 * total : -1], refs[-1]
+    factor = clip[0, 0]
+    copies = []
+    for index, (height, rate, decay, begin, reduced) in enumerate(jobs):
+        trio = slice(3 * index, 3 * index + 3)
+        whole = news[3 * index].shape[0]
+        for piece in range(0, whole, height):
+            rows = slice(piece, piece + height)
+            if reduced:
+                change = jnp.sum(grads[index][...], -1)
+            elif begin is not None:
+                change = grads[index][begin : begin + whole, 0 : news[3 * index].shape[1]]
+            else:
+                change = grads[index][rows]
+            values = update_piece(
+                *(ref[rows] for ref in olds[trio]), factor * change, rate, decay
+            )
+            for which, value in enumerate(values):
+                new, out = news[3 * index + which], outs[3 * index + which]
+                new[rows] = value
+                part = pl.ds(piece, height)
+                copy = pltpu.make_async_copy(new.at[part], out.at[part], done.at[len(copies)])
+                copy.start()
+                copies.append(copy)
+    for copy in copies:
+        copy.wait()
+
+
+def run_update(clip, jobs, grads, olds):
+    shapes = [old.shape for old in olds]
+    pieces = sum(3 * shapes[3 * k][0] // job[0] for k, job in enumerate(jobs))
+    results = pl.pallas_call(
+        functools.partial(update_kernel, jobs),
+        out_shape=[jax.ShapeDtypeStruct(shape, F32) for shape in shapes],
+        in_specs=[pl.BlockSpec(memory_space=pltpu.SMEM)] + [WHOLE] * (len(grads) + len(olds)),
+        out_specs=[pl.BlockSpec(memory_space=pltpu.HBM)] * len(shapes),
+        scratch_shapes=[pltpu.VMEM(shape, F32) for shape in shapes] + [DMA((pieces,))],
+        compiler_params=pltpu.CompilerParams(vmem_limit_bytes=UPDATE_BYTES),
+        name="update",
+    )(clip, *grads, *olds)
+    return [results[3 * k : 3 * k + 3] for k in range(len(jobs))]
+
+
+def fast_local(
+    token_ids,
+    targets,
+    loss_offsets,
+    routes,
+    picture_start,
+    buckets,
+    embedding,
+    embedding_first,
+    embedding_second,
+    attn_proj,
+    attn_proj_first,
+    attn_proj_second,
+    out_proj,
+    out_proj_first,
+    out_proj_second,
+    router,
+    router_first,
+    router_second,
+    expert_in,
+    expert_in_first,
+    expert_in_second,
+    expert_out,
+    expert_out_first,
+    expert_out_second,
+    norm_gains,
+    norm_gains_first,
+    norm_gains_second,
+    position_bias,
+    position_bias_first,
+    position_bias_second,
+):
+    dp_count = lax.axis_size("dp")
+    tensor_count = lax.axis_size("tensor")
+    experts = router.shape[0]
+    small = dict(
+        own_ids=token_ids[None, :],
+        own_targets=targets[None, :],
+        own_offsets=loss_offsets[None, :],
+        own_routes=routes.T,
+        own_buckets=buckets[None, :],
+        own_router=router,
+        own_gains=norm_gains,
+    )
+    held = dict(
+        proj_weight=attn_proj,
+        map_weight=out_proj,
+        table_weight=embedding.T,
+        in_weight=expert_in,
+        out_weight=expert_out,
+        table_first=embedding_first.T,
+        table_second=embedding_second.T,
+        in_first=expert_in_first,
+        in_second=expert_in_second,
+        out_first=expert_out_first,
+        out_second=expert_out_second,
+        proj_first=attn_proj_first,
+        proj_second=attn_proj_second,
+        map_first=out_proj_first,
+        map_second=out_proj_second,
+    )
+    scalars = dict(position_bias=position_bias, picture_start=picture_start)
+    g = types.SimpleNamespace(**run_step(dp_count, tensor_count, experts, small, held, scalars))
+    kinds = (
+        (8, 0, None, False),
+        (expert_in.shape[0] // 8, 4, None, False),
+        (expert_out.shape[0] // 8, 5, None, False),
+        (1, 1, None, False),
+        (out_proj.shape[0], 2, None, False),
+        (experts, 3, 0, False),
+        (3, 6, 4, False),
+        (position_bias.shape[0], 7, None, True),
+    )
+    jobs = tuple(
+        (height, RATES[k], DECAYS[k], begin, reduced) for height, k, begin, reduced in kinds
+    )
+    grads = (g.grad_table, g.grad_in, g.grad_out, g.grad_proj, g.grad_map)
+    grads += (g.grad_small, g.grad_small, g.grad_bias)
+    olds = (g.table_weight, g.table_first, g.table_second, g.in_weight, g.in_first, g.in_second)
+    olds += (g.out_weight, g.out_first, g.out_second, g.proj_weight, g.proj_first, g.proj_second)
+    olds += (g.map_weight, g.map_first, g.map_second, router, router_first, router_second)
+    olds += (norm_gains, norm_gains_first, norm_gains_second)
+    olds += (position_bias, position_bias_first, position_bias_second)
+    new = run_update(g.clip, jobs, grads, olds)
+    results = [value.T for value in new[0]]
+    for k in (3, 4, 5, 1, 2, 6, 7):
+        results.extend(new[k])
+    grad_norm, loss_sum, loss_count = (
+        value.reshape(()) for value in (g.norm, g.loss_sum, g.loss_count)
+    )
+    return (*results, grad_norm, loss_sum, loss_count)
 
 
 def local(
@@ -492,6 +1676,29 @@
     )
 
 
+def fits(dp_count, tensor_count, arrays):
+    token_ids, loss_offsets, routes, picture_start = arrays[0], arrays[2], arrays[3], arrays[4]
+    columns, router, gains = arrays[6].shape[1], arrays[15], arrays[24]
+    rows, picks = token_ids.shape[0], loss_offsets.shape[0]
+    return (
+        rows == 128
+        and rows * dp_count <= SEQ
+        and picture_start.shape[0] == 1
+        and picks == 16
+        and picks * dp_count == 128
+        and dp_count % 4 == 0
+        and tensor_count == 4
+        and dp_count % router.shape[0] == 0
+        and dp_count % 2 == 0
+        and dp_count <= 8
+        and router.shape[0] <= 4
+        and routes.shape[1] == 2
+        and gains.shape[0] == 3
+        and columns % 16 == 0
+        and columns <= 128
+    )
+
+
 def solution(mesh):
     in_specs = (
         P("dp"),
@@ -554,4 +1761,9 @@
         P(),
         P(),
     )
-    return jax.shard_map(local, mesh=mesh, in_specs=in_specs, out_specs=out_specs, check_vma=False)
+
+    def chosen(*arrays):
+        sizes = lax.axis_size("dp"), lax.axis_size("tensor")
+        return (fast_local if fits(*sizes, arrays) else local)(*arrays)
+
+    return jax.shard_map(chosen, mesh=mesh, in_specs=in_specs, out_specs=out_specs, check_vma=False)

time: 1700 us -> 189 us (0.11)
  waiting for transfers between devices: 938 us -> 0 us
  blocking collectives: 350 us -> 0 us
  local copies, waits for them, and re-layouts: 219 us -> 0.04 us
  Pallas kernels: 0 us -> 182 us
  other arithmetic: 82.9 us -> 0 us
  matrix products: 54.8 us -> 0 us
  between operations: 25.2 us -> 6.69 us
    unnamed x18 -> x0, waiting for transfers between devices: 565 us -> none
    all_gather x6 -> x0, blocking collectives: 195 us -> none  [the longest x1 43 us: local(): lax.all_gather(attn_proj.astype(bf16), 'dp', axis=1, tiled=True)]
    psum x6 -> x0, waiting for transfers between devices: 190 us -> none  [tensor_total(): return lax.psum(value, 'tensor')]
    pallas_call x0 -> x2, Pallas kernels: none -> 182 us  [the longest x1 174 us: run_step(): pl.pallas_call(functools.partial(step_kernel, names, tuple(small), tuple(...]
    all_gather x1 -> x0, waiting for transfers between devices: 88.3 us -> none  [local(): lax.all_gather(embedding.astype(bf16), 'dp', axis=1, tiled=True)]
    all_to_all x2 -> x0, blocking collectives: 82.9 us -> none  [route_exchange(): return lax.all_to_all(value, 'dp', split_axis=0, concat_axis=0, tiled=True)]
    psum x3 -> x0, blocking collectives: 66.7 us -> none  [the longest x1 39.6 us: local(): lax.psum((squares, loss_local / tensor_count, jnp.sum(weight) / tensor_co...]
    reduce_scatter x1 -> x0, waiting for transfers between devices: 64.8 us -> none  [local(): lax.psum_scatter(ordered, 'dp', scatter_dimension=1, tiled=True)]
  transfers between devices with their start and end apart: 15 -> 0, of which waited for: 13 -> 0; matrix products, arithmetic and copies ran while one was open for 5% -> 0% of each run, Pallas kernels for 0% -> 0%
where the time goes in v3:
time: 189 us
  Pallas kernels  182 us (96%)
  between operations  6.69 us (4%)
    pallas_call x1, Pallas kernels, run_step(): pl.pallas_call(functools.partial(step_kernel, names, tuple(small), tuple(...  174 us
    pallas_call x1, Pallas kernels, run_update(): pl.pallas_call(functools.partial(update_kernel, jobs), out_shape=[jax.Sha...  7.85 us

profile of v3, /device:TPU:0, one launch (start us, length us, event | category | flops | bytes accessed | tf_op | source)
XLA Modules:
  0.0 189.0 jit_solution(15579901927499354726)
XLA Ops:
  1.3 0.0 copy-start
  1.3 0.0 copy-start.1
  1.3 0.0 copy-start.2
  1.4 0.0 copy-start.3
  1.4 0.0 copy-start.4
  1.4 0.0 copy-start.5
  1.4 0.0 copy-start.6
  1.4 0.0 copy-start.7
  1.4 0.0 copy-start.8
  1.4 174.4 %training_step.1 = (f32[96,8000]{1,0:T(8,128)S(1)}, f32[3,96,192]{2,1,0:T(8,128)S(1)}, f32[192,96]{1,0:T(8,128)S(1)}, f32[8,128]{1,0:T(8,128)S(1)}, f32[768,384]...) custom-call(s32[1,128]{1,0:T(1,128)} %bitcast.19, ...), custom_call_target="tpu_custom_call" | custom-call | tf_op jit(solution)/shard_map/training_step/pallas_call | solution.py:1112
  175.8 0.0 copy-done
  175.8 0.0 copy-done.1
  175.8 0.0 copy-done.2
  175.8 0.0 copy-done.3
  175.8 0.0 copy-done.4
  175.8 0.0 copy-done.5
  175.9 0.0 copy-done.6
  175.9 0.0 copy-done.7
  175.9 0.0 copy-done.8
  175.9 7.9 %update.1 = (f32[96,8000]{1,0:T(8,128)}, f32[96,8000]{1,0:T(8,128)}, f32[96,8000]{1,0:T(8,128)}, f32[768,384]{1,0:T(8,128)}, f32[768,384]{1,0:T(8,128)}, /*index...) custom-call(f32[1,1]{1,0:T(1,128)} %get-tuple-element.77.clip, ...), custom_call_target="tpu_custom_call" | custom-call | tf_op jit(solution)/shard_map/update/pallas_call | solution.py:1175
Async XLA Ops:
  1.3 174.5 %copy-start = (f32[4,96]{1,0:T(4,128)S(1)}, f32[4,96]{1,0:T(4,128)}, u32[]{:S(2)}) copy-start(f32[4,96]{1,0:T(4,128)} %refs_23_.2) | copy-start | bytes 4612
  1.3 174.5 %copy-start.1 = (f32[3,96]{1,0:T(4,128)S(1)}, f32[3,96]{1,0:T(4,128)}, u32[]{:S(2)}) copy-start(f32[3,96]{1,0:T(4,128)} %refs_26_.1) | copy-start | bytes 3460
  1.3 174.5 %copy-start.2 = (f32[3,32]{1,0:T(4,128)S(1)}, f32[3,32]{1,0:T(4,128)}, u32[]{:S(2)}) copy-start(f32[3,32]{1,0:T(4,128)} %refs_29_.1) | copy-start | bytes 1156
  1.4 174.5 %copy-start.3 = (f32[4,96]{1,0:T(4,128)S(1)}, f32[4,96]{1,0:T(4,128)}, u32[]{:S(2)}) copy-start(f32[4,96]{1,0:T(4,128)} %refs_24_.1) | copy-start | bytes 4612
  1.4 174.5 %copy-start.4 = (f32[4,96]{1,0:T(4,128)S(1)}, f32[4,96]{1,0:T(4,128)}, u32[]{:S(2)}) copy-start(f32[4,96]{1,0:T(4,128)} %refs_25_.1) | copy-start | bytes 4612
  1.4 174.5 %copy-start.5 = (f32[3,96]{1,0:T(4,128)S(1)}, f32[3,96]{1,0:T(4,128)}, u32[]{:S(2)}) copy-start(f32[3,96]{1,0:T(4,128)} %refs_27_.1) | copy-start | bytes 3460
  1.4 174.5 %copy-start.6 = (f32[3,96]{1,0:T(4,128)S(1)}, f32[3,96]{1,0:T(4,128)}, u32[]{:S(2)}) copy-start(f32[3,96]{1,0:T(4,128)} %refs_28_.1) | copy-start | bytes 3460
  1.4 174.5 %copy-start.7 = (f32[3,32]{1,0:T(4,128)S(1)}, f32[3,32]{1,0:T(4,128)}, u32[]{:S(2)}) copy-start(f32[3,32]{1,0:T(4,128)} %refs_30_.1) | copy-start | bytes 1156
  1.4 174.5 %copy-start.8 = (f32[3,32]{1,0:T(4,128)S(1)}, f32[3,32]{1,0:T(4,128)}, u32[]{:S(2)}) copy-start(f32[3,32]{1,0:T(4,128)} %refs_31_.1) | copy-start | bytes 1156

commit v4 on v3

--- a/solution.py
+++ b/solution.py
@@ -285,6 +285,114 @@
                 self.copy(kind, index).wait_send()
 
 
+def split_again(tile):
+    value = tile + pltpu.roll(tile, 64, 1)
+    high = value.astype(BF16).astype(F32)
+    return jnp.where(lanes(tile.shape) < 64, high, value - high)
+
+
+class AllSum:
+    def __init__(self, source, scratch, sems, halves):
+        self.source, self.sems, self.halves = source, sems, halves
+        self.parts, self.tiles, self.arrived, self.done, self.whole = scratch
+        self.here, self.block = lax.axis_index(TENSOR), lax.axis_index(DP)
+        self.height = self.parts.shape[1]
+        self.owners = self.tiles.shape[0]
+        self.own = pl.ds(pl.multiple_of(self.here * self.height, self.height), self.height)
+        self.first = scatter_rows(TENSOR, source, self.parts, sems[0])
+        self.parts[self.here] = source[self.own, :]
+
+    def owned(self, act):
+        pl.when(self.block < self.owners)(act)
+
+    def to_owner(self, owner):
+        return pltpu.make_async_remote_copy(
+            src_ref=self.tiles.at[owner],
+            dst_ref=self.arrived.at[self.block],
+            send_sem=self.sems[1].at[0, owner],
+            recv_sem=self.sems[1].at[1, self.block],
+            device_id={DP: owner},
+            device_id_type=MESH,
+        )
+
+    def from_block(self, k):
+        return pltpu.make_async_remote_copy(
+            src_ref=self.tiles.at[0],
+            dst_ref=self.arrived.at[k],
+            send_sem=self.sems[1].at[0, 0],
+            recv_sem=self.sems[1].at[1, k],
+            device_id={DP: k},
+            device_id_type=MESH,
+        )
+
+    def others(self, limit, act):
+        for k in range(limit):
+            pl.when(self.block != k)(lambda k=k: act(k))
+
+    def tile_to(self, k):
+        return pltpu.make_async_remote_copy(
+            src_ref=self.done.at[self.block],
+            dst_ref=self.done.at[self.block],
+            send_sem=self.sems[2].at[0, k],
+            recv_sem=self.sems[2].at[1, self.block],
+            device_id={DP: k},
+            device_id_type=MESH,
+        )
+
+    def tile_from(self, k):
+        return pltpu.make_async_remote_copy(
+            src_ref=self.done.at[k],
+            dst_ref=self.done.at[k],
+            send_sem=self.sems[2].at[0, k],
+            recv_sem=self.sems[2].at[1, k],
+            device_id={DP: k},
+            device_id_type=MESH,
+        )
+
+    def scatter(self, factor=None):
+        self.first.arrive()
+        total = sum_blocks(self.parts)
+        if factor is not None:
+            total = total * factor[self.own, :]
+        for owner in range(self.owners):
+            tile = total[:, owner * 128 : (owner + 1) * 128]
+            if self.halves and owner == self.owners - 1:
+                tile = split_again(tile)
+            self.tiles[owner] = tile.astype(BF16)
+        self.others(self.owners, lambda owner: self.to_owner(owner).start())
+
+        @self.owned
+        def _():
+            self.arrived[self.block] = self.tiles[self.block]
+
+    def gather(self):
+        blocks = lax.axis_size(DP)
+
+        @self.owned
+        def _():
+            self.others(blocks, lambda k: self.from_block(k).wait_recv())
+            tile = sum_blocks(self.arrived)
+            if self.halves:
+                tile = jnp.where(self.block == self.owners - 1, split_again(tile), tile)
+            self.done[self.block] = tile.astype(BF16)
+            self.others(blocks, lambda k: self.tile_to(k).start())
+
+    def result(self):
+        self.others(self.owners, lambda k: self.tile_from(k).wait_recv())
+        for k in range(self.owners):
+            self.whole[self.here, :, k * 128 : (k + 1) * 128] = self.done[k]
+        self.last = share_block(TENSOR, self.whole, self.sems[3])
+        self.last.arrive()
+        return across(self.whole, 0).astype(F32)
+
+    def finish(self):
+        self.first.finish()
+        self.others(self.owners, lambda owner: self.to_owner(owner).wait_send())
+        blocks = lax.axis_size(DP)
+        self.owned(lambda: self.others(blocks, lambda k: self.tile_to(k).wait_send()))
+        self.last.finish()
+
+
 class Everyone:
     def __init__(self, buffer, sems):
         self.buffer, self.sems = buffer, sems
@@ -357,14 +465,10 @@
 
 
 def tensor_sum(total, buffer, sems):
-    here = lax.axis_index(TENSOR)
-    buffer[here] = total
+    buffer[lax.axis_index(TENSOR)] = total.astype(BF16)
     move = share_block(TENSOR, buffer, sems)
     move.arrive()
-    total = buffer[0]
-    for k in range(1, buffer.shape[0]):
-        total = total + buffer[k]
-    return total, move
+    return sum_blocks(buffer), move
 
 
 def norm_back_rows(v, g, upstream):
@@ -375,21 +479,26 @@
     return back, jnp.sum(upstream * v * root, 0, keepdims=True)
 
 
-def merge_stats(parts):
-    peak = parts[0][0:1]
-    for part in parts[1:]:
-        peak = jnp.maximum(peak, part[0:1])
-    total = sum(part[1:2] * jnp.exp(part[0:1] - peak) for part in parts)
-    target = sum(part[2:3] for part in parts)
-    plain = sum(part[3:4] for part in parts)
-    return jnp.concatenate([peak, total, target, plain, parts[0][4:8]], 0)
-
-
 def sum_blocks(ref):
     total = ref[0].astype(F32)
     for k in range(1, ref.shape[0]):
         total = total + ref[k].astype(F32)
     return total
+
+
+def packed_rows(value):
+    rows, wide = value.shape
+    whole, half = wide // 128, rows // 2
+    tail = value[:, whole * 128 :]
+    parts = [value[:, t * 128 : (t + 1) * 128] for t in range(whole)]
+    return jnp.concatenate(parts + [jnp.concatenate([tail[0:half], tail[half:]], 1)], 0)
+
+
+def unpacked_rows(value, rows):
+    whole = value.shape[0] // rows
+    tail = value[whole * rows :]
+    parts = [value[t * rows : (t + 1) * rows] for t in range(whole)]
+    return jnp.concatenate(parts + [jnp.concatenate([tail[:, 0:64], tail[:, 64:]], 0)], 1)
 
 
 def across(ref, axis):
@@ -414,8 +523,12 @@
     share = r.pages.shape[2]
     group = blocks // tensor
     scale = 1.0 / math.sqrt(HD)
-    own_rows = pl.ds(pl.multiple_of(block * picks, picks), picks)
     moves = []
+
+    def all_sum(source, number):
+        scratch = [getattr(r, f"sum_{k}_{number}") for k in range(5)]
+        sems = [getattr(r, f"sum_sem_{k}_{number}") for k in range(4)]
+        return keep(AllSum(source, scratch, sems, number == 2))
 
     def keep(move):
         moves.append(move)
@@ -471,13 +584,15 @@
     )
     r.small[block] = jnp.concatenate([own_small, jnp.zeros((8, 128 - columns), F32)], 1)
     map_load.wait()
-    r.maps[here, block] = r.map_weight[...].T.astype(BF16)
+    r.maps[here, block] = packed_rows(r.map_weight[...].T).astype(BF16)
     proj_load.wait()
-    for s in range(3):
-        r.proj[block, :, s * width : (s + 1) * width] = r.proj_weight[s].astype(BF16)
+    own_proj = jnp.concatenate([r.proj_weight[s] for s in range(3)], 1)
+    r.proj[block] = packed_rows(own_proj).astype(BF16)
+    own_proj = own_proj.astype(BF16)
     pl.semaphore_wait(*greeting)
     to_known = keep(share_block(DP, r.known, r.sem_known))
     to_small = keep(share_block(DP, r.small, r.sem_small))
+    to_maps = keep(Relay(r.maps, r.sem_map, r.sem_maps).start())
     to_proj = keep(PairGather(r.proj, r.sem_proj).start())
 
     table_load.wait()
@@ -528,6 +643,7 @@
             to_total = keep(
                 Move(TENSOR, lambda target: r.looked.at[target], r.first, r.sem_first).start()
             )
+    to_maps.pass_on()
     to_proj.forward()
     r.first[here] = r.looked[here]
     to_total.arrive()
@@ -536,10 +652,8 @@
             BF16
         )
     to_streams = keep(Relay(r.streams, r.sem_stream, r.sem_streams).start())
-    to_maps = keep(Relay(r.maps, r.sem_map, r.sem_maps).start())
     to_streams.pass_on()
-    to_maps.pass_on()
-    pages_now = [pages_move((1, 7, 2, 6) if blocks == 8 else None)]
+    pages_now = [pages_move((4, 2, 6, 3))]
     to_small.arrive()
     gain_columns = [low(r.small[k].T[0:columns, 4:5]) for k in range(blocks)]
     small_rows = jnp.concatenate([r.small[k][:, 0:columns] for k in range(blocks)], 1)
@@ -616,7 +730,7 @@
     )
     to_streams.spread()
     to_proj.arrive()
-    all_proj = across(r.proj, 0)
+    all_proj = jnp.concatenate([unpacked_rows(r.proj[k], columns) for k in range(blocks)], 0)
     key_proj, value_proj = (
         all_proj[:, k * width : (k + 1) * width].astype(F32).T.astype(BF16) for k in (1, 2)
     )
@@ -664,7 +778,7 @@
 
     middle = stream
     for k in range(tensor):
-        full = jnp.concatenate([r.maps[k, i] for i in range(blocks)], 0)
+        full = jnp.concatenate([unpacked_rows(r.maps[k, i], columns) for i in range(blocks)], 0)
         middle = middle + dot_nt(r.heads[k], full)
     r.middle[...] = middle
     gain_middle, gain_final = r.gains[5:6, :], r.gains[6:7, :]
@@ -672,7 +786,7 @@
     inner = dot_nn(normed_mid, in_low)
     active = gelu_value(inner).astype(BF16)
     r.piece[...] = dot_nn(active, out_low).astype(BF16)
-    to_rows = keep(scatter_rows(DP, r.piece, r.arrived, r.sem_piece))
+    mixing = all_sum(r.piece, 0)
     router_logits = dot_nt(normed_mid, r.router[...])
     lane = lanes(router_logits.shape)
     hot_a, hot_b = lane == route_a, lane == route_b
@@ -682,31 +796,17 @@
     gate_a, gate_b = jnp.exp(logit_a - logit_top), jnp.exp(logit_b - logit_top)
     both = gate_a + gate_b
     r.gates[...] = jnp.where(hot_a, gate_a / both, 0.0) + jnp.where(hot_b, gate_b / both, 0.0)
-    own_gates = r.gates[own_rows, :]
-    own_middle = r.middle[own_rows, :]
-    if blocks == 8:
-        pages_now.append(pages_move((3,)))
-    r.arrived[block] = r.piece[own_rows, :]
-    to_rows.arrive()
-    depth = blocks // experts
-    mixed = jnp.zeros((picks, features), F32)
-    for e in range(experts):
-        part = r.arrived[e * depth].astype(F32)
-        for k in range(1, depth):
-            part = part + r.arrived[e * depth + k].astype(F32)
-        mixed = mixed + own_gates[:, e : e + 1] * part
-    mixed, to_sum = tensor_sum(mixed, r.summed, r.sem_summed)
-    keep(to_sum)
-    own_final = own_middle + mixed
-    r.final[block] = (own_final * root_of(own_final) * gain_final).astype(BF16)
-    to_final = keep(share_block(DP, r.final, r.sem_final))
-    if blocks == 8:
-        pages_now.append(pages_move((5, 4)))
-    to_final.arrive()
+    expert = block // (blocks // experts)
+    r.gate[...] = jnp.sum(jnp.where(lane == expert, r.gates[...], 0.0), 1, keepdims=True)
+    mixing.scatter(r.gate)
+    pages_now.append(pages_move((5,)))
+    mixing.gather()
+    pages_now.append(pages_move((1, 7)))
+    final = middle + mixing.result()
+    out = (final * root_of(final) * gain_final).astype(BF16)
     for move in pages_now:
         move.arrive()
 
-    out = across(r.final, 0)
     table = across(r.table, 0)
     logits = dot_nn(out, table)
     slot = lanes(logits.shape) + block * share
@@ -722,20 +822,24 @@
     packed = jnp.zeros((count, 128), F32)
     for k, column in enumerate(local_stats):
         packed = jnp.where(lane == k, column, packed)
-    r.stats_a[here] = packed.T[0:8, :]
-    to_stats = keep(share_block(TENSOR, r.stats_a, r.sem_stats_a))
-    to_stats.arrive()
-    r.stats_b[block] = merge_stats([r.stats_a[k] for k in range(tensor)])
-    to_stats = keep(share_block(DP, r.stats_b, r.sem_stats_b))
+    r.stats[block * tensor + here] = packed.T[0:4, :]
+    to_stats = keep(Everyone(r.stats, r.sem_stats).start())
     weight = (query_picture < 0).astype(F32)
     weight_row = jnp.where(lane == 0, weight, 0.0).T[0:1, :]
     to_stats.arrive()
-    stats = merge_stats([r.stats_b[k] for k in range(blocks)])
-    log_total = stats[0:1] + jnp.log(stats[1:2])
+    peaks = r.stats[:, 0]
+    peak = jnp.max(peaks, 0, keepdims=True)
+    stats = (
+        peak,
+        jnp.sum(r.stats[:, 1] * jnp.exp(peaks - peak), 0, keepdims=True),
+        jnp.sum(r.stats[:, 2], 0, keepdims=True),
+        jnp.sum(r.stats[:, 3], 0, keepdims=True),
+    )
+    log_total = stats[0] + jnp.log(stats[1])
     per_row = (
         log_total
-        - (1 - SMOOTH) * stats[2:3]
-        - SMOOTH * stats[3:4] / VOCAB
+        - (1 - SMOOTH) * stats[2]
+        - SMOOTH * stats[3] / VOCAB
         + ZLOSS * log_total * log_total
     )
     loss_sum = jnp.sum(weight_row * per_row, keepdims=True)
@@ -755,21 +859,14 @@
         keep(PairGather(part, r.sem_logits.at[k])) for k, part in enumerate(r.d_logits_parts)
     ]
     r.sent[...] = dot_nt(d_logits, table).astype(BF16)
-    to_rows = keep(scatter_rows(DP, r.sent, r.arrived_b, r.sem_sent))
-    r.arrived_b[block] = r.sent[own_rows, :]
-    to_rows.arrive()
+    summing = all_sum(r.sent, 1)
+    summing.scatter()
     logit_moves[0].start()
-    d_normed, to_sum = tensor_sum(sum_blocks(r.arrived_b), r.summed_b, r.sem_summed_b)
-    keep(to_sum)
-    d_final, grad_final = norm_back_rows(own_final, gain_final, d_normed)
-    r.d_final[block] = d_final.astype(BF16)
-    to_final = keep(share_block(DP, r.d_final, r.sem_d_final))
-    to_final.arrive()
+    summing.gather()
     logit_moves[0].forward()
     logit_moves[1].start()
-    upstream = across(r.d_final, 0).astype(F32)
-    expert = block // depth
-    gate = jnp.sum(jnp.where(lane == expert, r.gates[...], 0.0), 1, keepdims=True)
+    upstream, grad_final = norm_back_rows(final, gain_final, summing.result())
+    gate = r.gate[...]
     d_piece = (gate * upstream).astype(BF16)
     d_inner = (dot_nt(d_piece, out_low) * gelu_slope(inner)).astype(BF16)
     r.wide[:, 0:features] = dot_nt(d_inner, in_low).astype(BF16)
@@ -778,47 +875,38 @@
     r.wide[:, features:] = jnp.where(
         lane == expert, high, jnp.where(lane == expert + 64, gate_part - high, 0.0)
     ).astype(BF16)
-    to_rows = keep(scatter_rows(DP, r.wide, r.arrived_c, r.sem_wide))
-    r.arrived_c[block] = r.wide[own_rows, :]
+    summing = all_sum(r.wide, 2)
     grad_out = dot_nn(active.T, d_piece)
     grad_in = dot_nn(normed_mid.T, d_inner)
     r.grad_out[...] = grad_out
     r.grad_in[...] = grad_in
     squares = squared(grad_out) + squared(grad_in)
-    to_rows.arrive()
+    summing.scatter()
     logit_moves[1].forward()
     logit_moves[2].start()
-    total, to_sum = tensor_sum(sum_blocks(r.arrived_c), r.summed_c, r.sem_summed_c)
-    keep(to_sum)
+    summing.gather()
+    logit_moves[2].forward()
+    logit_moves[3].start()
+    total = summing.result()
     tail = total[:, features:]
     d_gates = tail + pltpu.roll(tail, 64, 1)
-    own_known = known.T[0:picks].astype(jnp.int32)
-    slim = lanes(tail.shape)
-    named = (slim == own_known[:, 2:3]) | (slim == own_known[:, 3:4])
+    named = hot_a | hot_b
     d_gates = jnp.where(named, d_gates, 0.0)
-    mean = jnp.sum(own_gates * d_gates, 1, keepdims=True)
-    d_router = jnp.where(named, own_gates * (d_gates - mean), 0.0).astype(BF16)
+    mean = jnp.sum(r.gates[...] * d_gates, 1, keepdims=True)
+    d_router = jnp.where(named, r.gates[...] * (d_gates - mean), 0.0).astype(BF16)
     d_normed_mid = total[:, 0:features] + dot_nn(d_router, r.router[...])
-    d_from_mid, grad_middle = norm_back_rows(own_middle, gain_middle, d_normed_mid)
-    r.d_middle[block, :, 0:features] = (d_final + d_from_mid).astype(BF16)
-    r.d_middle[block, :, features:] = d_router
-    r.gain_parts[block, 0:1, :] = grad_middle
-    r.gain_parts[block, 1:2, :] = grad_final
-    to_middle = keep(share_block(DP, r.d_middle, r.sem_d_middle))
-    to_gains = keep(share_block(DP, r.gain_parts, r.sem_gains))
-    logit_moves[2].forward()
-    logit_moves[3].start()
+    d_from_mid, grad_middle = norm_back_rows(middle, gain_middle, d_normed_mid)
+    d_attn = (upstream + d_from_mid).astype(BF16)
     stream_c = jnp.concatenate([r.streams[k, block] for k in range(tensor)], 1).astype(F32)
     roots = r.roots[...]
     gain_column = low(r.small[block].T[0:columns, 4:5])
     normed_c = (stream_c * roots * gain_column).astype(BF16)
     normed_loss = dot_nt(normed_c, back_hot).astype(BF16)
     query_wide = dot_nn(query.T, back_hot)
-    to_middle.arrive()
-
-    d_middle = across(r.d_middle, 0)
-    d_attn = d_middle[:, 0:features]
-    own_map = jnp.concatenate([r.maps[here, i] for i in range(blocks)], 0)
+
+    own_map = jnp.concatenate(
+        [unpacked_rows(r.maps[here, i], columns) for i in range(blocks)], 0
+    )
     d_attended = dot_nn(d_attn, own_map).astype(BF16)
     d_query = []
     for h in range(heads):
@@ -835,7 +923,6 @@
         r.d_values[h * HD : (h + 1) * HD, :] = dot_nn(d_head.T, soft.astype(BF16)).astype(BF16)
     d_query = jnp.concatenate(d_query, 1)
     d_query_wide = dot_nn(d_query.T, back_hot).astype(BF16)
-    own_proj = r.proj[block]
     d_columns = (
         dot_nn(own_proj[:, 0:width], d_query_wide)
         + dot_nn(own_proj[:, width : 2 * width], r.d_keys[...])
@@ -904,14 +991,12 @@
     grad_map = dot_nt(attended.T, d_attn_t)
     r.grad_map[...] = grad_map
     squares = squares + squared(grad_map)
-    grad_router = dot_nt(d_middle[:, features:].T, middle_t)[0:8]
+    grad_router = dot_nt(d_router.T, middle_t)[0:8]
     residual = dot_nn(d_attn_t, back_hot)
     logit_moves[3].forward()
-    to_gains.arrive()
-    gain_sum = r.gain_parts[0]
-    for k in range(1, blocks):
-        gain_sum = gain_sum + r.gain_parts[k]
-    gain_sum = jnp.concatenate([gain_sum, jnp.zeros((6, features), F32)], 0)
+    gain_sum = jnp.concatenate(
+        [grad_middle, grad_final, jnp.zeros((6, features), F32)], 0
+    )
     gain_sum = pltpu.roll(gain_sum, lax.rem(features - block * columns, features), 1)
     to_parts.arrive()
     parts = across(r.part_all, 1).astype(F32)
@@ -1025,8 +1110,8 @@
     scratch = dict(
         known=((blocks, 8, rows), F32),
         small=((blocks, 8, 128), F32),
-        proj=((blocks, columns, 3 * width), BF16),
-        maps=((tensor, blocks, columns, width), BF16),
+        proj=((blocks, columns * 3 * width // 128, 128), BF16),
+        maps=((tensor, blocks, columns * width // 128, 128), BF16),
         pages=((blocks, columns, share), BF16),
         table=((blocks, columns, share), BF16),
         id_row=((1, every), F32),
@@ -1049,21 +1134,11 @@
         middle=((count, features), F32),
         piece=((count, features), BF16),
         gates=((count, 128), F32),
-        arrived=((blocks, picks, features), BF16),
-        summed=((tensor, picks, features), F32),
-        final=((blocks, picks, features), BF16),
-        stats_a=((tensor, 8, 128), F32),
-        stats_b=((blocks, 8, 128), F32),
+        gate=((count, 1), F32),
+        stats=((blocks * tensor, 4, 128), F32),
         d_logits=((4, blocks, count // 4, share), BF16),
         sent=((count, features), BF16),
-        arrived_b=((blocks, picks, features), BF16),
-        summed_b=((tensor, picks, features), F32),
-        d_final=((blocks, picks, features), BF16),
         wide=((count, wide), BF16),
-        arrived_c=((blocks, picks, wide), BF16),
-        summed_c=((tensor, picks, wide), F32),
-        d_middle=((blocks, picks, wide), BF16),
-        gain_parts=((blocks, 2, features), F32),
         d_keys=((width, every), BF16),
         d_values=((width, every), BF16),
         part=((columns + 16, every), BF16),
@@ -1079,32 +1154,33 @@
         load_sems=(len(small),),
         held_sems=(len(held),),
         sem_squares=(2, blocks * tensor),
+        sem_stats=(2, blocks * tensor),
         sem_logits=(4, 2, blocks),
         sem_known=dp,
         sem_small=dp,
         sem_proj=dp,
         sem_map=dp,
         sem_pages=dp,
-        sem_piece=dp,
-        sem_final=dp,
-        sem_stats_b=dp,
-        sem_sent=dp,
-        sem_d_final=dp,
-        sem_wide=dp,
-        sem_d_middle=dp,
-        sem_gains=dp,
         sem_first=ten,
         sem_stream=dp,
         sem_streams=(2, 3, blocks),
         sem_maps=(2, 3, blocks),
         sem_heads=ten,
-        sem_summed=ten,
-        sem_stats_a=ten,
-        sem_summed_b=ten,
-        sem_summed_c=ten,
         sem_part=ten,
         sem_part_all=ten,
     )
+    height = count // tensor
+    for number, span in enumerate((features, features, wide)):
+        shapes = (
+            (tensor, height, span),
+            (span // 128, height, 128),
+            (blocks, height, 128),
+            (span // 128, height, 128),
+            (tensor, height, span),
+        )
+        scratch.update({f"sum_{k}_{number}": (shape, BF16) for k, shape in enumerate(shapes)})
+        for k, shape in enumerate((ten, dp, dp, ten)):
+            sems[f"sum_sem_{k}_{number}"] = shape
     copied = {**small, **held}
     names = tuple(name + OUTSIDE for name in copied) + tuple(scalars)
     names += tuple(outputs) + tuple(scratch) + tuple(sems)
@@ -1694,7 +1770,8 @@
         and router.shape[0] <= 4
         and routes.shape[1] == 2
         and gains.shape[0] == 3
-        and columns % 16 == 0
+        and columns % 32 == 0
+        and arrays[9].shape[2] % 128 == 64
         and columns <= 128
     )
 

time: 189 us -> 166 us (0.88)
  Pallas kernels: 182 us -> 159 us
    pallas_call x1, Pallas kernels: 174 us -> 151 us  [run_step(): pl.pallas_call(functools.partial(step_kernel, names, tuple(small), tuple(...]
where the time goes in v4:
time: 166 us; the launch traced here: 165 us
  Pallas kernels  159 us (96%)
  between operations  6.69 us (4%)
    pallas_call x1, Pallas kernels, run_step(): pl.pallas_call(functools.partial(step_kernel, names, tuple(small), tuple(...  151 us
    pallas_call x1, Pallas kernels, run_update(): pl.pallas_call(functools.partial(update_kernel, jobs), out_shape=[jax.Sha...  7.85 us

profile of v4, /device:TPU:0, one launch (start us, length us, event | category | flops | bytes accessed | tf_op | source)
XLA Modules:
  0.0 165.4 jit_solution(1489839492067690700)
XLA Ops:
  1.3 0.0 copy-start
  1.3 0.0 copy-start.1
  1.3 0.0 copy-start.2
  1.4 0.0 copy-start.3
  1.4 0.0 copy-start.4
  1.4 0.0 copy-start.5
  1.4 0.0 copy-start.6
  1.4 0.0 copy-start.7
  1.4 0.0 copy-start.8
  1.4 150.8 %training_step.1 = (f32[96,8000]{1,0:T(8,128)S(1)}, f32[3,96,192]{2,1,0:T(8,128)S(1)}, f32[192,96]{1,0:T(8,128)S(1)}, f32[8,128]{1,0:T(8,128)S(1)}, f32[768,384]...) custom-call(s32[1,128]{1,0:T(1,128)} %bitcast.19, ...), custom_call_target="tpu_custom_call" | custom-call | tf_op jit(solution)/shard_map/training_step/pallas_call | solution.py:1188
  152.2 0.0 copy-done
  152.2 0.0 copy-done.1
  152.2 0.0 copy-done.2
  152.3 0.0 copy-done.3
  152.3 0.0 copy-done.4
  152.3 0.0 copy-done.5
  152.3 0.0 copy-done.6
  152.3 0.0 copy-done.7
  152.3 0.0 copy-done.8
  152.3 7.9 %update.1 = (f32[96,8000]{1,0:T(8,128)}, f32[96,8000]{1,0:T(8,128)}, f32[96,8000]{1,0:T(8,128)}, f32[768,384]{1,0:T(8,128)}, f32[768,384]{1,0:T(8,128)}, /*index...) custom-call(f32[1,1]{1,0:T(1,128)} %get-tuple-element.77.clip, ...), custom_call_target="tpu_custom_call" | custom-call | tf_op jit(solution)/shard_map/update/pallas_call | solution.py:1251
Async XLA Ops:
  1.3 150.9 %copy-start = (f32[4,96]{1,0:T(4,128)S(1)}, f32[4,96]{1,0:T(4,128)}, u32[]{:S(2)}) copy-start(f32[4,96]{1,0:T(4,128)} %refs_23_.2) | copy-start | bytes 4612
  1.3 150.9 %copy-start.1 = (f32[3,96]{1,0:T(4,128)S(1)}, f32[3,96]{1,0:T(4,128)}, u32[]{:S(2)}) copy-start(f32[3,96]{1,0:T(4,128)} %refs_26_.1) | copy-start | bytes 3460
  1.3 150.9 %copy-start.2 = (f32[3,32]{1,0:T(4,128)S(1)}, f32[3,32]{1,0:T(4,128)}, u32[]{:S(2)}) copy-start(f32[3,32]{1,0:T(4,128)} %refs_29_.1) | copy-start | bytes 1156
  1.4 150.9 %copy-start.3 = (f32[4,96]{1,0:T(4,128)S(1)}, f32[4,96]{1,0:T(4,128)}, u32[]{:S(2)}) copy-start(f32[4,96]{1,0:T(4,128)} %refs_24_.1) | copy-start | bytes 4612
  1.4 150.9 %copy-start.4 = (f32[4,96]{1,0:T(4,128)S(1)}, f32[4,96]{1,0:T(4,128)}, u32[]{:S(2)}) copy-start(f32[4,96]{1,0:T(4,128)} %refs_25_.1) | copy-start | bytes 4612
  1.4 150.9 %copy-start.5 = (f32[3,96]{1,0:T(4,128)S(1)}, f32[3,96]{1,0:T(4,128)}, u32[]{:S(2)}) copy-start(f32[3,96]{1,0:T(4,128)} %refs_27_.1) | copy-start | bytes 3460
  1.4 150.9 %copy-start.6 = (f32[3,96]{1,0:T(4,128)S(1)}, f32[3,96]{1,0:T(4,128)}, u32[]{:S(2)}) copy-start(f32[3,96]{1,0:T(4,128)} %refs_28_.1) | copy-start | bytes 3460
  1.4 150.9 %copy-start.7 = (f32[3,32]{1,0:T(4,128)S(1)}, f32[3,32]{1,0:T(4,128)}, u32[]{:S(2)}) copy-start(f32[3,32]{1,0:T(4,128)} %refs_30_.1) | copy-start | bytes 1156
  1.4 150.9 %copy-start.8 = (f32[3,32]{1,0:T(4,128)S(1)}, f32[3,32]{1,0:T(4,128)}, u32[]{:S(2)}) copy-start(f32[3,32]{1,0:T(4,128)} %refs_31_.1) | copy-start | bytes 1156

commit v5 on v4

--- a/solution.py
+++ b/solution.py
@@ -860,13 +860,14 @@
     ]
     r.sent[...] = dot_nt(d_logits, table).astype(BF16)
     summing = all_sum(r.sent, 1)
+    logit_moves[0].start()
     summing.scatter()
-    logit_moves[0].start()
     summing.gather()
     logit_moves[0].forward()
     logit_moves[1].start()
     upstream, grad_final = norm_back_rows(final, gain_final, summing.result())
     gate = r.gate[...]
+    logit_moves[2].start()
     d_piece = (gate * upstream).astype(BF16)
     d_inner = (dot_nt(d_piece, out_low) * gelu_slope(inner)).astype(BF16)
     r.wide[:, 0:features] = dot_nt(d_inner, in_low).astype(BF16)
@@ -876,16 +877,15 @@
         lane == expert, high, jnp.where(lane == expert + 64, gate_part - high, 0.0)
     ).astype(BF16)
     summing = all_sum(r.wide, 2)
+    logit_moves[1].forward()
     grad_out = dot_nn(active.T, d_piece)
     grad_in = dot_nn(normed_mid.T, d_inner)
     r.grad_out[...] = grad_out
     r.grad_in[...] = grad_in
     squares = squared(grad_out) + squared(grad_in)
     summing.scatter()
-    logit_moves[1].forward()
-    logit_moves[2].start()
+    logit_moves[2].forward()
     summing.gather()
-    logit_moves[2].forward()
     logit_moves[3].start()
     total = summing.result()
     tail = total[:, features:]
@@ -1070,10 +1070,13 @@
     to_squares = keep(Everyone(r.squares, r.sem_squares).start())
     to_squares.arrive()
     norm = jnp.sqrt(sum_blocks(r.squares))
-    r.norm[...] = norm[:, 0:1]
-    r.clip[...] = (MAX_NORM / jnp.maximum(norm, MAX_NORM))[:, 0:1]
-    r.loss_sum[...] = loss_sum
-    r.loss_count[...] = loss_count
+    clip = MAX_NORM / jnp.maximum(norm, MAX_NORM)
+    place = lanes(norm.shape)
+    r.facts[...] = jnp.where(
+        place == 0,
+        clip,
+        jnp.where(place == 1, norm, jnp.where(place == 2, loss_sum, loss_count)),
+    )
     for copy in held[5:]:
         copy.wait()
     for move in moves:
@@ -1102,10 +1105,7 @@
         grad_in=(features, hidden),
         grad_out=(hidden, features),
         grad_bias=(heads, bucket_count, 128),
-        norm=(1, 1),
-        clip=(1, 1),
-        loss_sum=(1, 1),
-        loss_count=(1, 1),
+        facts=(1, 128),
     )
     scratch = dict(
         known=((blocks, 8, rows), F32),
@@ -1189,10 +1189,7 @@
         functools.partial(
             step_kernel, names, tuple(small), tuple(held), experts, vocab_rows, starts
         ),
-        out_shape=[
-            jax.ShapeDtypeStruct(shape, F32) if shape == (1, 1) else pltpu.VMEM(shape, F32)
-            for shape in outputs.values()
-        ],
+        out_shape=[pltpu.VMEM(shape, F32) for shape in outputs.values()],
         in_specs=[pl.BlockSpec(memory_space=pltpu.HBM)] * len(copied)
         + [pl.BlockSpec(memory_space=pltpu.SMEM)] * len(scalars),
         out_specs=[WHOLE] * len(outputs),
@@ -1214,11 +1211,18 @@
     return weight * (1 - rate * decay) - (rate / (1 - BETA1**STEP)) * step, first, second
 
 
-def update_kernel(jobs, clip, *refs):
+def spread_over(factor, change):
+    return factor.reshape((1,) * change.ndim) * change
+
+
+def update_kernel(jobs, facts, *refs):
     grads, refs = refs[: len(jobs)], refs[len(jobs) :]
     total = 3 * len(jobs)
-    olds, outs, news, done = refs[:total], refs[total : 2 * total], refs[2 * total : -1], refs[-1]
-    factor = clip[0, 0]
+    olds, outs, refs = refs[:total], refs[total : 2 * total], refs[2 * total :]
+    scalars, news, done = refs[:3], refs[3:-1], refs[-1]
+    for k, scalar in enumerate(scalars):
+        scalar[...] = facts[:, k + 1 : k + 2]
+    factor = facts[:, 0:1]
     copies = []
     for index, (height, rate, decay, begin, reduced) in enumerate(jobs):
         trio = slice(3 * index, 3 * index + 3)
@@ -1232,7 +1236,7 @@
             else:
                 change = grads[index][rows]
             values = update_piece(
-                *(ref[rows] for ref in olds[trio]), factor * change, rate, decay
+                *(ref[rows] for ref in olds[trio]), spread_over(factor, change), rate, decay
             )
             for which, value in enumerate(values):
                 new, out = news[3 * index + which], outs[3 * index + which]
@@ -1245,19 +1249,19 @@
         copy.wait()
 
 
-def run_update(clip, jobs, grads, olds):
+def run_update(facts, jobs, grads, olds):
     shapes = [old.shape for old in olds]
     pieces = sum(3 * shapes[3 * k][0] // job[0] for k, job in enumerate(jobs))
     results = pl.pallas_call(
         functools.partial(update_kernel, jobs),
-        out_shape=[jax.ShapeDtypeStruct(shape, F32) for shape in shapes],
-        in_specs=[pl.BlockSpec(memory_space=pltpu.SMEM)] + [WHOLE] * (len(grads) + len(olds)),
-        out_specs=[pl.BlockSpec(memory_space=pltpu.HBM)] * len(shapes),
+        out_shape=[jax.ShapeDtypeStruct(shape, F32) for shape in shapes + [(1, 1)] * 3],
+        in_specs=[WHOLE] * (1 + len(grads) + len(olds)),
+        out_specs=[pl.BlockSpec(memory_space=pltpu.HBM)] * len(shapes) + [WHOLE] * 3,
         scratch_shapes=[pltpu.VMEM(shape, F32) for shape in shapes] + [DMA((pieces,))],
         compiler_params=pltpu.CompilerParams(vmem_limit_bytes=UPDATE_BYTES),
         name="update",
-    )(clip, *grads, *olds)
-    return [results[3 * k : 3 * k + 3] for k in range(len(jobs))]
+    )(facts, *grads, *olds)
+    return [results[3 * k : 3 * k + 3] for k in range(len(jobs) + 1)]
 
 
 def fast_local(
@@ -1343,13 +1347,11 @@
     olds += (g.map_weight, g.map_first, g.map_second, router, router_first, router_second)
     olds += (norm_gains, norm_gains_first, norm_gains_second)
     olds += (position_bias, position_bias_first, position_bias_second)
-    new = run_update(g.clip, jobs, grads, olds)
+    new = run_update(g.facts, jobs, grads, olds)
     results = [value.T for value in new[0]]
     for k in (3, 4, 5, 1, 2, 6, 7):
         results.extend(new[k])
-    grad_norm, loss_sum, loss_count = (
-        value.reshape(()) for value in (g.norm, g.loss_sum, g.loss_count)
-    )
+    grad_norm, loss_sum, loss_count = (value.reshape(()) for value in new[-1])
     return (*results, grad_norm, loss_sum, loss_count)
 
 

time: 166 us -> 157 us (0.946)
  between operations: 6.69 us -> 1.63 us
  Pallas kernels: 159 us -> 155 us
    pallas_call x1, Pallas kernels: 151 us -> 147 us  [run_step(): pl.pallas_call(functools.partial(step_kernel, names, tuple(small), tuple(...]
where the time goes in v5:
time: 157 us
  Pallas kernels  155 us (99%)
  between operations  1.63 us (1%)
    pallas_call x1, Pallas kernels, run_step(): pl.pallas_call(functools.partial(step_kernel, names, tuple(small), tuple(...  147 us
    pallas_call x1, Pallas kernels, run_update(): pl.pallas_call(functools.partial(update_kernel, jobs), out_shape=[jax.Sha...  7.9 us

profile of v5, /device:TPU:0, one launch (start us, length us, event | category | flops | bytes accessed | tf_op | source)
XLA Modules:
  0.0 156.7 jit_solution(14891136216422538657)
XLA Ops:
  1.3 0.0 copy-start
  1.3 0.0 copy-start.1
  1.3 0.0 copy-start.2
  1.4 0.0 copy-start.3
  1.4 0.0 copy-start.4
  1.4 0.0 copy-start.5
  1.4 0.0 copy-start.6
  1.4 0.0 copy-start.7
  1.4 0.0 copy-start.8
  1.4 147.1 %training_step.1 = (f32[96,8000]{1,0:T(8,128)S(1)}, f32[3,96,192]{2,1,0:T(8,128)S(1)}, f32[192,96]{1,0:T(8,128)S(1)}, f32[8,128]{1,0:T(8,128)S(1)}, f32[768,384]...) custom-call(s32[1,128]{1,0:T(1,128)} %bitcast.19, ...), custom_call_target="tpu_custom_call" | custom-call | tf_op jit(solution)/shard_map/training_step/pallas_call | solution.py:1188
  148.5 0.0 copy-done
  148.5 0.0 copy-done.1
  148.6 0.0 copy-done.2
  148.6 0.0 copy-done.3
  148.6 0.0 copy-done.4
  148.6 0.0 copy-done.5
  148.6 0.0 copy-done.6
  148.6 0.0 copy-done.7
  148.6 0.0 copy-done.8
  148.6 7.9 %update.1 = (f32[96,8000]{1,0:T(8,128)}, f32[96,8000]{1,0:T(8,128)}, f32[96,8000]{1,0:T(8,128)}, f32[768,384]{1,0:T(8,128)}, f32[768,384]{1,0:T(8,128)}, /*index...) custom-call(f32[1,128]{1,0:T(1,128)S(1)} %get-tuple-element.77.facts, ...), custom_call_target="tpu_custom_call" | custom-call | tf_op jit(solution)/shard_map/update/pallas_call | solution.py:1255
Async XLA Ops:
  1.3 147.2 %copy-start = (f32[4,96]{1,0:T(4,128)S(1)}, f32[4,96]{1,0:T(4,128)}, u32[]{:S(2)}) copy-start(f32[4,96]{1,0:T(4,128)} %refs_23_.2) | copy-start | bytes 4612
  1.3 147.2 %copy-start.1 = (f32[3,96]{1,0:T(4,128)S(1)}, f32[3,96]{1,0:T(4,128)}, u32[]{:S(2)}) copy-start(f32[3,96]{1,0:T(4,128)} %refs_26_.1) | copy-start | bytes 3460
  1.3 147.2 %copy-start.2 = (f32[3,32]{1,0:T(4,128)S(1)}, f32[3,32]{1,0:T(4,128)}, u32[]{:S(2)}) copy-start(f32[3,32]{1,0:T(4,128)} %refs_29_.1) | copy-start | bytes 1156
  1.4 147.2 %copy-start.3 = (f32[4,96]{1,0:T(4,128)S(1)}, f32[4,96]{1,0:T(4,128)}, u32[]{:S(2)}) copy-start(f32[4,96]{1,0:T(4,128)} %refs_24_.1) | copy-start | bytes 4612
  1.4 147.2 %copy-start.4 = (f32[4,96]{1,0:T(4,128)S(1)}, f32[4,96]{1,0:T(4,128)}, u32[]{:S(2)}) copy-start(f32[4,96]{1,0:T(4,128)} %refs_25_.1) | copy-start | bytes 4612
  1.4 147.2 %copy-start.5 = (f32[3,96]{1,0:T(4,128)S(1)}, f32[3,96]{1,0:T(4,128)}, u32[]{:S(2)}) copy-start(f32[3,96]{1,0:T(4,128)} %refs_27_.1) | copy-start | bytes 3460
  1.4 147.2 %copy-start.6 = (f32[3,96]{1,0:T(4,128)S(1)}, f32[3,96]{1,0:T(4,128)}, u32[]{:S(2)}) copy-start(f32[3,96]{1,0:T(4,128)} %refs_28_.1) | copy-start | bytes 3460
  1.4 147.2 %copy-start.7 = (f32[3,32]{1,0:T(4,128)S(1)}, f32[3,32]{1,0:T(4,128)}, u32[]{:S(2)}) copy-start(f32[3,32]{1,0:T(4,128)} %refs_30_.1) | copy-start | bytes 1156
  1.4 147.2 %copy-start.8 = (f32[3,32]{1,0:T(4,128)S(1)}, f32[3,32]{1,0:T(4,128)}, u32[]{:S(2)}) copy-start(f32[3,32]{1,0:T(4,128)} %refs_31_.1) | copy-start | bytes 1156

commit v6 on v5

--- a/solution.py
+++ b/solution.py
@@ -998,6 +998,23 @@
         [grad_middle, grad_final, jnp.zeros((6, features), F32)], 0
     )
     gain_sum = pltpu.roll(gain_sum, lax.rem(features - block * columns, features), 1)
+    for move in logit_moves[:-1]:
+        move.arrive()
+    late_rows = r.d_logits_parts[-1].shape[1]
+    out_early, out_late = out_t[:, 0 : count - late_rows], out_t[:, count - late_rows :]
+    whole = vocab_rows // share
+
+    def first_page(k, where, size):
+        page = jnp.concatenate([part[k] for part in r.d_logits_parts[:-1]], 0)
+        r.grad_table[:, where] = dot_nn(out_early, page)[:, 0:size]
+
+    def first_pages(k, carry):
+        first_page(k, pl.ds(pl.multiple_of(k * share, share), share), share)
+        return carry
+
+    lax.fori_loop(0, whole, first_pages, 0)
+    if vocab_rows > whole * share:
+        first_page(whole, slice(whole * share, vocab_rows), vocab_rows - whole * share)
     to_parts.arrive()
     parts = across(r.part_all, 1).astype(F32)
     d_columns = parts[0:columns]
@@ -1035,7 +1052,7 @@
         found = dot_nn(jnp.concatenate(masked, 0), r.id_low[...])
         begin = pl.multiple_of(k * 4 * STRIP, STRIP)
         for n in range(4):
-            r.grad_table[:, pl.ds(begin + n * STRIP, STRIP)] = found[
+            r.grad_table[:, pl.ds(begin + n * STRIP, STRIP)] += found[
                 n * columns : (n + 1) * columns
             ]
         return carry
@@ -1044,23 +1061,21 @@
     masked = jnp.concatenate([low_half * strip_mask(float(k)) for k, size in ends], 0)
     found = dot_nn(masked, r.id_low[...])
     for n, (k, size) in enumerate(ends):
-        r.grad_table[:, k * STRIP : k * STRIP + size] = found[
+        r.grad_table[:, k * STRIP : k * STRIP + size] += found[
             n * columns : (n + 1) * columns, 0:size
         ]
-    for move in logit_moves:
-        move.arrive()
+    logit_moves[-1].arrive()
 
     def page_strips(k, total):
         begin = pl.multiple_of(k * share, share)
         return total + add_page(k, pl.ds(begin, share))
 
     def add_page(k, where, size=share):
-        page = jnp.concatenate([part[k] for part in r.d_logits_parts], 0)
-        value = r.grad_table[:, where] + dot_nn(out_t, page)[:, 0:size]
+        page = r.d_logits_parts[-1][k]
+        value = r.grad_table[:, where] + dot_nn(out_late, page)[:, 0:size]
         r.grad_table[:, where] = value
         return squared(value)
 
-    whole = vocab_rows // share
     squares = squares + lax.fori_loop(0, whole, page_strips, jnp.zeros((1, 1), F32))
     if vocab_rows > whole * share:
         squares = squares + add_page(

time: 157 us -> 157 us (level)
  no operation moved by 1% of the time
where the time goes in v6:
time: 157 us
  Pallas kernels  156 us (99%)
  between operations  1.63 us (1%)
    pallas_call x1, Pallas kernels, run_step(): pl.pallas_call(functools.partial(step_kernel, names, tuple(small), tuple(...  148 us
    pallas_call x1, Pallas kernels, run_update(): pl.pallas_call(functools.partial(update_kernel, jobs), out_shape=[jax.Sha...  7.9 us

profile of v6, /device:TPU:0, one launch (start us, length us, event | category | flops | bytes accessed | tf_op | source)
XLA Modules:
  0.0 157.3 jit_solution(12228206579680885051)
XLA Ops:
  1.3 0.0 copy-start
  1.3 0.0 copy-start.1
  1.3 0.0 copy-start.2
  1.4 0.0 copy-start.3
  1.4 0.0 copy-start.4
  1.4 0.0 copy-start.5
  1.4 0.0 copy-start.6
  1.4 0.0 copy-start.7
  1.4 0.0 copy-start.8
  1.4 147.7 %training_step.1 = (f32[96,8000]{1,0:T(8,128)S(1)}, f32[3,96,192]{2,1,0:T(8,128)S(1)}, f32[192,96]{1,0:T(8,128)S(1)}, f32[8,128]{1,0:T(8,128)S(1)}, f32[768,384]...) custom-call(s32[1,128]{1,0:T(1,128)} %bitcast.19, ...), custom_call_target="tpu_custom_call" | custom-call | tf_op jit(solution)/shard_map/training_step/pallas_call | solution.py:1203
  149.1 0.0 copy-done
  149.1 0.0 copy-done.1
  149.2 0.0 copy-done.2
  149.2 0.0 copy-done.3
  149.2 0.0 copy-done.4
  149.2 0.0 copy-done.5
  149.2 0.0 copy-done.6
  149.2 0.0 copy-done.7
  149.2 0.0 copy-done.8
  149.2 7.9 %update.1 = (f32[96,8000]{1,0:T(8,128)}, f32[96,8000]{1,0:T(8,128)}, f32[96,8000]{1,0:T(8,128)}, f32[768,384]{1,0:T(8,128)}, f32[768,384]{1,0:T(8,128)}, /*index...) custom-call(f32[1,128]{1,0:T(1,128)S(1)} %get-tuple-element.77.facts, ...), custom_call_target="tpu_custom_call" | custom-call | tf_op jit(solution)/shard_map/update/pallas_call | solution.py:1270
Async XLA Ops:
  1.3 147.8 %copy-start = (f32[4,96]{1,0:T(4,128)S(1)}, f32[4,96]{1,0:T(4,128)}, u32[]{:S(2)}) copy-start(f32[4,96]{1,0:T(4,128)} %refs_23_.2) | copy-start | bytes 4612
  1.3 147.8 %copy-start.1 = (f32[3,96]{1,0:T(4,128)S(1)}, f32[3,96]{1,0:T(4,128)}, u32[]{:S(2)}) copy-start(f32[3,96]{1,0:T(4,128)} %refs_26_.1) | copy-start | bytes 3460
  1.3 147.8 %copy-start.2 = (f32[3,32]{1,0:T(4,128)S(1)}, f32[3,32]{1,0:T(4,128)}, u32[]{:S(2)}) copy-start(f32[3,32]{1,0:T(4,128)} %refs_29_.1) | copy-start | bytes 1156
  1.4 147.8 %copy-start.3 = (f32[4,96]{1,0:T(4,128)S(1)}, f32[4,96]{1,0:T(4,128)}, u32[]{:S(2)}) copy-start(f32[4,96]{1,0:T(4,128)} %refs_24_.1) | copy-start | bytes 4612
  1.4 147.8 %copy-start.4 = (f32[4,96]{1,0:T(4,128)S(1)}, f32[4,96]{1,0:T(4,128)}, u32[]{:S(2)}) copy-start(f32[4,96]{1,0:T(4,128)} %refs_25_.1) | copy-start | bytes 4612
  1.4 147.8 %copy-start.5 = (f32[3,96]{1,0:T(4,128)S(1)}, f32[3,96]{1,0:T(4,128)}, u32[]{:S(2)}) copy-start(f32[3,96]{1,0:T(4,128)} %refs_27_.1) | copy-start | bytes 3460
  1.4 147.8 %copy-start.6 = (f32[3,96]{1,0:T(4,128)S(1)}, f32[3,96]{1,0:T(4,128)}, u32[]{:S(2)}) copy-start(f32[3,96]{1,0:T(4,128)} %refs_28_.1) | copy-start | bytes 3460
  1.4 147.8 %copy-start.7 = (f32[3,32]{1,0:T(4,128)S(1)}, f32[3,32]{1,0:T(4,128)}, u32[]{:S(2)}) copy-start(f32[3,32]{1,0:T(4,128)} %refs_30_.1) | copy-start | bytes 1156
  1.4 147.8 %copy-start.8 = (f32[3,32]{1,0:T(4,128)S(1)}, f32[3,32]{1,0:T(4,128)}, u32[]{:S(2)}) copy-start(f32[3,32]{1,0:T(4,128)} %refs_31_.1) | copy-start | bytes 1156
